TPU v7x, 32 devices: a whole 2x2x4 slice. The times are simulated.
32 devices in a mesh: gx: 8 (over y, x, core), ba: 4 (over z).
Axes of the slice: x: 2, y: 2, z: 4, core: 2. Of those that a mesh axis runs over, the one named last changes fastest.
Arguments:
- phi_start: float32 [64, 16, 256, 256], P('gx', 'ba'), may hold values from -6 to 6
- coeff: float32 [64, 256, 256], P('gx'), may hold values from 1 to 3
- forward: float32 [2, 2, 64, 256, 256], P(None, None, None, 'gx'), may hold values from -6 to 6
- rates: float32 [16], P('ba'), may hold values from 0.02 to 0.2
- speeds: float32 [16], P('ba'), may hold values from 0.5 to 2
- shares: float32 [16], P('ba'), may hold values from 0.02 to 0.12
Outputs:
- phi_out: float32 [64, 16, 256, 256], P('gx', 'ba')
- grad: float32 [64, 12, 16], P('gx', None, 'ba')
All inputs are finite; a program needn't handle non-finite values.
Results may differ from a plain program's by a relative error of at most 0.00026.
Values sent between devices are 32-bit elements; how exact they have to be, the bound alone decides.
No kernel may reach another device: no remote copies, remote signals or barrier semaphores. Data moves between devices by JAX's collectives and lax.ppermute only.
A program may use at most 192 MiB of HBM per device.

v0:
```python
import math

import jax
import jax.numpy as jnp
from jax import lax
from jax.sharding import PartitionSpec as P


def quadrature():
    level = jnp.arange(6).astype(jnp.float32)
    polar = 0.2 + 0.15 * level
    cosine = jnp.concatenate([-polar, polar])
    azimuth = jnp.concatenate([level * (math.pi / 3.0) + math.pi / 6.0, level * (math.pi / 3.0)])
    sine = jnp.sqrt(1.0 - cosine * cosine)
    return (cosine, sine * jnp.cos(azimuth), sine * jnp.sin(azimuth))


def frequency(count, start, length):
    index = jnp.arange(length, dtype=jnp.int32) + start
    signed = (index + count // 2) % count - count // 2
    return signed.astype(jnp.float32) * (1.5 * 2.0 * math.pi / count)


def tables(count):
    index = jnp.arange(count, dtype=jnp.int32)
    product = index[:, None] * index[None, :] % count
    angle = product.astype(jnp.float32) * (2.0 * math.pi / count)
    factor = 1.0 / math.sqrt(count)
    return (jnp.cos(angle) * factor, jnp.sin(angle) * factor)


def forward_transform(phi, cos_x, sin_x, cos_y, sin_y):
    highest = lax.Precision.HIGHEST
    row_re = jnp.einsum("zbxy,yk->zbxk", phi, cos_y, precision=highest)
    row_im = -jnp.einsum("zbxy,yk->zbxk", phi, sin_y, precision=highest)
    spec_re = jnp.einsum("kx,zbxy->zbky", cos_x, row_re, precision=highest) + jnp.einsum(
        "kx,zbxy->zbky", sin_x, row_im, precision=highest
    )
    spec_im = jnp.einsum("kx,zbxy->zbky", cos_x, row_im, precision=highest) - jnp.einsum(
        "kx,zbxy->zbky", sin_x, row_re, precision=highest
    )
    return (spec_re, spec_im)


def inverse_transform(spec_re, spec_im, cos_x, sin_x, cos_y, sin_y):
    highest = lax.Precision.HIGHEST
    col_re = jnp.einsum("zbxk,ky->zbxy", spec_re, cos_y, precision=highest) - jnp.einsum(
        "zbxk,ky->zbxy", spec_im, sin_y, precision=highest
    )
    col_im = jnp.einsum("zbxk,ky->zbxy", spec_im, cos_y, precision=highest) + jnp.einsum(
        "zbxk,ky->zbxy", spec_re, sin_y, precision=highest
    )
    return jnp.einsum("xk,zbky->zbxy", cos_x, col_re, precision=highest) - jnp.einsum(
        "xk,zbky->zbxy", sin_x, col_im, precision=highest
    )


def sweep(
    source_re,
    source_im,
    inv_re,
    inv_im,
    couple,
    start_re,
    start_im,
    target_re,
    target_im,
    scale,
    reverse,
):
    depth = source_re.shape[0]
    blocks = depth // 8

    def fold(value):
        return value.reshape((blocks, 8) + value.shape[1:])

    cells = list(range(7, -1, -1)) if reverse else list(range(8))

    def block(carried, inputs):
        psi_real, psi_imag = carried
        rows_re, rows_im, aims_re, aims_im = inputs
        phi_real = [None] * 8
        phi_imag = [None] * 8
        sums = [None] * 8
        for cell in cells:
            sum_real = rows_re[cell] + couple * psi_real
            sum_imag = rows_im[cell] + couple * psi_imag
            psi_real = inv_re * sum_real - inv_im * sum_imag
            psi_imag = inv_re * sum_imag + inv_im * sum_real
            phi_real[cell] = jnp.sum(psi_real, axis=0) / 12.0
            phi_imag[cell] = jnp.sum(psi_imag, axis=0) / 12.0
            sums[cell] = (
                jnp.sum(psi_real * aims_re[cell] + psi_imag * aims_im[cell], axis=(2, 3)) * scale
            )
        return ((psi_real, psi_imag), (jnp.stack(phi_real), jnp.stack(phi_imag), jnp.stack(sums)))

    carried, outputs = lax.scan(
        block,
        (start_re, start_im),
        (fold(source_re), fold(source_im), fold(target_re), fold(target_im)),
        reverse=reverse,
    )

    def unfold(value):
        return value.reshape((depth,) + value.shape[2:])

    return (carried, unfold(outputs[0]), unfold(outputs[1]), unfold(outputs[2]))


def solve_modes(
    spec_re, spec_im, rates, speeds, shares, freq_x, freq_y, target_re, target_im, scale, wall_sum
):
    cosine, along_x, along_y = quadrature()
    rate = rates[:, None, None]
    speed = speeds[:, None, None]
    source_re = spec_re * rate
    source_im = spec_im * rate
    wave = speed[None] * (
        along_x[:, None, None, None] * freq_x[:, None]
        + along_y[:, None, None, None] * freq_y[None, :]
    )
    couple = jnp.abs(cosine)[:, None, None, None] * speed[None]
    real_part = rate[None] + couple
    denom = real_part * real_part + wave * wave
    inv_re = real_part / denom
    inv_im = -wave / denom
    zeros = jnp.zeros_like(inv_re[:6])
    down_end, down_re, down_im, down_grad = sweep(
        source_re,
        source_im,
        inv_re[:6],
        inv_im[:6],
        couple[:6],
        zeros,
        zeros,
        target_re,
        target_im,
        scale,
        True,
    )
    weight = (jnp.abs(cosine[:6]) / 12.0)[:, None, None, None]
    flux_re = jnp.sum(weight * down_end[0], axis=(0, 1))
    flux_im = jnp.sum(weight * down_end[1], axis=(0, 1))
    flux_re, flux_im = wall_sum(flux_re, flux_im)
    share = shares[:, None, None]
    start_re = jnp.broadcast_to(share * flux_re, zeros.shape)
    start_im = jnp.broadcast_to(share * flux_im, zeros.shape)
    up_end, up_re, up_im, up_grad = sweep(
        source_re,
        source_im,
        inv_re[6:],
        inv_im[6:],
        couple[6:],
        start_re,
        start_im,
        target_re,
        target_im,
        scale,
        False,
    )
    return (down_re + up_re, down_im + up_im, jnp.concatenate([down_grad, up_grad], axis=1))


def body(phi_start, coeff, forward, rates, speeds, shares):
    depth_local, band_local, width_x, width_y = phi_start.shape
    cos_x, sin_x = tables(width_x)
    cos_y, sin_y = tables(width_y)
    scale = 1.0 / width_x
    freq_y = frequency(width_y, 0, width_y)
    width_modes = forward.shape[3]
    freq_x = frequency(width_x, lax.axis_index("gx") * width_modes, width_modes)
    band_rates, band_speeds, band_shares = (rates, speeds, shares)

    def wall(flux_re, flux_im):
        return lax.psum((flux_re, flux_im), "ba")

    phi = phi_start
    total = None
    for step in range(forward.shape[0]):
        spec_re, spec_im = forward_transform(phi, cos_x, sin_x, cos_y, sin_y)
        mode_re = lax.all_to_all(spec_re, "gx", split_axis=2, concat_axis=0, tiled=True)
        mode_im = lax.all_to_all(spec_im, "gx", split_axis=2, concat_axis=0, tiled=True)
        new_re, new_im, grad_step = solve_modes(
            mode_re,
            mode_im,
            band_rates,
            band_speeds,
            band_shares,
            freq_x,
            freq_y,
            forward[step, 0],
            forward[step, 1],
            scale,
            wall,
        )
        total = grad_step if step == 0 else total + grad_step
        back_re = lax.all_to_all(new_re, "gx", split_axis=0, concat_axis=2, tiled=True)
        back_im = lax.all_to_all(new_im, "gx", split_axis=0, concat_axis=2, tiled=True)
        phi = coeff[:, None] * inverse_transform(back_re, back_im, cos_x, sin_x, cos_y, sin_y)
    return (phi, lax.psum_scatter(total, "gx", scatter_dimension=0, tiled=True))


def solution(mesh):
    in_specs = (
        P("gx", "ba", None, None),
        P("gx", None, None),
        P(None, None, None, "gx", None),
        P("ba"),
        P("ba"),
        P("ba"),
    )
    out_specs = (P("gx", "ba", None, None), P("gx", None, "ba"))
    return jax.shard_map(body, mesh=mesh, in_specs=in_specs, out_specs=out_specs, check_vma=False)
```

profile of v0, /device:TPU:0, one launch (start us, length us, event | category | flops | bytes accessed | tf_op | source)
XLA Modules:
  0.0 2943.7 jit_solution(5675500133150806077)
XLA Ops:
  7.2 18.8 fusion.61
  26.0 14.8 fusion.80
  48.5 11.0 add_bitcast_fusion.1
  59.5 10.3 copy.281
  74.9 11.1 fusion.4
  86.0 13.1 subtract_bitcast_fusion.1
  99.1 10.3 copy.283
  109.4 60.1 %all-to-all-done = f32[8,4,256,256]{3,1,0,2:T(4,128)} async-done(((f32[8,4,256,256]{3,1,0,2:T(4,128)}), f32[8,4,256,256]{3,1,0,2:T(4,128)}, u32[]{:S(2)}, u32[]{:S(2)}) %all-to-all-start) | async-done | bytes 8388640 | tf_op jit(solution)/shard_map/all_to_all | solution.py:181
  184.7 11.4 copy.282
  196.1 72.3 %all-to-all-done.1 = f32[8,4,256,256]{3,1,0,2:T(4,128)} async-done(((f32[8,4,256,256]{3,1,0,2:T(4,128)}), f32[8,4,256,256]{3,1,0,2:T(4,128)}, u32[]{:S(2)}, u32[]{:S(2)}) %all-to-all-start.1) | async-done | bytes 8388640 | tf_op jit(solution)/shard_map/all_to_all | solution.py:182
  268.5 11.8 copy.284
  308.8 340.4 %while.84 = (s32[]{:T(128)}, f32[6,4,32,256]{3,2,1,0:T(8,128)}, f32[6,4,32,256]{3,2,1,0:T(8,128)}, f32[8,8,4,32,256]{4,3,2,1,0:T(8,128)}, f32[8,8,4,32,256]{4,3,...) while((s32[]{:T(128)}, f32[6,4,32,256]{3,2,1,0:T(8,128)}, ...), condition=%wide.region_25.26_spmd.clone, body=%wide.region_0.25_spmd.clone.sunk | while | flops 25559048 | bytes 63492708 | solution.py:97
  652.0 34.4 %all-reduce.8.cloned.1.call-done = (f32[32,256]{1,0:T(8,128)}, f32[32,256]{1,0:T(8,128)}) async-done(((f32[32,256]{1,0:T(8,128)}, f32[32,256]{1,0:T(8,128)}), (f32[32,256]{1,0:T(8,128)}, f32[32,256]{1,0:T(8,128)})) %all-reduce.8.cloned.1.call-update) | async-done | bytes 65552 | tf_op jit(solution)/shard_map/psum | solution.py:175
  698.5 470.6 %while.82 = (s32[]{:T(128)}, f32[6,4,32,256]{3,2,1,0:T(8,128)}, f32[6,4,32,256]{3,2,1,0:T(8,128)}, f32[8,8,4,32,256]{4,3,2,1,0:T(8,128)}, f32[8,8,4,32,256]{4,3,...) while((s32[]{:T(128)}, f32[6,4,32,256]{3,2,1,0:T(8,128)}, ...), condition=%wide.region_55.56_spmd, body=%wide.region_30.55_spmd.sunk | while | flops 25165832 | bytes 46443788 | solution.py:97
  706.4 8.6 add_reduce_fusion.64
  765.2 8.6 add_reduce_fusion.64
  824.0 8.6 add_reduce_fusion.64
  882.8 8.6 add_reduce_fusion.64
  941.6 8.6 add_reduce_fusion.64
  1000.4 8.6 add_reduce_fusion.64
  1169.1 12.5 add.1907
  1186.6 12.2 add.1909
  1198.8 81.9 %all-to-all-done.2 = f32[64,4,32,256]{3,2,1,0:T(8,128)} async-done(((f32[64,4,32,256]{3,2,1,0:T(8,128)}), f32[64,4,32,256]{3,2,1,0:T(8,128)}, u32[]{:S(2)}, u32[]{:S(2)}) %all-to-all-start.2) | async-done | bytes 8388640 | tf_op jit(solution)/shard_map/all_to_all | solution.py:197
  1293.1 10.8 fusion.55
  1303.9 10.8 fusion.76
  1314.7 65.5 %all-to-all-done.3 = f32[64,4,32,256]{3,2,1,0:T(8,128)} async-done(((f32[64,4,32,256]{3,2,1,0:T(8,128)}), f32[64,4,32,256]{3,2,1,0:T(8,128)}, u32[]{:S(2)}, u32[]{:S(2)}) %all-to-all-start.3) | async-done | bytes 8388640 | tf_op jit(solution)/shard_map/all_to_all | solution.py:198
  1384.5 11.0 fusion.73
  1395.5 10.8 fusion.57
  1406.3 19.7 fusion.16
  1426.0 21.4 bitcast_multiply_fusion.1
  1447.4 12.1 fusion.71
  1459.5 15.1 fusion.52
  1474.6 14.1 fusion.69
  1488.7 17.6 add_bitcast_fusion
  1506.3 10.3 copy.297
  1521.8 11.1 fusion.49
  1532.9 19.4 subtract_bitcast_fusion
  1552.3 10.3 copy.301
  1562.6 53.3 %all-to-all-done.4 = f32[8,4,256,256]{3,1,0,2:T(4,128)} async-done(((f32[8,4,256,256]{3,1,0,2:T(4,128)}), f32[8,4,256,256]{3,1,0,2:T(4,128)}, u32[]{:S(2)}, u32[]{:S(2)}) %all-to-all-start.4) | async-done | bytes 8388640 | tf_op jit(solution)/shard_map/all_to_all | solution.py:181
  1621.1 11.4 copy.298
  1632.5 82.3 %all-to-all-done.5 = f32[8,4,256,256]{3,1,0,2:T(4,128)} async-done(((f32[8,4,256,256]{3,1,0,2:T(4,128)}), f32[8,4,256,256]{3,1,0,2:T(4,128)}, u32[]{:S(2)}, u32[]{:S(2)}) %all-to-all-start.5) | async-done | bytes 8388640 | tf_op jit(solution)/shard_map/all_to_all | solution.py:182
  1714.9 11.8 copy.302
  1755.5 327.7 %while.85 = (s32[]{:T(128)}, f32[6,4,32,256]{3,2,1,0:T(8,128)S(1)}, f32[6,4,32,256]{3,2,1,0:T(8,128)S(1)}, f32[8,8,4,32,256]{4,3,2,1,0:T(8,128)}, f32[8,8,4,32,2...) while((s32[]{:T(128)}, f32[6,4,32,256]{3,2,1,0:T(8,128)S(1)}, ...), condition=%wide.region_81.82_spmd.clone, body=%wide.region_56.81_spmd.clone.sunk | while | flops 25559048 | bytes 63492708 | solution.py:97
  2084.6 32.1 %all-reduce.6.cloned.1.call-done = (f32[32,256]{1,0:T(8,128)}, f32[32,256]{1,0:T(8,128)}) async-done(((f32[32,256]{1,0:T(8,128)}, f32[32,256]{1,0:T(8,128)}), (f32[32,256]{1,0:T(8,128)}, f32[32,256]{1,0:T(8,128)})) %all-reduce.6.cloned.1.call-update) | async-done | bytes 65552 | tf_op jit(solution)/shard_map/psum | solution.py:175
  2128.8 476.6 %while.83 = (s32[]{:T(128)}, f32[6,4,32,256]{3,2,1,0:T(8,128)}, f32[6,4,32,256]{3,2,1,0:T(8,128)}, f32[8,8,4,32,256]{4,3,2,1,0:T(8,128)}, f32[8,8,4,32,256]{4,3,...) while((s32[]{:T(128)}, f32[6,4,32,256]{3,2,1,0:T(8,128)}, ...), condition=%wide.region_111.112_spmd, body=%wide.region_86.111_spmd.sunk | while | flops 25165832 | bytes 46443368 | solution.py:97
  2137.3 8.6 add_reduce_fusion.72
  2196.9 8.6 add_reduce_fusion.72
  2256.5 8.6 add_reduce_fusion.72
  2316.0 8.6 add_reduce_fusion.72
  2375.6 8.6 add_reduce_fusion.72
  2435.1 8.6 add_reduce_fusion.72
  2494.7 8.6 add_reduce_fusion.72
  2554.2 8.6 add_reduce_fusion.72
  2605.4 12.0 add.1914
  2622.3 12.2 add.1916
  2634.5 81.9 %all-to-all-done.6 = f32[64,4,32,256]{3,2,1,0:T(8,128)} async-done(((f32[64,4,32,256]{3,2,1,0:T(8,128)}), f32[64,4,32,256]{3,2,1,0:T(8,128)}, u32[]{:S(2)}, u32[]{:S(2)}) %all-to-all-start.6) | async-done | bytes 8388640 | tf_op jit(solution)/shard_map/all_to_all | solution.py:197
  2723.5 110.1 %all-reduce = f32[64,12,4]{1,2,0:T(4,128)S(1)} all-reduce(f32[64,12,4]{1,2,0:T(4,128)S(1)} %copy.315), channel_id=2, replica_groups=mesh['gx'=8,'ba'=4] {'gx'}, use_global_device_ids=true, to_apply=%region_112.113.clone | all-reduce | flops 3072 | bytes 24576
  2838.5 10.8 fusion.45
  2849.3 10.8 fusion.66
  2864.3 11.3 fusion.63
  2875.6 10.8 fusion.47
  2886.4 19.7 fusion.12
  2906.1 21.3 bitcast_multiply_fusion
  2927.5 9.1 copy.316
  (2754 shorter events, 1656.1 us)
Async XLA Ops:
  7.2 18.8 copy-start.13
  26.0 22.5 copy-start.10
  69.8 99.7 %all-to-all-start = ((f32[8,4,256,256]{3,1,0,2:T(4,128)}), f32[8,4,256,256]{3,1,0,2:T(4,128)}, u32[]{:S(2)}, u32[]{:S(2)}) async-start(f32[8,4,256,256]{3,1,0,2:T(4,128)} %copy.281), calls=%async_computation | async-start | bytes 16777216 | tf_op jit(solution)/shard_map/all_to_all | solution.py:181
  109.4 66.2 %copy-start.78 = (f32[4]{0:T(128)S(1)}, f32[4]{0:T(128)}, u32[]{:S(2)}) copy-start(f32[4]{0:T(128)} %param.18) | copy-start | bytes 52
  109.4 67.0 %copy-start.76 = (f32[4]{0:T(128)S(1)}, f32[4]{0:T(128)}, u32[]{:S(2)}) copy-start(f32[4]{0:T(128)} %param.17) | copy-start | bytes 52
  169.4 99.0 %all-to-all-start.1 = ((f32[8,4,256,256]{3,1,0,2:T(4,128)}), f32[8,4,256,256]{3,1,0,2:T(4,128)}, u32[]{:S(2)}, u32[]{:S(2)}) async-start(f32[8,4,256,256]{3,1,0,2:T(4,128)} %copy.283), calls=%async_computation.1 | async-start | bytes 16777216 | tf_op jit(solution)/shard_map/all_to_all | solution.py:182
  174.4 512.0 %all-reduce.8.cloned.1.call-start = ((), (), s32[]{:S(2)}) async-start(), calls=%async_computation.9 | async-start | bytes 131072 | tf_op jit(solution)/shard_map/psum | solution.py:175
  326.9 15.9 copy-start.20
  369.5 15.9 copy-start.20
  412.2 15.9 copy-start.20
  454.8 15.9 copy-start.20
  497.4 15.9 copy-start.20
  540.1 15.9 copy-start.20
  582.7 15.9 copy-start.20
  625.3 15.9 copy-start.20
  649.2 48.6 %copy-start = (f32[6,4,32,256]{3,2,1,0:T(8,128)}, f32[6,4,32,256]{3,2,1,0:T(8,128)S(1)}, u32[]{:S(2)}) copy-start(f32[6,4,32,256]{3,2,1,0:T(8,128)S(1)} %get-tuple-element.2653) | copy-start | bytes 2359300
  649.2 48.6 %copy-start.2 = (f32[6,4,32,256]{3,2,1,0:T(8,128)}, f32[6,4,32,256]{3,2,1,0:T(8,128)S(1)}, u32[]{:S(2)}) copy-start(f32[6,4,32,256]{3,2,1,0:T(8,128)S(1)} %get-tuple-element.2654) | copy-start | bytes 2359300
  714.9 35.5 %copy-start.18 = (f32[4,32,256]{2,1,0:T(8,128)S(1)}, f32[4,32,256]{2,1,0:T(8,128)}, u32[]{:S(2)}) copy-start(f32[4,32,256]{2,1,0:T(8,128)} %get-tuple-element.2103) | copy-start | bytes 393220 | tf_op jit(solution)/shard_map/while
  714.9 41.1 %copy-start.16 = (f32[4,32,256]{2,1,0:T(8,128)S(1)}, f32[4,32,256]{2,1,0:T(8,128)}, u32[]{:S(2)}) copy-start(f32[4,32,256]{2,1,0:T(8,128)} %get-tuple-element.2095) | copy-start | bytes 393220 | tf_op jit(solution)/shard_map/while
  773.7 35.5 %copy-start.18 = (f32[4,32,256]{2,1,0:T(8,128)S(1)}, f32[4,32,256]{2,1,0:T(8,128)}, u32[]{:S(2)}) copy-start(f32[4,32,256]{2,1,0:T(8,128)} %get-tuple-element.2103) | copy-start | bytes 393220 | tf_op jit(solution)/shard_map/while
  773.7 41.1 %copy-start.16 = (f32[4,32,256]{2,1,0:T(8,128)S(1)}, f32[4,32,256]{2,1,0:T(8,128)}, u32[]{:S(2)}) copy-start(f32[4,32,256]{2,1,0:T(8,128)} %get-tuple-element.2095) | copy-start | bytes 393220 | tf_op jit(solution)/shard_map/while
  832.6 35.5 %copy-start.18 = (f32[4,32,256]{2,1,0:T(8,128)S(1)}, f32[4,32,256]{2,1,0:T(8,128)}, u32[]{:S(2)}) copy-start(f32[4,32,256]{2,1,0:T(8,128)} %get-tuple-element.2103) | copy-start | bytes 393220 | tf_op jit(solution)/shard_map/while
  832.6 41.1 %copy-start.16 = (f32[4,32,256]{2,1,0:T(8,128)S(1)}, f32[4,32,256]{2,1,0:T(8,128)}, u32[]{:S(2)}) copy-start(f32[4,32,256]{2,1,0:T(8,128)} %get-tuple-element.2095) | copy-start | bytes 393220 | tf_op jit(solution)/shard_map/while
  891.4 35.5 %copy-start.18 = (f32[4,32,256]{2,1,0:T(8,128)S(1)}, f32[4,32,256]{2,1,0:T(8,128)}, u32[]{:S(2)}) copy-start(f32[4,32,256]{2,1,0:T(8,128)} %get-tuple-element.2103) | copy-start | bytes 393220 | tf_op jit(solution)/shard_map/while
  891.4 41.1 %copy-start.16 = (f32[4,32,256]{2,1,0:T(8,128)S(1)}, f32[4,32,256]{2,1,0:T(8,128)}, u32[]{:S(2)}) copy-start(f32[4,32,256]{2,1,0:T(8,128)} %get-tuple-element.2095) | copy-start | bytes 393220 | tf_op jit(solution)/shard_map/while
  950.2 35.5 %copy-start.18 = (f32[4,32,256]{2,1,0:T(8,128)S(1)}, f32[4,32,256]{2,1,0:T(8,128)}, u32[]{:S(2)}) copy-start(f32[4,32,256]{2,1,0:T(8,128)} %get-tuple-element.2103) | copy-start | bytes 393220 | tf_op jit(solution)/shard_map/while
  950.2 41.1 %copy-start.16 = (f32[4,32,256]{2,1,0:T(8,128)S(1)}, f32[4,32,256]{2,1,0:T(8,128)}, u32[]{:S(2)}) copy-start(f32[4,32,256]{2,1,0:T(8,128)} %get-tuple-element.2095) | copy-start | bytes 393220 | tf_op jit(solution)/shard_map/while
  1008.9 35.5 %copy-start.18 = (f32[4,32,256]{2,1,0:T(8,128)S(1)}, f32[4,32,256]{2,1,0:T(8,128)}, u32[]{:S(2)}) copy-start(f32[4,32,256]{2,1,0:T(8,128)} %get-tuple-element.2103) | copy-start | bytes 393220 | tf_op jit(solution)/shard_map/while
  1008.9 41.1 %copy-start.16 = (f32[4,32,256]{2,1,0:T(8,128)S(1)}, f32[4,32,256]{2,1,0:T(8,128)}, u32[]{:S(2)}) copy-start(f32[4,32,256]{2,1,0:T(8,128)} %get-tuple-element.2095) | copy-start | bytes 393220 | tf_op jit(solution)/shard_map/while
  1067.8 35.5 %copy-start.18 = (f32[4,32,256]{2,1,0:T(8,128)S(1)}, f32[4,32,256]{2,1,0:T(8,128)}, u32[]{:S(2)}) copy-start(f32[4,32,256]{2,1,0:T(8,128)} %get-tuple-element.2103) | copy-start | bytes 393220 | tf_op jit(solution)/shard_map/while
  1067.8 41.1 %copy-start.16 = (f32[4,32,256]{2,1,0:T(8,128)S(1)}, f32[4,32,256]{2,1,0:T(8,128)}, u32[]{:S(2)}) copy-start(f32[4,32,256]{2,1,0:T(8,128)} %get-tuple-element.2095) | copy-start | bytes 393220 | tf_op jit(solution)/shard_map/while
  1126.6 35.5 %copy-start.18 = (f32[4,32,256]{2,1,0:T(8,128)S(1)}, f32[4,32,256]{2,1,0:T(8,128)}, u32[]{:S(2)}) copy-start(f32[4,32,256]{2,1,0:T(8,128)} %get-tuple-element.2103) | copy-start | bytes 393220 | tf_op jit(solution)/shard_map/while
  1126.6 41.1 %copy-start.16 = (f32[4,32,256]{2,1,0:T(8,128)S(1)}, f32[4,32,256]{2,1,0:T(8,128)}, u32[]{:S(2)}) copy-start(f32[4,32,256]{2,1,0:T(8,128)} %get-tuple-element.2095) | copy-start | bytes 393220 | tf_op jit(solution)/shard_map/while
  1181.7 99.0 %all-to-all-start.2 = ((f32[64,4,32,256]{3,2,1,0:T(8,128)}), f32[64,4,32,256]{3,2,1,0:T(8,128)}, u32[]{:S(2)}, u32[]{:S(2)}) async-start(f32[64,4,32,256]{3,2,1,0:T(8,128)} %bitcast.875), calls=%async_computation.2 | async-start | bytes 16777216 | tf_op jit(solution)/shard_map/all_to_all | solution.py:197
  1280.7 99.5 %all-to-all-start.3 = ((f32[64,4,32,256]{3,2,1,0:T(8,128)}), f32[64,4,32,256]{3,2,1,0:T(8,128)}, u32[]{:S(2)}, u32[]{:S(2)}) async-start(f32[64,4,32,256]{3,2,1,0:T(8,128)} %bitcast.870), calls=%async_computation.3 | async-start | bytes 16777216 | tf_op jit(solution)/shard_map/all_to_all | solution.py:198
  1288.1 137.9 %copy-start.14 = (f32[8,256,256]{1,2,0:T(8,128)}, f32[8,256,256]{1,2,0:T(8,128)S(1)}, u32[]{:S(2)}) copy-start(f32[8,256,256]{1,2,0:T(8,128)S(1)} %copy.278) | copy-start | bytes 6291460
  1384.5 21.8 slice-start
  1516.6 99.2 %all-to-all-start.4 = ((f32[8,4,256,256]{3,1,0,2:T(4,128)}), f32[8,4,256,256]{3,1,0,2:T(4,128)}, u32[]{:S(2)}, u32[]{:S(2)}) async-start(f32[8,4,256,256]{3,1,0,2:T(4,128)} %copy.297), calls=%async_computation.4 | async-start | bytes 16777216 | tf_op jit(solution)/shard_map/all_to_all | solution.py:181
  1615.8 99.0 %all-to-all-start.5 = ((f32[8,4,256,256]{3,1,0,2:T(4,128)}), f32[8,4,256,256]{3,1,0,2:T(4,128)}, u32[]{:S(2)}, u32[]{:S(2)}) async-start(f32[8,4,256,256]{3,1,0,2:T(4,128)} %copy.301), calls=%async_computation.5 | async-start | bytes 16777216 | tf_op jit(solution)/shard_map/all_to_all | solution.py:182
  1620.8 495.9 %all-reduce.6.cloned.1.call-start = ((), (), s32[]{:S(2)}) async-start(), calls=%async_computation.8 | async-start | bytes 131072 | tf_op jit(solution)/shard_map/psum | solution.py:175
  1632.5 94.1 %copy-start.77 = (f32[4]{0:T(128)S(1)}, f32[4]{0:T(128)}, u32[]{:S(2)}) copy-start(f32[4]{0:T(128)} %param.17) | copy-start | bytes 52
  1773.7 14.7 copy-start.21
  1814.7 14.7 copy-start.21
  1855.6 14.7 copy-start.21
  1896.6 14.8 copy-start.21
  2145.9 35.5 %copy-start.19 = (f32[4,32,256]{2,1,0:T(8,128)S(1)}, f32[4,32,256]{2,1,0:T(8,128)}, u32[]{:S(2)}) copy-start(f32[4,32,256]{2,1,0:T(8,128)} %get-tuple-element.2190) | copy-start | bytes 393220 | tf_op jit(solution)/shard_map/while
  2145.9 41.1 %copy-start.17 = (f32[4,32,256]{2,1,0:T(8,128)S(1)}, f32[4,32,256]{2,1,0:T(8,128)}, u32[]{:S(2)}) copy-start(f32[4,32,256]{2,1,0:T(8,128)} %get-tuple-element.2182) | copy-start | bytes 393220 | tf_op jit(solution)/shard_map/while
  2205.5 35.5 %copy-start.19 = (f32[4,32,256]{2,1,0:T(8,128)S(1)}, f32[4,32,256]{2,1,0:T(8,128)}, u32[]{:S(2)}) copy-start(f32[4,32,256]{2,1,0:T(8,128)} %get-tuple-element.2190) | copy-start | bytes 393220 | tf_op jit(solution)/shard_map/while
  2205.5 41.1 %copy-start.17 = (f32[4,32,256]{2,1,0:T(8,128)S(1)}, f32[4,32,256]{2,1,0:T(8,128)}, u32[]{:S(2)}) copy-start(f32[4,32,256]{2,1,0:T(8,128)} %get-tuple-element.2182) | copy-start | bytes 393220 | tf_op jit(solution)/shard_map/while
  2265.0 35.5 %copy-start.19 = (f32[4,32,256]{2,1,0:T(8,128)S(1)}, f32[4,32,256]{2,1,0:T(8,128)}, u32[]{:S(2)}) copy-start(f32[4,32,256]{2,1,0:T(8,128)} %get-tuple-element.2190) | copy-start | bytes 393220 | tf_op jit(solution)/shard_map/while
  2265.1 41.1 %copy-start.17 = (f32[4,32,256]{2,1,0:T(8,128)S(1)}, f32[4,32,256]{2,1,0:T(8,128)}, u32[]{:S(2)}) copy-start(f32[4,32,256]{2,1,0:T(8,128)} %get-tuple-element.2182) | copy-start | bytes 393220 | tf_op jit(solution)/shard_map/while
  2324.6 35.5 %copy-start.19 = (f32[4,32,256]{2,1,0:T(8,128)S(1)}, f32[4,32,256]{2,1,0:T(8,128)}, u32[]{:S(2)}) copy-start(f32[4,32,256]{2,1,0:T(8,128)} %get-tuple-element.2190) | copy-start | bytes 393220 | tf_op jit(solution)/shard_map/while
  2324.6 41.1 %copy-start.17 = (f32[4,32,256]{2,1,0:T(8,128)S(1)}, f32[4,32,256]{2,1,0:T(8,128)}, u32[]{:S(2)}) copy-start(f32[4,32,256]{2,1,0:T(8,128)} %get-tuple-element.2182) | copy-start | bytes 393220 | tf_op jit(solution)/shard_map/while
  2384.2 35.5 %copy-start.19 = (f32[4,32,256]{2,1,0:T(8,128)S(1)}, f32[4,32,256]{2,1,0:T(8,128)}, u32[]{:S(2)}) copy-start(f32[4,32,256]{2,1,0:T(8,128)} %get-tuple-element.2190) | copy-start | bytes 393220 | tf_op jit(solution)/shard_map/while
  2384.2 41.1 %copy-start.17 = (f32[4,32,256]{2,1,0:T(8,128)S(1)}, f32[4,32,256]{2,1,0:T(8,128)}, u32[]{:S(2)}) copy-start(f32[4,32,256]{2,1,0:T(8,128)} %get-tuple-element.2182) | copy-start | bytes 393220 | tf_op jit(solution)/shard_map/while
  2443.7 35.5 %copy-start.19 = (f32[4,32,256]{2,1,0:T(8,128)S(1)}, f32[4,32,256]{2,1,0:T(8,128)}, u32[]{:S(2)}) copy-start(f32[4,32,256]{2,1,0:T(8,128)} %get-tuple-element.2190) | copy-start | bytes 393220 | tf_op jit(solution)/shard_map/while
  2443.7 41.1 %copy-start.17 = (f32[4,32,256]{2,1,0:T(8,128)S(1)}, f32[4,32,256]{2,1,0:T(8,128)}, u32[]{:S(2)}) copy-start(f32[4,32,256]{2,1,0:T(8,128)} %get-tuple-element.2182) | copy-start | bytes 393220 | tf_op jit(solution)/shard_map/while
  2503.3 35.5 %copy-start.19 = (f32[4,32,256]{2,1,0:T(8,128)S(1)}, f32[4,32,256]{2,1,0:T(8,128)}, u32[]{:S(2)}) copy-start(f32[4,32,256]{2,1,0:T(8,128)} %get-tuple-element.2190) | copy-start | bytes 393220 | tf_op jit(solution)/shard_map/while
  2503.3 41.1 %copy-start.17 = (f32[4,32,256]{2,1,0:T(8,128)S(1)}, f32[4,32,256]{2,1,0:T(8,128)}, u32[]{:S(2)}) copy-start(f32[4,32,256]{2,1,0:T(8,128)} %get-tuple-element.2182) | copy-start | bytes 393220 | tf_op jit(solution)/shard_map/while
  2562.8 35.5 %copy-start.19 = (f32[4,32,256]{2,1,0:T(8,128)S(1)}, f32[4,32,256]{2,1,0:T(8,128)}, u32[]{:S(2)}) copy-start(f32[4,32,256]{2,1,0:T(8,128)} %get-tuple-element.2190) | copy-start | bytes 393220 | tf_op jit(solution)/shard_map/while
  2562.8 41.1 %copy-start.17 = (f32[4,32,256]{2,1,0:T(8,128)S(1)}, f32[4,32,256]{2,1,0:T(8,128)}, u32[]{:S(2)}) copy-start(f32[4,32,256]{2,1,0:T(8,128)} %get-tuple-element.2182) | copy-start | bytes 393220 | tf_op jit(solution)/shard_map/while
  2617.4 99.0 %all-to-all-start.6 = ((f32[64,4,32,256]{3,2,1,0:T(8,128)}), f32[64,4,32,256]{3,2,1,0:T(8,128)}, u32[]{:S(2)}, u32[]{:S(2)}) async-start(f32[64,4,32,256]{3,2,1,0:T(8,128)} %bitcast.876), calls=%async_computation.6 | async-start | bytes 16777216 | tf_op jit(solution)/shard_map/all_to_all | solution.py:197
  2716.4 143.6 %all-to-all-start.7 = ((f32[64,4,32,256]{3,2,1,0:T(8,128)}), f32[64,4,32,256]{3,2,1,0:T(8,128)}, u32[]{:S(2)}, u32[]{:S(2)}) async-start(f32[64,4,32,256]{3,2,1,0:T(8,128)} %bitcast.869), calls=%async_computation.7 | async-start | bytes 16777216 | tf_op jit(solution)/shard_map/all_to_all | solution.py:198
  2886.4 19.7 copy-start.15
  (413 other events, 2449.0 us)
Sparse Core Ops, SparseCore 0:
  652.1 34.2 all-reduce.7
  2084.7 31.9 all-reduce.5
where the time goes:
time: 2980 us; the launch traced here: 2940 us
  other arithmetic  1160 us (39%)
  local copies, waits for them, and re-layouts  712 us (24%)
  waiting for transfers between devices  564 us (19%)
  matrix products  335 us (11%)
  blocking collectives  110 us (4%)
  starting transfers between devices  41.5 us (1%)
    reduce_sum x256, other arithmetic, block(): jnp.sum(psi_real * aims_re[cell] + psi_imag * aims_im[cell], axis=(2, 3))  599 us
    while x448, other arithmetic  397 us
    all_to_all x2, waiting for transfers between devices, body(): lax.all_to_all(new_re, 'gx', split_axis=0, concat_axis=2, tiled=True)  164 us
    all_to_all x2, waiting for transfers between devices, body(): lax.all_to_all(spec_im, 'gx', split_axis=2, concat_axis=0, tiled=True)  155 us
    mul x256, local copies, waits for them, and re-layouts, block(): jnp.sum(psi_real * aims_re[cell] + psi_imag * aims_im[cell], axis=(2, 3))  123 us
    all_to_all x2, waiting for transfers between devices, body(): lax.all_to_all(spec_re, 'gx', split_axis=2, concat_axis=0, tiled=True)  113 us
    unnamed x1, blocking collectives  110 us
    mul x256, other arithmetic, block(): jnp.sum(psi_real * aims_re[cell] + psi_imag * aims_im[cell], axis=(2, 3))  93.1 us
  transfers between devices with their start and end apart: 10, of which 9 were waited for; matrix products, arithmetic and copies ran while one was open for 6% of the time, Pallas kernels for 0%

commit v1 on v0

v1 whole, which is shorter than its diff:
```python
import functools
import math

import jax
import jax.numpy as jnp
import ml_dtypes
import numpy as np
from jax import lax
from jax.experimental import pallas as pl
from jax.experimental.pallas import tpu as pltpu
from jax.sharding import PartitionSpec as P

LANES = 128
VMEM = 56 * 1024 * 1024
CHUNK_ROWS = 16


def split_host(table):
    high = table.astype(ml_dtypes.bfloat16)
    low = (table - high.astype(np.float64)).astype(ml_dtypes.bfloat16)
    return high, low


def tables(count):
    half = count // 2
    index = np.arange(count)
    angle = (np.outer(index, index) % count) * (2.0 * np.pi / count)
    cos, sin = np.cos(angle) / math.sqrt(count), np.sin(angle) / math.sqrt(count)
    alternate = np.where(index % 2 == 0, 1.0, -1.0) / math.sqrt(count)
    into = np.concatenate([cos[:, :half], alternate[:, None], -sin[:, 1:half]], axis=1)
    weight = np.where(np.arange(half) == 0, 1.0, 2.0)[:, None]
    back = np.concatenate([weight * cos[:half], alternate[None], -2.0 * sin[1:half]], axis=0) / 12.0
    stacked = np.concatenate([cos, sin], axis=0)
    beside = np.concatenate([cos, sin], axis=1)
    return [part for table in (into, stacked, beside, back) for part in split_host(table)]


def quadrature():
    level = np.arange(6)
    polar = 0.2 + 0.15 * level
    cosine = np.concatenate([-polar, polar])
    azimuth = np.concatenate([level * (np.pi / 3.0) + np.pi / 6.0, level * (np.pi / 3.0)])
    sine = np.sqrt(1.0 - cosine * cosine)
    return (cosine, sine * np.cos(azimuth), sine * np.sin(azimuth))


def split(value):
    high = value.astype(jnp.bfloat16)
    low = (value - high.astype(jnp.float32)).astype(jnp.bfloat16)
    return high, low


def dot(left, right):
    return jnp.dot(left, right, preferred_element_type=jnp.float32)


def dot3(left, right):
    return dot(left[0], right[0]) + (dot(left[0], right[1]) + dot(left[1], right[0]))


class Plan:
    def __init__(self, shards, cells, bands, width, rows):
        self.shards, self.cells, self.bands, self.width, self.rows = shards, cells, bands, width, rows
        self.half = width // 2
        self.chunk = min(CHUNK_ROWS, rows)
        self.chunks = rows // self.chunk
        self.tiles = self.chunk // 2
        self.main = 2 * bands * self.chunk
        self.depth = shards * cells

    def height(self, chunk):
        return self.main + (16 if chunk == 0 else 0)

    def shape(self, chunk):
        return (self.shards, self.cells, self.height(chunk), LANES)


def forward_slabs(plan, phis, into, stacked, outs):
    width, half, rows, chunk = plan.width, plan.half, plan.rows, plan.chunk
    lane = lax.broadcasted_iota(jnp.int32, (width, half), 1)
    first = lane == 0
    columns = jnp.zeros((width, half), jnp.float32)
    for band in range(plan.bands):
        packed = dot3(split(phis(band)), into)
        both = dot3(stacked, split(packed))
        cos_re, cos_im = both[:width, :half], both[:width, half:]
        sin_re, sin_im = both[width:, :half], both[width:, half:]
        real = cos_re + jnp.where(first, 0.0, sin_im)
        imag = jnp.where(first, 0.0, cos_im) - sin_re
        for at in range(plan.chunks):
            for shard in range(plan.shards):
                start = shard * rows + at * chunk
                outs[at][shard, 0, band * chunk : (band + 1) * chunk, :] = real[start : start + chunk]
                low = (plan.bands + band) * chunk
                outs[at][shard, 0, low : low + chunk, :] = imag[start : start + chunk]
        place = 2 * band + 1
        columns = jnp.where(lane == place, pltpu.roll(cos_im, place, 1), columns)
        columns = jnp.where(lane == place + 8, -pltpu.roll(sin_im, place + 8, 1), columns)
    turned = columns.T[:16]
    slot = lax.broadcasted_iota(jnp.int32, (16, LANES), 1)
    for shard in range(plan.shards):
        start = shard * rows
        piece = turned[:, start // LANES * LANES : start // LANES * LANES + LANES]
        if start % LANES:
            piece = pltpu.roll(piece, LANES - start % LANES, 1)
        outs[0][shard, 0, plan.main :, :] = jnp.where(slot < rows, piece, 0.0)


def inverse_slabs(plan, ins, beside, back, take):
    width, half, rows, chunk = plan.width, plan.half, plan.rows, plan.chunk
    slot = lax.broadcasted_iota(jnp.int32, (16, LANES), 1)
    pieces = []
    for group in range(width // LANES):
        piece = jnp.zeros((16, LANES), jnp.float32)
        for shard in range(plan.shards):
            start = shard * rows
            if start // LANES == group:
                held = ins[0][shard, 0, plan.main :, :]
                if start % LANES:
                    held = pltpu.roll(held, start % LANES, 1)
                inside = (slot >= start % LANES) & (slot < start % LANES + rows)
                piece = jnp.where(inside, held, piece)
        pieces.append(piece)
    turned = jnp.concatenate(pieces, axis=1)
    columns = jnp.concatenate([turned, jnp.zeros((LANES - 16, width), jnp.float32)], axis=0).T
    first = lax.broadcasted_iota(jnp.int32, (width, half), 1) == 0
    for band in range(plan.bands):
        reals, imags = [], []
        for shard in range(plan.shards):
            for at in range(plan.chunks):
                reals.append(ins[at][shard, 0, band * chunk : (band + 1) * chunk, :])
                low = (plan.bands + band) * chunk
                imags.append(ins[at][shard, 0, low : low + chunk, :])
        real, imag = jnp.concatenate(reals, axis=0), jnp.concatenate(imags, axis=0)
        place = 2 * band + 1
        side_re = pltpu.roll(columns, LANES - place, 1)
        side_im = pltpu.roll(columns, LANES - place - 8, 1)
        upper = jnp.concatenate([real, jnp.where(first, side_re, imag)], axis=1)
        lower = jnp.concatenate([-imag, jnp.where(first, -side_im, real)], axis=1)
        mixed = dot3(beside, split(jnp.concatenate([upper, lower], axis=0)))
        take(band, dot3(split(mixed), back))


def first_kernel(plan, phi, into_h, into_l, stacked_h, stacked_l, *outs):
    forward_slabs(plan, lambda band: phi[0, band], (into_h[...], into_l[...]), (stacked_h[...], stacked_l[...]), outs)


def middle_kernel(plan, *refs):
    ins = refs[: plan.chunks]
    coeff = refs[plan.chunks]
    into_h, into_l, stacked_h, stacked_l, beside_h, beside_l, back_h, back_l = refs[plan.chunks + 1 : plan.chunks + 9]
    outs = refs[plan.chunks + 9 : 2 * plan.chunks + 9]
    held = refs[2 * plan.chunks + 9]

    def take(band, value):
        held[band] = value * coeff[0]

    inverse_slabs(plan, ins, (beside_h[...], beside_l[...]), (back_h[...], back_l[...]), take)
    forward_slabs(plan, lambda band: held[band], (into_h[...], into_l[...]), (stacked_h[...], stacked_l[...]), outs)


def last_kernel(plan, *refs):
    ins = refs[: plan.chunks]
    coeff, beside_h, beside_l, back_h, back_l, out = refs[plan.chunks :]

    def take(band, value):
        out[0, band] = value * coeff[0]

    inverse_slabs(plan, ins, (beside_h[...], beside_l[...]), (back_h[...], back_l[...]), take)


def whole(array):
    rank = len(array.shape)
    return pl.BlockSpec(array.shape, lambda cell: (0,) * rank)


def chunk_specs(plan):
    return [pl.BlockSpec((plan.shards, 1, plan.height(at), LANES), lambda cell: (0, cell, 0, 0)) for at in range(plan.chunks)]


def chunk_shapes(plan):
    return [jax.ShapeDtypeStruct(plan.shape(at), jnp.float32) for at in range(plan.chunks)]


def slab_spec(plan):
    return pl.BlockSpec((1, plan.bands, plan.width, plan.width), lambda cell: (cell, 0, 0, 0))


def coeff_spec(plan):
    return pl.BlockSpec((1, plan.width, plan.width), lambda cell: (cell, 0, 0))


def cost(plan, transforms):
    slabs = plan.cells * plan.bands
    return pl.CostEstimate(
        flops=transforms * slabs * 18 * plan.width**3, bytes_accessed=16 * slabs * plan.width**2, transcendentals=0
    )


def first(plan, phi, consts):
    return pl.pallas_call(
        functools.partial(first_kernel, plan),
        grid=(plan.cells,),
        in_specs=[slab_spec(plan)] + [whole(c) for c in consts[:4]],
        out_specs=chunk_specs(plan),
        out_shape=chunk_shapes(plan),
        compiler_params=pltpu.CompilerParams(vmem_limit_bytes=VMEM),
        cost_estimate=cost(plan, 1),
        name="into_modes",
    )(phi, *consts[:4])


def middle(plan, ins, coeff, consts):
    return pl.pallas_call(
        functools.partial(middle_kernel, plan),
        grid=(plan.cells,),
        in_specs=chunk_specs(plan) + [coeff_spec(plan)] + [whole(c) for c in consts],
        out_specs=chunk_specs(plan),
        out_shape=chunk_shapes(plan),
        scratch_shapes=[pltpu.VMEM((plan.bands, plan.width, plan.width), jnp.float32)],
        compiler_params=pltpu.CompilerParams(vmem_limit_bytes=VMEM),
        cost_estimate=cost(plan, 2),
        name="between_steps",
    )(*ins, coeff, *consts)


def last(plan, ins, coeff, consts):
    return pl.pallas_call(
        functools.partial(last_kernel, plan),
        grid=(plan.cells,),
        in_specs=chunk_specs(plan) + [coeff_spec(plan)] + [whole(c) for c in consts[4:]],
        out_specs=slab_spec(plan),
        out_shape=jax.ShapeDtypeStruct((plan.cells, plan.bands, plan.width, plan.width), jnp.float32),
        compiler_params=pltpu.CompilerParams(vmem_limit_bytes=VMEM),
        cost_estimate=cost(plan, 1),
        name="out_of_modes",
    )(*ins, coeff, *consts[4:])


def sweep_kernel(plan, at, upward, *refs):
    if upward:
        spec, aims, inv, couple, rate, part, start, keep, out, sums, totals = refs
    else:
        spec, aims, inv, couple, rate, out, flux, sums, totals = refs
    tiles, step_rows, depth = plan.tiles, plan.tiles, plan.depth
    imag_at = plan.bands * plan.chunk
    even = lax.broadcasted_iota(jnp.int32, (8, LANES), 0) % 2 == 0
    unroll = 4

    def rows(base, tile):
        return pl.ds(base + tile, 8, stride=step_rows)

    for tile in range(tiles + (1 if at == 0 else 0)):
        extra = tile == tiles
        inv_re = [inv[0, d, tile] for d in range(6)]
        inv_im = [inv[1, d, tile] for d in range(6)]

        def block(count, psi, tile=tile, extra=extra, inv_re=inv_re, inv_im=inv_im):
            psi_re, psi_im = list(psi[:6]), list(psi[6:])
            for inner in range(unroll):
                z = count * unroll + inner
                z = z if upward else depth - 1 - z
                if extra:
                    row_re = jnp.where(even, spec[z, rows(0, 0), :], spec[z, plan.main : plan.main + 8, :])
                    row_im = jnp.where(even, spec[z, rows(imag_at, 0), :], spec[z, plan.main + 8 : plan.main + 16, :])
                else:
                    row_re = spec[z, rows(0, tile), :]
                    row_im = spec[z, rows(imag_at, tile), :]
                row_re, row_im = rate[...] * row_re, rate[...] * row_im
                aim_re, aim_im = aims[z, 0, tile], aims[z, 1, tile]
                for d in range(6):
                    sum_re = row_re + couple[d] * psi_re[d]
                    sum_im = row_im + couple[d] * psi_im[d]
                    psi_re[d] = inv_re[d] * sum_re - inv_im[d] * sum_im
                    psi_im[d] = inv_re[d] * sum_im + inv_im[d] * sum_re
                    product = psi_re[d] * aim_re + psi_im[d] * aim_im
                    totals[d, z] = product if tile == 0 else totals[d, z] + product
                new_re = ((psi_re[0] + psi_re[1]) + (psi_re[2] + psi_re[3])) + (psi_re[4] + psi_re[5])
                new_im = ((psi_im[0] + psi_im[1]) + (psi_im[2] + psi_im[3])) + (psi_im[4] + psi_im[5])
                if extra:
                    at_re, at_im = slice(plan.main, plan.main + 8), slice(plan.main + 8, plan.main + 16)
                else:
                    at_re, at_im = rows(0, tile), rows(imag_at, tile)
                if upward:
                    new_re, new_im = new_re + part[z, at_re, :], new_im + part[z, at_im, :]
                if upward and extra:
                    pair = even & (keep[...] > 0.0)
                    main_re, main_im = out[z, rows(0, 0), :], out[z, rows(imag_at, 0), :]
                    out[z, rows(0, 0), :] = jnp.where(pair, 0.5 * (main_re + new_re), main_re)
                    out[z, rows(imag_at, 0), :] = jnp.where(pair, 0.5 * (main_im + new_im), main_im)
                out[z, at_re, :] = new_re
                out[z, at_im, :] = new_im
            return tuple(psi_re + psi_im)

        if upward:
            carried = (start[0, tile],) * 6 + (start[1, tile],) * 6
        else:
            carried = (jnp.zeros((8, LANES), jnp.float32),) * 12
        carried = lax.fori_loop(0, depth // unroll, block, carried)
        if not upward:
            cosine = [abs(float(c)) / 12.0 for c in quadrature()[0][:6]]
            for part_at in range(2):
                value = carried[6 * part_at] * cosine[0]
                for d in range(1, 6):
                    value = value + carried[6 * part_at + d] * cosine[d]
                value = value + pltpu.roll(value, 2, 0)
                flux[part_at, tile] = value + pltpu.roll(value, 4, 0)
    for d in range(6):
        sums[d] = jnp.sum(totals[d], axis=-1)


def sweep(plan, at, upward, *operands):
    tiles = plan.tiles + (1 if at == 0 else 0)
    out_shape = [jax.ShapeDtypeStruct((plan.depth, plan.height(at), LANES), jnp.float32)]
    if not upward:
        out_shape.append(jax.ShapeDtypeStruct((2, tiles, 8, LANES), jnp.float32))
    out_shape.append(jax.ShapeDtypeStruct((6, plan.depth, 8), jnp.float32))
    values = plan.depth * 6 * tiles * 8 * LANES
    return pl.pallas_call(
        functools.partial(sweep_kernel, plan, at, upward),
        in_specs=[pl.BlockSpec(memory_space=pltpu.VMEM)] * len(operands),
        out_specs=[pl.BlockSpec(memory_space=pltpu.VMEM)] * len(out_shape),
        out_shape=out_shape,
        scratch_shapes=[pltpu.VMEM((6, plan.depth, 8, LANES), jnp.float32)],
        compiler_params=pltpu.CompilerParams(vmem_limit_bytes=VMEM),
        cost_estimate=pl.CostEstimate(flops=values * 16, bytes_accessed=values * 4, transcendentals=0),
        name="upward" if upward else "downward",
    )(*operands)


def aims_kernel(plan, own, other, zeroth, lanes_turned, rows_turned, keep, edge, *outs):
    rows, half, chunk, tiles = plan.rows, plan.half, plan.chunk, plan.tiles
    cells = own.shape[1]
    held = outs[plan.chunks]
    row = lax.broadcasted_iota(jnp.int32, (cells * rows, half), 0) % rows
    lane = lax.broadcasted_iota(jnp.int32, (cells * rows, half), 1)
    owner = keep[...] > 0.0
    for part in range(2):
        sign = 1.0 if part == 0 else -1.0
        pairs = split(other[part].reshape(cells * rows, half))
        turned = dot(pairs[0], lanes_turned[...]) + dot(pairs[1], lanes_turned[...])
        pairs = split(turned)
        turned = dot(rows_turned[...], pairs[0]) + dot(rows_turned[...], pairs[1])
        pairs = split(zeroth[part])
        lead = dot(pairs[0], lanes_turned[...]) + dot(pairs[1], lanes_turned[...])
        lead = jnp.broadcast_to(lead[:, None, :], (cells, rows, half)).reshape(cells * rows, half)
        mirror = jnp.where(row == 0, jnp.where(owner[:1], 0.0, lead), turned)
        mirror = jnp.where(lane == 0, 0.0, mirror)
        held[...] = (own[part].reshape(cells * rows, half) + sign * mirror).reshape(cells, rows, half)
        partner = sign * jnp.where(owner[:1], lead, 0.0)
        partner = partner.reshape(cells, rows, half)
        for at in range(plan.chunks):
            for tile in range(tiles):
                for cell in range(cells):
                    pair = held[cell, pl.ds(at * chunk + tile, 2, stride=tiles), :]
                    outs[at][cell, part, tile] = jnp.concatenate([pair] * 4, axis=0)
        even = lax.broadcasted_iota(jnp.int32, (8, LANES), 0) % 2 == 0
        for cell in range(cells):
            side = jnp.broadcast_to(edge[part, cell : cell + 1], (8, LANES))
            outs[0][cell, part, tiles] = jnp.where(even, partner[cell, :8], side)


def make_aims(plan, own, other, zeroth, edge, keep, step):
    cells = 8
    rows, half = plan.rows, plan.half
    lanes_turned = np.zeros((half, half), ml_dtypes.bfloat16)
    rows_turned = np.zeros((cells * rows, cells * rows), ml_dtypes.bfloat16)
    for k in range(1, half):
        lanes_turned[half - k, k] = 1
    for c in range(cells):
        for r in range(1, rows):
            rows_turned[c * rows + r, c * rows + rows - r] = 1
    lanes_turned, rows_turned = jnp.asarray(lanes_turned), jnp.asarray(rows_turned)
    counts = [plan.tiles + (1 if at == 0 else 0) for at in range(plan.chunks)]
    return pl.pallas_call(
        functools.partial(aims_kernel, plan),
        grid=(plan.depth // cells,),
        in_specs=[
            pl.BlockSpec((None, 2, cells, rows, half), lambda z: (step, 0, z, 0, 0)),
            pl.BlockSpec((2, cells, rows, half), lambda z: (0, z, 0, 0)),
            pl.BlockSpec((2, cells, half), lambda z: (0, z, 0)),
            whole(lanes_turned),
            whole(rows_turned),
            whole(keep),
            pl.BlockSpec((2, cells, half), lambda z: (0, z, 0)),
        ],
        out_specs=[pl.BlockSpec((cells, 2, count, 8, LANES), lambda z: (z, 0, 0, 0, 0)) for count in counts],
        out_shape=[jax.ShapeDtypeStruct((plan.depth, 2, count, 8, LANES), jnp.float32) for count in counts],
        scratch_shapes=[pltpu.VMEM((cells, rows, half), jnp.float32)],
        compiler_params=pltpu.CompilerParams(vmem_limit_bytes=VMEM),
        name="targets",
    )(own, other, zeroth, lanes_turned, rows_turned, keep, edge)


def factors(plan, at, place, rate, speed):
    unit = 1.5 * 2.0 * math.pi / plan.width
    half, width = plan.half, plan.width
    base = place * plan.rows
    sub = jnp.arange(8) % 2
    row = base + at * plan.chunk + jnp.arange(plan.tiles)[:, None] + plan.tiles * sub[None, :]

    def signed(index):
        return ((index + half) % width - half).astype(jnp.float32) * unit

    freq_x = jnp.broadcast_to(signed(row)[:, :, None], (plan.tiles, 8, LANES))
    freq_y = jnp.broadcast_to(signed(jnp.arange(LANES)), (plan.tiles, 8, LANES))
    if at == 0:
        side_x = signed(base + jnp.arange(LANES))
        even = (sub == 0)[:, None]
        extra_x = jnp.where(even, -signed(base), side_x[None, :])
        extra_y = jnp.where(even, signed(jnp.arange(LANES))[None, :], signed(jnp.asarray(half)))
        freq_x = jnp.concatenate([freq_x, extra_x[None]], axis=0)
        freq_y = jnp.concatenate([freq_y, extra_y[None]], axis=0)
    cosine, along_x, along_y = [np.asarray(q, np.float32).reshape(12, 1, 1, 1) for q in quadrature()]
    wave = speed * (along_x * freq_x + along_y * freq_y)
    real = rate + np.abs(cosine) * speed
    denom = real * real + wave * wave
    return jnp.stack([real / denom, -wave / denom])


def body(phi_start, coeff, forward, rates, speeds, shares):
    shards = lax.axis_size("gx")
    groups = lax.axis_size("ba")
    place = lax.axis_index("gx")
    cells, bands, width, _ = phi_start.shape
    rows = forward.shape[3]
    plan = Plan(shards, cells, bands, width, rows)
    half, depth = plan.half, plan.depth
    consts = [jnp.asarray(part) for part in tables(width)]
    owner = place * rows == half
    keep = jnp.broadcast_to(jnp.where(owner, 1.0, 0.0).astype(jnp.float32), (8, LANES))

    def lift(value):
        return jnp.broadcast_to(jnp.repeat(value, 2)[:, None], (8, LANES))

    rate, speed, share = lift(rates), lift(speeds), lift(shares)
    polar = np.abs(np.asarray(quadrature()[0][:6], np.float32)).reshape(6, 1, 1)
    couple = polar * speed
    inverse = [factors(plan, at, place, rate, speed) for at in range(plan.chunks)]

    aims = []
    for step in range(forward.shape[0]):
        upper = forward[step, :, :, :, half:]
        other = lax.ppermute(upper, "gx", [(i, shards - 1 - i) for i in range(shards)])
        zeroth = lax.ppermute(upper[:, :, 0], "gx", [(i, (shards - i) % shards) for i in range(shards)])
        edge = jnp.pad(upper[..., 0], ((0, 0), (0, 0), (0, LANES - rows)))
        aims.append(make_aims(plan, forward, other, zeroth, edge, keep, step))

    def exchange(array):
        return lax.all_to_all(array, "gx", split_axis=0, concat_axis=0, tiled=True)

    down_sums, up_sums = [], []
    sent = first(plan, phi_start, consts)
    for step in range(forward.shape[0]):
        modes = [exchange(part).reshape((depth,) + part.shape[2:]) for part in sent]
        back = []
        for at in range(plan.chunks):
            spec = modes[at]
            inv = inverse[at]
            partial, flux, sums = sweep(plan, at, False, spec, aims[step][at], inv[:, :6], couple, rate)
            down_sums.append(sums)
            narrow = flux[:, :, :2]
            total = narrow
            for shift in range(1, groups):
                total = total + lax.ppermute(narrow, "ba", [(i, (i + shift) % groups) for i in range(groups)])
            start = share * jnp.concatenate([total] * 4, axis=2)
            new, sums = sweep(plan, at, True, spec, aims[step][at], inv[:, 6:], couple, rate, partial, start, keep)
            up_sums.append(sums)
            back.append(exchange(new.reshape(plan.shape(at))))
        if step + 1 < forward.shape[0]:
            sent = middle(plan, back, coeff, consts)
        else:
            phi = last(plan, back, coeff, consts)

    sums = jnp.stack([sum(down_sums), sum(up_sums)]).reshape(12, depth, bands, 2).sum(axis=3)
    sums = sums.transpose(1, 0, 2).reshape(shards, cells * 12 * bands) * (1.0 / width)
    grad = exchange(sums).sum(axis=0).reshape(cells, 12, bands)
    return (phi, grad)


def solution(mesh):
    in_specs = (
        P("gx", "ba", None, None),
        P("gx", None, None),
        P(None, None, None, "gx", None),
        P("ba"),
        P("ba"),
        P("ba"),
    )
    out_specs = (P("gx", "ba", None, None), P("gx", None, "ba"))
    return jax.shard_map(body, mesh=mesh, in_specs=in_specs, out_specs=out_specs, check_vma=False)
```

time: 2980 us -> 780 us (0.26); the launches traced: 2940 us -> 779 us
  other arithmetic: 1160 us -> 11.8 us
  local copies, waits for them, and re-layouts: 712 us -> 44.2 us
  waiting for transfers between devices: 564 us -> 223 us
  matrix products: 335 us -> 0 us
  Pallas kernels: 0 us -> 227 us
  blocking collectives: 110 us -> 229 us
    reduce_sum x258 -> x2, other arithmetic: 604 us -> 0.12 us  [the longest x1 0.09 us: body(): jnp.stack([sum(down_sums), sum(up_sums)]).reshape(12, depth, bands, 2)]
    all_to_all x8 -> x4, waiting for transfers between devices: 497 us -> 60.1 us  [exchange(): return lax.all_to_all(array, 'gx', split_axis=0, concat_axis=0, tiled=True)]
    while x448 -> x0, other arithmetic: 397 us -> none
    dot_general x24 -> x0, matrix products: 335 us -> none  [the longest x2 42.7 us: inverse_transform(): jnp.einsum('xk,zbky->zbxy', cos_x, col_re, precision=highest)]
    mul x352 -> x2, local copies, waits for them, and re-layouts: 243 us -> 0.5 us  [body(): sums.transpose(1, 0, 2).reshape(shards, cells * 12 * bands) * (1.0 / width)]
    all_to_all x0 -> x5, blocking collectives: none -> 229 us  [exchange(): return lax.all_to_all(array, 'gx', split_axis=0, concat_axis=0, tiled=True)]
    pallas_call x0 -> x13, Pallas kernels: none -> 227 us  [the longest x8 120 us: sweep(): pl.pallas_call(functools.partial(sweep_kernel, plan, at, upward), in_spec...]
    ppermute x0 -> x16, waiting for transfers between devices: none -> 163 us  [the longest x2 152 us: body(): lax.ppermute(upper, 'gx', [(i, shards - 1 - i) for i in range(shards)])]
  transfers between devices with their start and end apart: 10 -> 20, of which waited for: 9 -> 13; matrix products, arithmetic and copies ran while one was open for 6% -> 7% of each run, Pallas kernels for 0% -> 14%
where the time goes in v1:
time: 780 us; the launch traced here: 779 us
  blocking collectives  229 us (29%)
  Pallas kernels  227 us (29%)
  waiting for transfers between devices  223 us (29%)
  local copies, waits for them, and re-layouts  44.2 us (6%)
  starting transfers between devices  42.6 us (5%)
  other arithmetic  11.8 us (2%)
    all_to_all x5, blocking collectives, exchange(): return lax.all_to_all(array, 'gx', split_axis=0, concat_axis=0, tiled=True)  229 us
    ppermute x2, waiting for transfers between devices, body(): lax.ppermute(upper, 'gx', [(i, shards - 1 - i) for i in range(shards)])  152 us
    pallas_call x8, Pallas kernels, sweep(): pl.pallas_call(functools.partial(sweep_kernel, plan, at, upward), in_spec...  120 us
    all_to_all x4, waiting for transfers between devices, exchange(): return lax.all_to_all(array, 'gx', split_axis=0, concat_axis=0, tiled=True)  60.1 us
    pallas_call x1, Pallas kernels, middle(): pl.pallas_call(functools.partial(middle_kernel, plan), grid=(plan.cells,)...  41.1 us
    pallas_call x1, Pallas kernels, last(): pl.pallas_call(functools.partial(last_kernel, plan), grid=(plan.cells,),...  27.1 us
    pallas_call x2, Pallas kernels, make_aims(): pl.pallas_call(functools.partial(aims_kernel, plan), grid=(plan.depth //...  21.3 us
    all_to_all x4, starting transfers between devices, exchange(): return lax.all_to_all(array, 'gx', split_axis=0, concat_axis=0, tiled=True)  18.4 us
  transfers between devices with their start and end apart: 20, of which 13 were waited for; matrix products, arithmetic and copies ran while one was open for 7% of the time, Pallas kernels for 14%

profile of v1, /device:TPU:0, one launch (start us, length us, event | category | flops | bytes accessed | tf_op | source)
XLA Modules:
  0.0 778.6 jit_solution(16550022986175008939)
XLA Ops:
  0.6 17.7 %into_modes.1 = (f32[8,8,144,128]{3,2,1,0:T(8,128)}, f32[8,8,128,128]{3,2,1,0:T(8,128)}) custom-call(f32[8,4,256,256]{3,2,1,0:T(8,128)} %phi.1, bf16[256,256]{1,0:T(8,128)(2,1)} %constant.146.clone.into_h.refs_3_, bf16[256,256]{1,0:T(8,128)(2,1)} %constant.147.clone.into_l.refs_4_, bf16[512,256]{1,0:T(8,128)(2,1)} %constant.148.clone.stacked_h.refs_5_, ...), custom_call_target="tpu_custom_call" | custom-call | flops 9663676416 | bytes 33554432 | tf_op jit(solution)/shard_map/into_modes/pallas_call | solution.py:201
  18.3 54.3 %all_to_all.46 = f32[8,8,128,128]{3,2,1,0:T(8,128)} all-to-all(f32[8,8,128,128]{3,2,1,0:T(8,128)} %get-tuple-element.35), channel_id=1, replica_groups=mesh['gx'=8,'ba'=4] {'gx'}, dimensions={0} | all-to-all | bytes 8388608 | tf_op jit(solution)/shard_map/all_to_all | solution.py:450
  72.6 4.6 all-to-all-start
  77.3 5.5 fusion.21
  82.7 2.6 collective-permute-start
  85.3 8.4 %copy.52 = f32[1,2,64,32,128]{3,2,1,4,0:T(8,128)} copy(f32[1,2,64,32,128]{4,3,2,1,0:T(8,128)} %get-tuple-element.65) | data formatting | bytes 4194304
  93.7 6.6 copy.43
  102.2 0.8 slice_bitcast_fusion.1
  103.3 1.0 pad_maximum_fusion.1
  104.9 71.6 %collective-permute-done.other = f32[2,64,32,128]{3,2,1,0:T(8,128)} collective-permute-done((f32[2,64,32,128]{3,2,1,0:T(8,128)}, f32[2,64,32,128]{3,2,1,0:T(8,128)}, u32[]{:S(2)}, u32[]{:S(2)}) %collective-permute-start) | collective-permute-done | bytes 2097184 | tf_op jit(solution)/shard_map/ppermute | solution.py:444
  177.1 10.6 %targets.2 = (f32[64,2,9,8,128]{4,3,2,1,0:T(8,128)}, f32[64,2,8,8,128]{4,3,2,1,0:T(8,128)}) custom-call(f32[2,2,64,32,256]{4,3,2,1,0:T(8,128)} %own.3, f32[2,64,32,128]{3,2,1,0:T(8,128)} %collective-permute-done.other, f32[2,64,128]{2,1,0:T(8,128)} %copy-done.6, bf16[128,128]{1,0:T(8,128)(2,1)} %constant.158.clone.lanes_turned, ...), custom_call_target="tpu_custom_call" | custom-call | tf_op jit(solution)/shard_map/targets/pallas_call | solution.py:375
  188.4 13.5 %downward.5 = (f32[64,128,128]{2,1,0:T(8,128)}, f32[2,8,8,128]{3,2,1,0:T(8,128)}, f32[6,64,8]{2,1,0:T(8,128)}) custom-call(f32[64,128,128]{2,1,0:T(8,128)} %bitcast.29, f32[64,2,8,8,128]{4,3,2,1,0:T(8,128)} %get-tuple-element.36.refs_1_, f32[2,6,8,8,128]{4,3,2,1,0:T(8,128)} %get-tuple-element.68.refs_2_, f32[6,8,128]{2,1,0:T(8,128)} %broadcast_multiply_fusion.refs_3_, ...), custom_call_target="tpu_custom_call" | custom-call | flops 50331648 | bytes 12582912 | tf_op jit(solution)/shard_map/downward/pallas_call | solution.py:319
  201.9 0.8 slice.54
  202.8 2.2 collective-permute-start.5
  205.0 2.6 collective-permute-start.6
  207.6 1.3 collective-permute-start.7
  209.6 1.7 collective-permute-done.7
  211.3 0.9 add_add_fusion.3
  212.2 0.7 maximum_multiply_fusion.2.refs_6_
  212.9 14.6 %upward.5 = (f32[64,128,128]{2,1,0:T(8,128)}, f32[6,64,8]{2,1,0:T(8,128)}) custom-call(f32[64,128,128]{2,1,0:T(8,128)} %bitcast.30, f32[64,2,8,8,128]{4,3,2,1,0:T(8,128)} %get-tuple-element.36.refs_1_, f32[2,6,8,8,128]{4,3,2,1,0:T(8,128)} %get-tuple-element.69.refs_2_, f32[6,8,128]{2,1,0:T(8,128)} %broadcast_multiply_fusion.refs_3_, ...), custom_call_target="tpu_custom_call" | custom-call | flops 50331648 | bytes 12582912 | tf_op jit(solution)/shard_map/upward/pallas_call | solution.py:319
  227.5 4.6 all-to-all-start.3
  232.5 1.0 pad_maximum_fusion
  233.5 15.0 %downward.4 = (f32[64,144,128]{2,1,0:T(8,128)}, f32[2,9,8,128]{3,2,1,0:T(8,128)}, f32[6,64,8]{2,1,0:T(8,128)}) custom-call(f32[64,144,128]{2,1,0:T(8,128)} %bitcast.refs_0_, f32[64,2,9,8,128]{4,3,2,1,0:T(8,128)} %get-tuple-element.31.refs_1_, f32[2,6,9,8,128]{4,3,2,1,0:T(8,128)} %get-tuple-element.66.refs_2_, f32[6,8,128]{2,1,0:T(8,128)} %broadcast_multiply_fusion.refs_3_, ...), custom_call_target="tpu_custom_call" | custom-call | flops 56623104 | bytes 14155776 | tf_op jit(solution)/shard_map/downward/pallas_call | solution.py:319
  248.6 0.9 slice.51
  249.5 3.6 collective-permute-start.3
  253.3 1.7 collective-permute-done.2
  255.3 1.6 collective-permute-done.4
  256.9 0.9 add_add_fusion.1
  257.8 0.7 maximum_multiply_fusion.refs_6_
  258.5 16.4 %upward.4 = (f32[64,144,128]{2,1,0:T(8,128)}, f32[6,64,8]{2,1,0:T(8,128)}) custom-call(f32[64,144,128]{2,1,0:T(8,128)} %bitcast.refs_0_, f32[64,2,9,8,128]{4,3,2,1,0:T(8,128)} %get-tuple-element.31.refs_1_, f32[2,6,9,8,128]{4,3,2,1,0:T(8,128)} %get-tuple-element.67.refs_2_, f32[6,8,128]{2,1,0:T(8,128)} %broadcast_multiply_fusion.refs_3_, ...), custom_call_target="tpu_custom_call" | custom-call | flops 56623104 | bytes 14155776 | tf_op jit(solution)/shard_map/upward/pallas_call | solution.py:319
  275.0 6.3 all-to-all-done.3.refs_1_
  281.2 59.2 %all_to_all.47.refs_0_ = f32[8,8,144,128]{3,2,1,0:T(8,128)} all-to-all(f32[8,8,144,128]{3,2,1,0:T(8,128)} %bitcast.38), channel_id=1, replica_groups=mesh['gx'=8,'ba'=4] {'gx'}, dimensions={0} | all-to-all | bytes 9437184 | tf_op jit(solution)/shard_map/all_to_all | solution.py:450
  340.4 41.1 %between_steps.1 = (f32[8,8,144,128]{3,2,1,0:T(8,128)}, f32[8,8,128,128]{3,2,1,0:T(8,128)}) custom-call(f32[8,8,144,128]{3,2,1,0:T(8,128)} %all_to_all.47.refs_0_, f32[8,8,128,128]{3,2,1,0:T(8,128)} %all-to-all-done.3.refs_1_, f32[8,256,256]{2,1,0:T(8,128)} %refs_2_.3, bf16[256,256]{1,0:T(8,128)(2,1)} %constant.146.clone.into_h.refs_3_, ...), custom_call_target="tpu_custom_call" | custom-call | flops 19327352832 | bytes 33554432 | tf_op jit(solution)/shard_map/between_steps/pallas_call | solution.py:214
  381.6 53.6 %all_to_all.48 = f32[8,8,128,128]{3,2,1,0:T(8,128)} all-to-all(f32[8,8,128,128]{3,2,1,0:T(8,128)} %get-tuple-element.45), channel_id=1, replica_groups=mesh['gx'=8,'ba'=4] {'gx'}, dimensions={0} | all-to-all | bytes 8388608 | tf_op jit(solution)/shard_map/all_to_all | solution.py:450
  435.1 4.6 all-to-all-start.4
  439.8 2.6 collective-permute-start.8
  442.4 7.5 copy.53
  449.8 6.6 copy.46
  457.1 0.8 slice_bitcast_fusion
  458.5 80.5 %collective-permute-done.8.other = f32[2,64,32,128]{3,2,1,0:T(8,128)} collective-permute-done((f32[2,64,32,128]{3,2,1,0:T(8,128)}, f32[2,64,32,128]{3,2,1,0:T(8,128)}, u32[]{:S(2)}, u32[]{:S(2)}) %collective-permute-start.8) | collective-permute-done | bytes 2097184 | tf_op jit(solution)/shard_map/ppermute | solution.py:444
  539.0 10.6 %targets.3 = (f32[64,2,9,8,128]{4,3,2,1,0:T(8,128)}, f32[64,2,8,8,128]{4,3,2,1,0:T(8,128)}) custom-call(f32[2,2,64,32,256]{4,3,2,1,0:T(8,128)} %own.3, f32[2,64,32,128]{3,2,1,0:T(8,128)} %collective-permute-done.8.other, f32[2,64,128]{2,1,0:T(8,128)} %copy-done.7, bf16[128,128]{1,0:T(8,128)(2,1)} %constant.158.clone.lanes_turned, ...), custom_call_target="tpu_custom_call" | custom-call | tf_op jit(solution)/shard_map/targets/pallas_call | solution.py:375
  549.6 13.6 %downward.7 = (f32[64,128,128]{2,1,0:T(8,128)}, f32[2,8,8,128]{3,2,1,0:T(8,128)}, f32[6,64,8]{2,1,0:T(8,128)}) custom-call(f32[64,128,128]{2,1,0:T(8,128)} %bitcast.31, f32[64,2,8,8,128]{4,3,2,1,0:T(8,128)} %get-tuple-element.46.refs_1_, f32[2,6,8,8,128]{4,3,2,1,0:T(8,128)} %get-tuple-element.68.refs_2_, f32[6,8,128]{2,1,0:T(8,128)} %broadcast_multiply_fusion.refs_3_, ...), custom_call_target="tpu_custom_call" | custom-call | flops 50331648 | bytes 12582912 | tf_op jit(solution)/shard_map/downward/pallas_call | solution.py:319
  563.2 0.8 slice.59
  564.2 3.6 collective-permute-start.14
  567.9 1.8 collective-permute-done.13
  569.7 2.0 collective-permute-done.15
  571.7 0.9 add_add_fusion.2
  573.2 14.7 %upward.7 = (f32[64,128,128]{2,1,0:T(8,128)}, f32[6,64,8]{2,1,0:T(8,128)}) custom-call(f32[64,128,128]{2,1,0:T(8,128)} %bitcast.32, f32[64,2,8,8,128]{4,3,2,1,0:T(8,128)} %get-tuple-element.46.refs_1_, f32[2,6,8,8,128]{4,3,2,1,0:T(8,128)} %get-tuple-element.69.refs_2_, f32[6,8,128]{2,1,0:T(8,128)} %broadcast_multiply_fusion.refs_3_, ...), custom_call_target="tpu_custom_call" | custom-call | flops 50331648 | bytes 12582912 | tf_op jit(solution)/shard_map/upward/pallas_call | solution.py:319
  587.9 15.1 %downward.6 = (f32[64,144,128]{2,1,0:T(8,128)}, f32[2,9,8,128]{3,2,1,0:T(8,128)}, f32[6,64,8]{2,1,0:T(8,128)}) custom-call(f32[64,144,128]{2,1,0:T(8,128)} %bitcast.7.refs_0_, f32[64,2,9,8,128]{4,3,2,1,0:T(8,128)} %get-tuple-element.41.refs_1_, f32[2,6,9,8,128]{4,3,2,1,0:T(8,128)} %get-tuple-element.66.refs_2_, f32[6,8,128]{2,1,0:T(8,128)} %broadcast_multiply_fusion.refs_3_, ...), custom_call_target="tpu_custom_call" | custom-call | flops 56623104 | bytes 14155776 | tf_op jit(solution)/shard_map/downward/pallas_call | solution.py:319
  603.1 0.9 slice.58
  604.6 1.8 collective-permute-start.11
  606.5 1.3 collective-permute-start.12
  607.8 1.0 add_bitcast_fusion.1
  609.5 0.7 collective-permute-done.12
  610.2 0.9 add_add_fusion
  611.1 0.7 maximum_multiply_fusion.1.refs_6_
  611.8 16.5 %upward.6 = (f32[64,144,128]{2,1,0:T(8,128)}, f32[6,64,8]{2,1,0:T(8,128)}) custom-call(f32[64,144,128]{2,1,0:T(8,128)} %bitcast.7.refs_0_, f32[64,2,9,8,128]{4,3,2,1,0:T(8,128)} %get-tuple-element.41.refs_1_, f32[2,6,9,8,128]{4,3,2,1,0:T(8,128)} %get-tuple-element.67.refs_2_, f32[6,8,128]{2,1,0:T(8,128)} %broadcast_multiply_fusion.refs_3_, ...), custom_call_target="tpu_custom_call" | custom-call | flops 56623104 | bytes 14155776 | tf_op jit(solution)/shard_map/upward/pallas_call | solution.py:319
  628.3 1.0 add_bitcast_fusion
  630.0 8.6 %all_to_all.49 = f32[8,1,384]{2,1,0:T(1,128)S(1)} all-to-all(f32[8,1,384]{2,1,0:T(1,128)S(1)} %mul.337), channel_id=1, replica_groups=mesh['gx'=8,'ba'=4] {'gx'}, dimensions={0} | all-to-all | bytes 24576 | tf_op jit(solution)/shard_map/all_to_all | solution.py:450
  638.6 53.5 %all_to_all.50.refs_1_ = f32[8,8,128,128]{3,2,1,0:T(8,128)} all-to-all(f32[8,8,128,128]{3,2,1,0:T(8,128)} %bitcast.40), channel_id=1, replica_groups=mesh['gx'=8,'ba'=4] {'gx'}, dimensions={0} | all-to-all | bytes 8388608 | tf_op jit(solution)/shard_map/all_to_all | solution.py:450
  692.2 4.6 all-to-all-start.5
  696.9 0.7 copy.51
  697.6 53.9 %all-to-all-done.5.refs_0_ = f32[8,8,144,128]{3,2,1,0:T(8,128)} async-done(((f32[8,8,144,128]{3,2,1,0:T(8,128)}), f32[8,8,144,128]{3,2,1,0:T(8,128)}, u32[]{:S(2)}, u32[]{:S(2)}) %all-to-all-start.5) | async-done | bytes 4718624 | tf_op jit(solution)/shard_map/all_to_all | solution.py:450
  751.5 27.1 %out_of_modes.1 = f32[8,4,256,256]{3,2,1,0:T(8,128)} custom-call(f32[8,8,144,128]{3,2,1,0:T(8,128)} %all-to-all-done.5.refs_0_, f32[8,8,128,128]{3,2,1,0:T(8,128)} %all_to_all.50.refs_1_, f32[8,256,256]{2,1,0:T(8,128)} %refs_2_.3, bf16[256,512]{1,0:T(8,128)(2,1)} %constant.150.clone.refs_7_.refs_3_, bf16[256,512]{1,0:T(8,128)(2,1)} %constant.151.clone.refs_8_.refs_4_, ...), custom_call_target="tpu_custom_call" | custom-call | flops 9663676416 | bytes 33554432 | tf_op jit(solution)/shard_map/out_of_modes/pallas_call | solution.py:228
  (82 shorter events, 10.0 us)
Async XLA Ops:
  72.6 154.9 %all-to-all-start = ((f32[8,8,144,128]{3,2,1,0:T(8,128)}), f32[8,8,144,128]{3,2,1,0:T(8,128)}, u32[]{:S(2)}, u32[]{:S(2)}) async-start(f32[8,8,144,128]{3,2,1,0:T(8,128)} %get-tuple-element.30), calls=%async_computation | async-start | bytes 9437184 | tf_op jit(solution)/shard_map/all_to_all | solution.py:450
  82.7 93.7 %collective-permute-start = (f32[2,64,32,128]{3,2,1,0:T(8,128)}, f32[2,64,32,128]{3,2,1,0:T(8,128)}, u32[]{:S(2)}, u32[]{:S(2)}) collective-permute-start(f32[2,64,32,128]{3,2,1,0:T(8,128)} %get-tuple-element.63), channel_id=1, source_target_pairs={{0,28},{4,24},{8,20},{12,16},{16,12},{20,8},{24,4},{28,0},{1,29},{... | collective-permute-start | bytes 6291464 | tf_op jit(solution)/shard_map/ppermute | solution.py:444
  93.7 7.3 copy-start.11
  93.7 7.5 copy-start.12
  93.7 7.8 copy-start.14
  93.7 8.5 %copy-start.10 = (f32[12]{0:T(128)S(1)}, f32[12]{0:T(128)}, u32[]{:S(2)}) copy-start(f32[12]{0:T(128)} %constant.164) | copy-start | bytes 148
  93.7 9.4 %copy-start.8 = (f32[12]{0:T(128)S(1)}, f32[12]{0:T(128)}, u32[]{:S(2)}) copy-start(f32[12]{0:T(128)} %constant.165) | copy-start | bytes 148
  93.7 9.4 %copy-start.9 = (f32[12]{0:T(128)S(1)}, f32[12]{0:T(128)}, u32[]{:S(2)}) copy-start(f32[12]{0:T(128)} %constant.166) | copy-start | bytes 148
  100.3 4.6 collective-permute-start.1
  104.9 72.2 %copy-start.6 = (f32[2,64,128]{2,1,0:T(8,128)}, f32[2,64,128]{2,1,0:T(8,128)S(1)}, u32[]{:S(2)}) copy-start(f32[2,64,128]{2,1,0:T(8,128)S(1)} %collective-permute-done.1.zeroth) | copy-start | bytes 196612
  188.4 20.6 %copy-start.13 = (f32[4]{0:T(128)S(1)}, f32[4]{0:T(128)}, u32[]{:S(2)}) copy-start(f32[4]{0:T(128)} %param.30) | copy-start | bytes 52
  202.8 6.3 collective-permute-start.5
  205.0 4.6 collective-permute-start.6
  207.6 3.7 collective-permute-start.7
  227.5 53.7 %all-to-all-start.3 = ((f32[8,8,128,128]{3,2,1,0:T(8,128)}), f32[8,8,128,128]{3,2,1,0:T(8,128)}, u32[]{:S(2)}, u32[]{:S(2)}) async-start(f32[8,8,128,128]{3,2,1,0:T(8,128)} %bitcast.39), calls=%async_computation.3 | async-start | bytes 8388608 | tf_op jit(solution)/shard_map/all_to_all | solution.py:450
  249.5 5.6 collective-permute-start.2
  249.5 5.8 collective-permute-start.3
  253.2 3.8 collective-permute-start.4
  435.1 152.8 %all-to-all-start.4 = ((f32[8,8,144,128]{3,2,1,0:T(8,128)}), f32[8,8,144,128]{3,2,1,0:T(8,128)}, u32[]{:S(2)}, u32[]{:S(2)}) async-start(f32[8,8,144,128]{3,2,1,0:T(8,128)} %get-tuple-element.40), calls=%async_computation.4 | async-start | bytes 9437184 | tf_op jit(solution)/shard_map/all_to_all | solution.py:450
  439.8 99.2 %collective-permute-start.8 = (f32[2,64,32,128]{3,2,1,0:T(8,128)}, f32[2,64,32,128]{3,2,1,0:T(8,128)}, u32[]{:S(2)}, u32[]{:S(2)}) collective-permute-start(f32[2,64,32,128]{3,2,1,0:T(8,128)} %get-tuple-element.64), channel_id=1, source_target_pairs={{0,28},{4,24},{8,20},{12,16},{16,12},{20,8},{24,4},{28,0},{1,29},{... | collective-permute-start | bytes 6291464 | tf_op jit(solution)/shard_map/ppermute | solution.py:444
  456.4 2.1 collective-permute-start.9
  458.5 80.5 %copy-start.7 = (f32[2,64,128]{2,1,0:T(8,128)}, f32[2,64,128]{2,1,0:T(8,128)S(1)}, u32[]{:S(2)}) copy-start(f32[2,64,128]{2,1,0:T(8,128)S(1)} %collective-permute-done.9.zeroth) | copy-start | bytes 196612
  564.1 5.6 collective-permute-start.13
  564.2 5.5 collective-permute-start.14
  567.8 3.9 collective-permute-start.15
  587.9 19.9 %copy-start.1 = (f32[6,64,8]{2,1,0:T(8,128)S(1)}, f32[6,64,8]{2,1,0:T(8,128)}, u32[]{:S(2)}) copy-start(f32[6,64,8]{2,1,0:T(8,128)} %get-tuple-element.51) | copy-start | bytes 36868
  587.9 19.9 %copy-start.3 = (f32[6,64,8]{2,1,0:T(8,128)S(1)}, f32[6,64,8]{2,1,0:T(8,128)}, u32[]{:S(2)}) copy-start(f32[6,64,8]{2,1,0:T(8,128)} %get-tuple-element.50) | copy-start | bytes 36868
  587.9 19.9 %copy-start.5 = (f32[6,64,8]{2,1,0:T(8,128)S(1)}, f32[6,64,8]{2,1,0:T(8,128)}, u32[]{:S(2)}) copy-start(f32[6,64,8]{2,1,0:T(8,128)} %get-tuple-element.53) | copy-start | bytes 36868
  604.0 5.6 collective-permute-start.10
  604.6 4.9 collective-permute-start.11
  606.5 3.8 collective-permute-start.12
  611.8 16.5 %copy-start = (f32[6,64,8]{2,1,0:T(8,128)S(1)}, f32[6,64,8]{2,1,0:T(8,128)}, u32[]{:S(2)}) copy-start(f32[6,64,8]{2,1,0:T(8,128)} %get-tuple-element.55) | copy-start | bytes 36868
  611.8 16.5 %copy-start.2 = (f32[6,64,8]{2,1,0:T(8,128)S(1)}, f32[6,64,8]{2,1,0:T(8,128)}, u32[]{:S(2)}) copy-start(f32[6,64,8]{2,1,0:T(8,128)} %get-tuple-element.54) | copy-start | bytes 36868
  611.8 16.5 %copy-start.4 = (f32[6,64,8]{2,1,0:T(8,128)S(1)}, f32[6,64,8]{2,1,0:T(8,128)}, u32[]{:S(2)}) copy-start(f32[6,64,8]{2,1,0:T(8,128)} %get-tuple-element.57) | copy-start | bytes 36868
  692.2 59.4 %all-to-all-start.5 = ((f32[8,8,144,128]{3,2,1,0:T(8,128)}), f32[8,8,144,128]{3,2,1,0:T(8,128)}, u32[]{:S(2)}, u32[]{:S(2)}) async-start(f32[8,8,144,128]{3,2,1,0:T(8,128)} %bitcast.37), calls=%async_computation.5 | async-start | bytes 9437184 | tf_op jit(solution)/shard_map/all_to_all | solution.py:450

commit v2 on v1

v2 whole, which is shorter than its diff:
```python
import functools
import math

import jax
import jax.numpy as jnp
import ml_dtypes
import numpy as np
from jax import lax
from jax.experimental import pallas as pl
from jax.experimental.pallas import tpu as pltpu
from jax.sharding import PartitionSpec as P

LANES = 128
VMEM = 56 * 1024 * 1024
CHUNK_ROWS = 16


def split_host(table):
    high = table.astype(ml_dtypes.bfloat16)
    low = (table - high.astype(np.float64)).astype(ml_dtypes.bfloat16)
    return high, low


def tables(count):
    half = count // 2
    index = np.arange(count)
    angle = (np.outer(index, index) % count) * (2.0 * np.pi / count)
    cos, sin = np.cos(angle) / math.sqrt(count), np.sin(angle) / math.sqrt(count)
    alternate = np.where(index % 2 == 0, 1.0, -1.0) / math.sqrt(count)
    into = np.concatenate([cos[:, :half], alternate[:, None], -sin[:, 1:half]], axis=1)
    weight = np.where(np.arange(half) == 0, 1.0, 2.0)[:, None]
    back = np.concatenate([weight * cos[:half], alternate[None], -2.0 * sin[1:half]], axis=0) / 12.0
    stacked = np.concatenate([cos, sin], axis=0)
    beside = np.concatenate([cos, sin], axis=1)
    return [part for table in (into, stacked, beside, back) for part in split_host(table)]


def quadrature():
    level = np.arange(6)
    polar = 0.2 + 0.15 * level
    cosine = np.concatenate([-polar, polar])
    azimuth = np.concatenate([level * (np.pi / 3.0) + np.pi / 6.0, level * (np.pi / 3.0)])
    sine = np.sqrt(1.0 - cosine * cosine)
    return (cosine, sine * np.cos(azimuth), sine * np.sin(azimuth))


def split(value):
    high = value.astype(jnp.bfloat16)
    low = (value - high.astype(jnp.float32)).astype(jnp.bfloat16)
    return high, low


def dot(left, right):
    return jnp.dot(left, right, preferred_element_type=jnp.float32)


def dot3(left, right):
    return dot(left[0], right[0]) + (dot(left[0], right[1]) + dot(left[1], right[0]))


class Plan:
    def __init__(self, shards, cells, width, rows):
        self.shards, self.cells, self.width, self.rows = shards, cells, width, rows
        self.half = width // 2
        self.chunk = min(CHUNK_ROWS, rows)
        self.chunks = rows // self.chunk
        self.tiles = self.chunk // 4
        self.main = 4 * self.chunk
        self.depth = shards * cells
        self.edge = cells * self.main
        self.pad = (cells + 7) // 8 * 8

    def height(self, chunk):
        return self.edge + (self.pad if chunk == 0 else 0)

    def shapes(self, chunk, sides):
        return [jax.ShapeDtypeStruct((self.shards, 2 // sides * self.height(chunk), LANES), jnp.float32)] * sides

    def sides_sent(self, chunk):
        return 2 if chunk == 0 else 1

    def sides_back(self, chunk):
        return 2 if chunk == self.chunks - 1 else 1

    def steps(self, chunk):
        return self.tiles + (1 if chunk == 0 else 0)


class View:
    def __init__(self, ref, offset=0):
        self.ref, self.offset = ref, offset

    def moved(self, rows):
        return pl.ds(self.offset + rows.start, rows.size, stride=rows.stride)

    def at(self, shard, rows):
        return self.ref[shard, self.moved(rows), :]

    def put(self, shard, rows, value):
        self.ref[shard, self.moved(rows), :] = value


def views(plan, at, refs):
    if len(refs) == 2:
        return [View(ref) for ref in refs]
    return [View(refs[0], side * plan.height(at)) for side in range(2)]


def forward_slabs(plan, cell, phis, into, stacked, outs):
    width, half, rows, chunk = plan.width, plan.half, plan.rows, plan.chunk
    lane = lax.broadcasted_iota(jnp.int32, (width, half), 1)
    first = lane == 0
    columns = jnp.zeros((width, half), jnp.float32)
    for band in range(2):
        packed = dot3(split(phis(band)), into)
        both = dot3(stacked, split(packed))
        cos_re, cos_im = both[:width, :half], both[:width, half:]
        sin_re, sin_im = both[width:, :half], both[width:, half:]
        real = cos_re + jnp.where(first, 0.0, sin_im)
        imag = jnp.where(first, 0.0, cos_im) - sin_re
        for at in range(plan.chunks):
            base = pl.multiple_of(cell * plan.main, 8) if at == 0 else 0
            for shard in range(plan.shards):
                start = shard * rows + at * chunk
                outs[at][shard, pl.ds(base + band * chunk, chunk), :] = real[start : start + chunk]
                outs[at][shard, pl.ds(base + (2 + band) * chunk, chunk), :] = imag[start : start + chunk]
        columns = jnp.where(lane == band, pltpu.roll(cos_im, band, 1) if band else cos_im, columns)
        columns = jnp.where(lane == band + 2, -pltpu.roll(sin_im, band + 2, 1), columns)
    turned = columns.T[:8]
    slot = lax.broadcasted_iota(jnp.int32, (1, LANES), 1)
    for shard in range(plan.shards):
        start = shard * rows
        piece = turned[:, start // LANES * LANES : start // LANES * LANES + LANES]
        row = jnp.zeros((1, LANES), jnp.float32)
        for group in range(4):
            shift = (group * rows - start) % LANES
            held = pltpu.roll(piece, shift, 1) if shift else piece
            row = jnp.where((slot >= group * rows) & (slot < (group + 1) * rows), held[group : group + 1], row)
        outs[0][shard, pl.ds(plan.edge + cell, 1), :] = row


def inverse_slabs(plan, cell, ins, beside, back, take):
    width, half, rows, chunk = plan.width, plan.half, plan.rows, plan.chunk
    lines = [ins[0][shard, pl.ds(plan.edge + cell, 1), :] for shard in range(plan.shards)]
    lines.append(jnp.zeros((LANES - plan.shards, LANES), jnp.float32))
    turned = jnp.concatenate(lines, axis=0).T[: 4 * rows]
    shifted = [pltpu.roll(turned, LANES - shard, 1) if shard else turned for shard in range(plan.shards)]
    sides = [jnp.concatenate([held[g * rows : (g + 1) * rows] for held in shifted], axis=0) for g in range(4)]
    first = lax.broadcasted_iota(jnp.int32, (width, half), 1) == 0
    for band in range(2):
        reals, imags = [], []
        for shard in range(plan.shards):
            for at in range(plan.chunks):
                base = pl.multiple_of(cell * plan.main, 8) if at == 0 else 0
                reals.append(ins[at][shard, pl.ds(base + band * chunk, chunk), :])
                imags.append(ins[at][shard, pl.ds(base + (2 + band) * chunk, chunk), :])
        real, imag = jnp.concatenate(reals, axis=0), jnp.concatenate(imags, axis=0)
        upper = jnp.concatenate([real, jnp.where(first, sides[band], imag)], axis=1)
        lower = jnp.concatenate([-imag, jnp.where(first, -sides[band + 2], real)], axis=1)
        mixed = dot3(beside, split(jnp.concatenate([upper, lower], axis=0)))
        take(band, dot3(split(mixed), back))


def first_kernel(plan, kept, phi, into_h, into_l, stacked_h, stacked_l, *refs):
    cell = pl.program_id(0)
    outs = refs[kept:]
    into, stacked = (into_h[...], into_l[...]), (stacked_h[...], stacked_l[...])
    forward_slabs(plan, cell, lambda band: phi[0, band], into, stacked, outs)


def middle_kernel(plan, kept, *refs):
    cell = pl.program_id(0)
    ins = refs[: plan.chunks]
    coeff = refs[plan.chunks]
    into_h, into_l, stacked_h, stacked_l, beside_h, beside_l, back_h, back_l = refs[plan.chunks + 1 : plan.chunks + 9]
    outs, held = refs[plan.chunks + 9 + kept : -1], refs[-1]

    def take(band, value):
        held[band] = value * coeff[0]

    inverse_slabs(plan, cell, ins, (beside_h[...], beside_l[...]), (back_h[...], back_l[...]), take)
    into, stacked = (into_h[...], into_l[...]), (stacked_h[...], stacked_l[...])
    forward_slabs(plan, cell, lambda band: held[band], into, stacked, outs)


def last_kernel(plan, *refs):
    ins = refs[: plan.chunks]
    coeff, beside_h, beside_l, back_h, back_l = refs[plan.chunks : plan.chunks + 5]
    out = refs[-1]

    def take(band, value):
        out[0, band] = value * coeff[0]

    inverse_slabs(plan, pl.program_id(0), ins, (beside_h[...], beside_l[...]), (back_h[...], back_l[...]), take)


def whole(array):
    rank = len(array.shape)
    return pl.BlockSpec(array.shape, lambda cell: (0,) * rank)


def piece_specs(plan, side, sides):
    specs = []
    for at in range(plan.chunks):
        merged = sides(at) == 1
        if at == 0:
            shape = (plan.shards, plan.height(0), LANES)
            specs.append(pl.BlockSpec(shape, lambda cell, first=side if merged else 0: (0, first, 0)))
        else:
            shape = (plan.shards, plan.main, LANES)
            specs.append(pl.BlockSpec(shape, lambda cell, first=side * plan.cells if merged else 0: (0, first + cell, 0)))
    return specs


def sent_shapes(plan):
    return [plan.shapes(at, plan.sides_sent(at))[0] for at in range(plan.chunks)]


def slab_spec(plan, side):
    return pl.BlockSpec((1, 2, plan.width, plan.width), lambda cell: (cell, side, 0, 0))


def coeff_spec(plan):
    return pl.BlockSpec((1, plan.width, plan.width), lambda cell: (cell, 0, 0))


def cost(microseconds):
    return pl.CostEstimate(flops=0, bytes_accessed=int(microseconds * 3.69e6), transcendentals=0)


PARAMS = pltpu.CompilerParams(vmem_limit_bytes=VMEM)


def send(kernel, plan, side, operands, in_specs, held, microseconds, scratch, name):
    aliases = {}
    for at in range(plan.chunks):
        if held is not None and plan.sides_sent(at) == 1:
            aliases[len(operands)] = at
            operands, in_specs = operands + [held[at]], in_specs + [pl.BlockSpec(memory_space=pl.ANY)]
    return pl.pallas_call(
        functools.partial(kernel, plan, len(aliases)),
        grid=(plan.cells,),
        in_specs=in_specs,
        out_specs=piece_specs(plan, side, plan.sides_sent),
        out_shape=sent_shapes(plan),
        input_output_aliases=aliases,
        scratch_shapes=scratch,
        compiler_params=PARAMS,
        cost_estimate=cost(microseconds),
        name=name,
    )(*operands)


def first(plan, side, phi, consts, held):
    in_specs = [slab_spec(plan, side)] + [whole(c) for c in consts[:4]]
    return send(first_kernel, plan, side, [phi, *consts[:4]], in_specs, held, 12, [], "into_modes")


def middle(plan, side, ins, coeff, consts, held):
    in_specs = piece_specs(plan, side, plan.sides_back) + [coeff_spec(plan)] + [whole(c) for c in consts]
    scratch = [pltpu.VMEM((2, plan.width, plan.width), jnp.float32)]
    return send(middle_kernel, plan, side, [*ins, coeff, *consts], in_specs, held, 25, scratch, "between_steps")


def last(plan, side, ins, coeff, consts, held):
    operands = [*ins, coeff, *consts[4:]]
    in_specs = piece_specs(plan, side, plan.sides_back) + [coeff_spec(plan)] + [whole(c) for c in consts[4:]]
    aliases = {}
    if held is not None:
        aliases = {len(operands): 0}
        operands.append(held)
        in_specs.append(pl.BlockSpec(memory_space=pl.ANY))
    return pl.pallas_call(
        functools.partial(last_kernel, plan),
        grid=(plan.cells,),
        in_specs=in_specs,
        out_specs=slab_spec(plan, side),
        out_shape=jax.ShapeDtypeStruct((plan.cells, 4, plan.width, plan.width), jnp.float32),
        input_output_aliases=aliases,
        compiler_params=PARAMS,
        cost_estimate=cost(16),
        name="out_of_modes",
    )(*operands)


def sweep_kernel(plan, at, upward, groups, *refs):
    refs = list(refs)

    def pop(count):
        taken = refs[:count]
        del refs[:count]
        return taken

    specs = views(plan, at, pop(plan.sides_sent(at)))
    aims, inv, couple, rate = pop(4)
    if upward:
        parts = views(plan, at, pop(2))
        extras = pop(1)[0] if at == 0 else None
        share, keep = pop(2)
        fluxes = pop(groups)
        outs = views(plan, at, pop(plan.sides_back(at)))
        sums, totals = refs
    else:
        outs = views(plan, at, pop(2))
        flux, sums = pop(2)
        extras = pop(1)[0] if at == 0 else None
        totals = refs[0]
    tiles, depth, cells, main, rows = plan.tiles, plan.depth, plan.cells, plan.main, plan.rows
    imag_at = 2 * plan.chunk
    sub = lax.broadcasted_iota(jnp.int32, (8, LANES), 0)
    lane = lax.broadcasted_iota(jnp.int32, (1, LANES), 1)
    zeros = jnp.zeros((8, LANES), jnp.float32)
    cosine = [abs(float(c)) / 12.0 for c in quadrature()[0][:6]]

    def place(cell, base, tile):
        return pl.ds(cell * main + base + tile, 8, stride=tiles)

    def extra_source(shard, cell, base):
        edge = []
        for s in range(2):
            line = specs[s].at(shard, pl.ds(plan.edge + cell, 1))
            line = pltpu.roll(line, LANES - 2 * rows, 1) if base else line
            edge.append(jnp.where(sub < 4, line, pltpu.roll(line, LANES - rows, 1)))
        row0 = [specs[s].at(shard, place(cell, base, 0)) for s in range(2)]
        kind = sub % 4
        value = jnp.where(kind == 0, row0[0], jnp.where(kind == 1, pltpu.roll(row0[1], 1, 0), 0.0))
        return jnp.where(kind == 2, edge[0], jnp.where(kind == 3, edge[1], value))

    def extra_store(shard, cell, new_re, new_im):
        if not upward:
            extras[shard * cells + cell, 0] = new_re
            extras[shard * cells + cell, 1] = new_im
            return
        new_re = new_re + extras[shard * cells + cell, 0]
        new_im = new_im + extras[shard * cells + cell, 1]
        spread = [new_re, pltpu.roll(new_re, rows, 1), pltpu.roll(new_im, 2 * rows, 1), pltpu.roll(new_im, 3 * rows, 1)]
        for side in range(2):
            row = spread[0][2 + side : 3 + side]
            for group in range(1, 4):
                at_sub = 2 + side + 4 * (group % 2)
                row = jnp.where(lane < group * rows, row, spread[group][at_sub : at_sub + 1])
            outs[side].put(shard, pl.ds(plan.edge + cell, 1), row)
            for base, value in ((0, new_re), (imag_at, new_im)):
                value = pltpu.roll(value, 7, 0) if side else value
                held = outs[side].at(shard, place(cell, base, 0))
                pair = (sub % 4 == 0) & (keep[...] > 0.0)
                outs[side].put(shard, place(cell, base, 0), jnp.where(pair, 0.5 * (held + value), held))

    for count in range(2 * tiles + (1 if at == 0 else 0)):
        extra = count == 2 * tiles
        side, tile = (2, tiles) if extra else (count // tiles, count % tiles)
        inv_re = [inv[0, d, count] for d in range(6)]
        inv_im = [inv[1, d, count] for d in range(6)]
        fresh = extra or tile == 0

        def block(step, psi, extra=extra, side=side, tile=tile, inv_re=inv_re, inv_im=inv_im, fresh=fresh):
            psi_re, psi_im = list(psi[:6]), list(psi[6:])
            shard = step if upward else plan.shards - 1 - step
            for cell in range(cells) if upward else range(cells - 1, -1, -1):
                z = shard * cells + cell
                if extra:
                    row_re, row_im = extra_source(shard, cell, 0), extra_source(shard, cell, imag_at)
                else:
                    row_re = specs[side].at(shard, place(cell, 0, tile))
                    row_im = specs[side].at(shard, place(cell, imag_at, tile))
                row_re, row_im = rate[side] * row_re, rate[side] * row_im
                aim_re, aim_im = aims[z, 0, tile], aims[z, 1, tile]
                for d in range(6):
                    sum_re = row_re + couple[side, d] * psi_re[d]
                    sum_im = row_im + couple[side, d] * psi_im[d]
                    psi_re[d] = inv_re[d] * sum_re - inv_im[d] * sum_im
                    psi_im[d] = inv_re[d] * sum_im + inv_im[d] * sum_re
                    product = psi_re[d] * aim_re + psi_im[d] * aim_im
                    totals[side, d, z] = product if fresh else totals[side, d, z] + product
                new_re = ((psi_re[0] + psi_re[1]) + (psi_re[2] + psi_re[3])) + (psi_re[4] + psi_re[5])
                new_im = ((psi_im[0] + psi_im[1]) + (psi_im[2] + psi_im[3])) + (psi_im[4] + psi_im[5])
                if extra:
                    extra_store(shard, cell, new_re, new_im)
                    continue
                if upward:
                    new_re = new_re + parts[side].at(shard, place(cell, 0, tile))
                    new_im = new_im + parts[side].at(shard, place(cell, imag_at, tile))
                outs[side].put(shard, place(cell, 0, tile), new_re)
                outs[side].put(shard, place(cell, imag_at, tile), new_im)
            return tuple(psi_re + psi_im)

        if upward:
            start = []
            for part in range(2):
                value = fluxes[0][part, tile]
                for other in fluxes[1:]:
                    value = value + other[part, tile]
                start += [share[side] * value] * 6
        else:
            start = [zeros] * 12
        carried = lax.fori_loop(0, plan.shards, block, tuple(start))
        if not upward:
            for part in range(2):
                value = carried[6 * part] * cosine[0]
                for d in range(1, 6):
                    value = value + carried[6 * part + d] * cosine[d]
                value = value + pltpu.roll(value, 4, 0)
                if extra:
                    swapped = jnp.where(sub % 2 == 0, pltpu.roll(value, 7, 0), pltpu.roll(value, 1, 0))
                    flux[part, tile] = value + swapped
                elif side == 0:
                    flux[part, tile] = value
                else:
                    flux[part, tile] = flux[part, tile] + value
    for side in range(3 if at == 0 else 2):
        for d in range(6):
            sums[side, d] = jnp.sum(totals[side, d], axis=-1)


def sweep(plan, at, upward, groups, *operands):
    tiles = plan.steps(at)
    sides = 3 if at == 0 else 2
    vmem = pl.BlockSpec(memory_space=pltpu.VMEM)
    out_shape = plan.shapes(at, plan.sides_back(at) if upward else 2)
    if not upward:
        out_shape.append(jax.ShapeDtypeStruct((2, tiles, 8, LANES), jnp.float32))
    out_shape.append(jax.ShapeDtypeStruct((sides, 6, plan.depth, 8), jnp.float32))
    if not upward and at == 0:
        out_shape.append(jax.ShapeDtypeStruct((plan.depth, 2, 8, LANES), jnp.float32))
    return pl.pallas_call(
        functools.partial(sweep_kernel, plan, at, upward, groups),
        in_specs=[vmem] * len(operands),
        out_specs=[vmem] * len(out_shape),
        out_shape=out_shape,
        scratch_shapes=[pltpu.VMEM((sides, 6, plan.depth, 8, LANES), jnp.float32)],
        compiler_params=PARAMS,
        cost_estimate=cost(13),
        name="upward" if upward else "downward",
    )(*operands)


def mirror_kernel(plan, group, upper, lanes_turned, rows_turned, turned, lead):
    rows, half = plan.rows, plan.half
    cells = upper.shape[1]
    for part in range(2):
        sign = 1.0 if part == 0 else -1.0
        pairs = split(sign * upper[part].reshape(cells * rows, half))
        value = dot(pairs[0], lanes_turned[...]) + dot(pairs[1], lanes_turned[...])
        lead[part] = value.reshape(cells, rows, half)[:, 0, :]
        pairs = split(value)
        value = dot(rows_turned[...], pairs[0]) + dot(rows_turned[...], pairs[1])
        turned[part] = value.reshape(cells, rows, half)


def mirror(plan, forward, groups):
    cells = 8
    rows, half = plan.rows, plan.half
    share = plan.depth // groups
    lanes_turned = np.zeros((half, half), ml_dtypes.bfloat16)
    rows_turned = np.zeros((cells * rows, cells * rows), ml_dtypes.bfloat16)
    for k in range(1, half):
        lanes_turned[half - k, k] = 1
    for c in range(cells):
        for r in range(1, rows):
            rows_turned[c * rows + r, c * rows + rows - r] = 1
    lanes_turned, rows_turned = jnp.asarray(lanes_turned), jnp.asarray(rows_turned)
    blocks = share // cells
    group = lax.axis_index("ba").astype(jnp.int32).reshape(1)
    spec = pltpu.PrefetchScalarGridSpec(
        num_scalar_prefetch=1,
        grid=(forward.shape[0], blocks),
        in_specs=[
            pl.BlockSpec((None, 2, cells, rows, half), lambda step, z, at: (step, 0, at[0] * blocks + z, 0, 1)),
            pl.BlockSpec(lanes_turned.shape, lambda step, z, at: (0, 0)),
            pl.BlockSpec(rows_turned.shape, lambda step, z, at: (0, 0)),
        ],
        out_specs=[
            pl.BlockSpec((None, 2, cells, rows, half), lambda step, z, at: (step, 0, z, 0, 0)),
            pl.BlockSpec((None, 2, cells, half), lambda step, z, at: (step, 0, z, 0)),
        ],
    )
    return pl.pallas_call(
        functools.partial(mirror_kernel, plan),
        grid_spec=spec,
        out_shape=[
            jax.ShapeDtypeStruct((forward.shape[0], 2, share, rows, half), jnp.float32),
            jax.ShapeDtypeStruct((forward.shape[0], 2, share, half), jnp.float32),
        ],
        compiler_params=PARAMS,
        cost_estimate=cost(5),
        name="mirrored",
    )(group, forward, lanes_turned, rows_turned)


def aims_kernel(plan, group, own, other, keep, *refs):
    outs, held = refs[:-1], refs[-1]
    rows, half, chunk, tiles = plan.rows, plan.half, plan.chunk, plan.tiles
    cells = own.shape[1]
    owner = keep[...] > 0.0
    row = lax.broadcasted_iota(jnp.int32, (rows, half), 0)
    sub = lax.broadcasted_iota(jnp.int32, (8, LANES), 0)
    lane = lax.broadcasted_iota(jnp.int32, (1, LANES), 1)
    for part in range(2):
        line = own[part, :, :, half:].reshape(cells * rows, half).T[:1]
        if cells * rows < LANES:
            line = jnp.concatenate([line, jnp.zeros((1, LANES - cells * rows), jnp.float32)], axis=1)
        for cell in range(cells):
            mine, theirs = own[part, cell, :, :half], other[part, cell]
            held[...] = mine + jnp.where((row == 0) & owner[:1], 0.0, theirs)
            for at in range(plan.chunks):
                for tile in range(tiles):
                    four = held[pl.ds(at * chunk + tile, 4, stride=tiles), :]
                    outs[at][cell, part, tile] = jnp.concatenate([four, four], axis=0)
            partner = jnp.where(owner, theirs[:1], 0.0)
            start = cell * rows
            piece = line[:, start // LANES * LANES : start // LANES * LANES + LANES]
            at_zero = pltpu.roll(piece, LANES - start % LANES, 1) if start % LANES else piece
            outs[0][cell, part, tiles] = jnp.where(sub % 4 < 2, partner, jnp.where(lane < rows, at_zero, 0.0))


def make_aims(plan, own, other, keep, step):
    cells = 8
    rows, half = plan.rows, plan.half
    groups = other.shape[0]
    blocks = other.shape[2] // cells
    group = lax.axis_index("ba").astype(jnp.int32).reshape(1)

    def sender(z, at):
        return (lax.rem(at[0] + groups - z // blocks, groups), 0, z % blocks, 0, 0)

    spec = pltpu.PrefetchScalarGridSpec(
        num_scalar_prefetch=1,
        grid=(plan.depth // cells,),
        in_specs=[
            pl.BlockSpec((None, 2, cells, rows, plan.width), lambda z, at: (step, 0, z, 0, 0)),
            pl.BlockSpec((None, 2, cells, rows, half), sender),
            pl.BlockSpec(keep.shape, lambda z, at: (0, 0)),
        ],
        out_specs=[pl.BlockSpec((cells, 2, plan.steps(at), 8, LANES), lambda z, at: (z, 0, 0, 0, 0)) for at in range(plan.chunks)],
        scratch_shapes=[pltpu.VMEM((rows, half), jnp.float32)],
    )
    return pl.pallas_call(
        functools.partial(aims_kernel, plan),
        grid_spec=spec,
        out_shape=[jax.ShapeDtypeStruct((plan.depth, 2, plan.steps(at), 8, LANES), jnp.float32) for at in range(plan.chunks)],
        compiler_params=PARAMS,
        cost_estimate=cost(8),
        name="targets",
    )(group, own, other, keep)


def lift(value):
    main = jnp.broadcast_to(value.reshape(2, 2, 1), (2, 2, 4)).reshape(2, 8)
    extra = jnp.broadcast_to(value.reshape(2, 2).T[:, None, :], (2, 2, 2)).reshape(1, 8)
    return jnp.broadcast_to(jnp.concatenate([main, extra])[:, :, None], (3, 8, LANES))


def factors(plan, at, place, rate, speed):
    unit = 1.5 * 2.0 * math.pi / plan.width
    half, width, tiles = plan.half, plan.width, plan.tiles
    base = place * plan.rows
    sub = jnp.arange(8)

    def signed(index):
        return ((index + half) % width - half).astype(jnp.float32) * unit

    row = base + at * plan.chunk + jnp.arange(tiles)[:, None] + tiles * (sub % 4)[None, :]
    freq_x = jnp.broadcast_to(signed(row)[None, :, :, None], (2, tiles, 8, LANES)).reshape(2 * tiles, 8, LANES)
    freq_y = jnp.broadcast_to(signed(jnp.arange(LANES)), (2 * tiles, 8, LANES))
    sides = [0] * tiles + [1] * tiles
    if at == 0:
        partner = (sub % 4 < 2)[:, None]
        extra_x = jnp.where(partner, -signed(base), signed(base + jnp.arange(LANES) % plan.rows)[None, :])
        extra_y = jnp.where(partner, signed(jnp.arange(LANES))[None, :], signed(jnp.asarray(half)))
        freq_x = jnp.concatenate([freq_x, extra_x[None]], axis=0)
        freq_y = jnp.concatenate([freq_y, extra_y[None]], axis=0)
        sides.append(2)
    rate, speed = [jnp.concatenate([v[s : s + 1] for s in sides]) for v in (rate, speed)]
    cosine, along_x, along_y = [np.asarray(q, np.float32).reshape(12, 1, 1, 1) for q in quadrature()]
    wave = speed * (along_x * freq_x + along_y * freq_y)
    real = rate + np.abs(cosine) * speed
    denom = real * real + wave * wave
    return jnp.stack([real / denom, -wave / denom])


def body(phi_start, coeff, forward, rates, speeds, shares):
    shards = lax.axis_size("gx")
    groups = lax.axis_size("ba")
    place = lax.axis_index("gx")
    cells, bands, width, _ = phi_start.shape
    rows = forward.shape[3]
    steps = forward.shape[0]
    plan = Plan(shards, cells, width, rows)
    depth = plan.depth
    consts = [jnp.asarray(part) for part in tables(width)]
    owner = place * rows == plan.half
    keep = jnp.broadcast_to(jnp.where(owner, 1.0, 0.0).astype(jnp.float32), (8, LANES))
    rate, speed, share = lift(rates), lift(speeds), lift(shares)
    polar = np.abs(np.asarray(quadrature()[0][:6], np.float32)).reshape(1, 6, 1, 1)
    couple = polar * speed[:, None]
    inverse = [factors(plan, at, place, rate, speed) for at in range(plan.chunks)]

    def tie(value, *others):
        return lax.optimization_barrier((value, *others))[0]

    def swap_targets(turned, lead):
        turned = lax.ppermute(turned, "gx", [(i, shards - 1 - i) for i in range(shards)])
        lead = lax.ppermute(lead, "gx", [(i, (shards - i) % shards) for i in range(shards)])
        return jnp.where(jnp.arange(rows)[:, None] == 0, lead[:, :, :, None, :], turned)

    def spread_targets(turned):
        parts = [turned]
        for shift in range(1, groups):
            parts.append(lax.ppermute(turned, "ba", [(i, (i + shift) % groups) for i in range(groups)]))
        return parts

    def exchange(array):
        return lax.all_to_all(array, "gx", split_axis=0, concat_axis=0, tiled=True)

    main_sums, extra_sums = [[], []], [[], []]

    def collect(sums, way):
        main_sums[way].append(sums[:2])
        if sums.shape[0] == 3:
            extra_sums[way].append(sums[2])

    def into(transform):
        pieces, held = [[] for _ in range(plan.chunks)], None
        for side in range(2):
            held = transform(side, held)
            for at in range(plan.chunks):
                if plan.sides_sent(at) == 2 or side == 1:
                    pieces[at].append(held[at])
        return pieces

    def in_order(pieces, after, besides=()):
        arrived = []
        for piece in pieces:
            if after is not None:
                piece = tie(piece, after, *besides)
            after = exchange(piece)
            arrived.append(after)
        return arrived

    flipped = mirror(plan, forward, groups)
    swapped = swap_targets(*flipped)
    starts = [tie(phi_start, *flipped), tie(phi_start, swapped)]
    sent = into(lambda side, held: first(plan, side, starts[side], consts, held))
    spread = [spread_targets(swapped[step]) for step in range(steps)]
    aims = [None] * steps
    for step in range(steps):
        modes, after = [], None
        for at in range(plan.chunks):
            besides = spread[0][1 : 2 if at == 0 and plan.chunks > 1 else groups] if step == 0 else ()
            modes.append(in_order(sent[at], after, besides))
            after = modes[at][-1]
        if step == 0:
            aims[0] = make_aims(plan, forward, jnp.stack(spread[0]), keep, 0)
        back = []
        for at in range(plan.chunks):
            inv = inverse[at]
            common = (*modes[at], aims[step][at])
            part0, part1, flux, sums, *extras = sweep(plan, at, False, groups, *common, inv[:, :6], couple, rate)
            collect(sums, 0)
            fluxes = [flux]
            for shift in range(1, groups):
                fluxes.append(lax.ppermute(flux, "ba", [(i, (i + shift) % groups) for i in range(groups)]))
            rest = (part0, part1, *extras, share, keep, *fluxes)
            *new, sums = sweep(plan, at, True, groups, *common, inv[:, 6:], couple, rate, *rest)
            collect(sums, 1)
            if step + 1 < steps and at == 0:
                new[0] = tie(new[0], *spread[step + 1])
            if step + 1 < steps and at == plan.chunks - 1:
                aims[step + 1] = make_aims(plan, forward, jnp.stack(spread[step + 1]), keep, step + 1)
                new[0] = tie(new[0], *aims[step + 1])
            back.append(in_order(new, back[-1][-1] if back else None))
        ends = [[pieces[side % len(pieces)] for pieces in back] for side in range(2)]
        if step + 1 < steps:
            sent = into(lambda side, held: middle(plan, side, ends[side], coeff, consts, held))
        else:
            upper = last(plan, 0, ends[0], coeff, consts, None)
            phi = last(plan, 1, ends[1], coeff, consts, upper)

    grads = []
    for way in range(2):
        main = sum(main_sums[way]).reshape(2, 6, depth, 2, 4).sum(axis=4)
        extra = sum(extra_sums[way]).reshape(6, depth, 2, 2, 2).sum(axis=3)
        grads.append(main.transpose(2, 1, 0, 3) + extra.transpose(1, 0, 3, 2))
    sums = jnp.stack(grads, axis=1).reshape(shards, cells * 12 * bands) * (1.0 / width)
    grad = exchange(tie(sums, back[-1][-1], upper)).sum(axis=0).reshape(cells, 12, bands)
    return (phi, grad)


def solution(mesh):
    in_specs = (
        P("gx", "ba", None, None),
        P("gx", None, None),
        P(None, None, None, "gx", None),
        P("ba"),
        P("ba"),
        P("ba"),
    )
    out_specs = (P("gx", "ba", None, None), P("gx", None, "ba"))
    return jax.shard_map(body, mesh=mesh, in_specs=in_specs, out_specs=out_specs, check_vma=False)
```

time: 780 us -> 549 us (0.70)
  blocking collectives: 229 us -> 93.1 us
  waiting for transfers between devices: 223 us -> 108 us
  starting transfers between devices: 42.6 us -> 78.5 us
  local copies, waits for them, and re-layouts: 44.2 us -> 15.3 us
  Pallas kernels: 227 us -> 238 us
    all_to_all x5 -> x3, blocking collectives: 229 us -> 93.1 us  [exchange(): return lax.all_to_all(array, 'gx', split_axis=0, concat_axis=0, tiled=True)]
    ppermute x16 -> x20, waiting for transfers between devices: 163 us -> 62.1 us  [the longest x6 36.6 us: spread_targets(): lax.ppermute(turned, 'ba', [(i, (i + shift) % groups) for i in range(grou...]
    all_to_all x4 -> x10, starting transfers between devices: 18.4 us -> 42.5 us  [exchange(): return lax.all_to_all(array, 'gx', split_axis=0, concat_axis=0, tiled=True)]
    slice x7 -> x3, local copies, waits for them, and re-layouts: 22.1 us -> 1.22 us  [the longest x1 1.08 us: body(): spread = [spread_targets(swapped[step]) for step in range(steps)]]
    all_to_all x4 -> x10, waiting for transfers between devices: 60.1 us -> 45.5 us  [exchange(): return lax.all_to_all(array, 'gx', split_axis=0, concat_axis=0, tiled=True)]
    ppermute x16 -> x20, starting transfers between devices: 24.1 us -> 36 us  [the longest x12 20.7 us: body(): lax.ppermute(flux, 'ba', [(i, (i + shift) % groups) for i in range(groups)])]
    unnamed x33 -> x79, local copies, waits for them, and re-layouts: 16.6 us -> 6.97 us
    pallas_call x12 -> x15, Pallas kernels: 200 us -> 206 us  [the longest x8 112 us: sweep(): pl.pallas_call(functools.partial(sweep_kernel, plan, at, upward, groups),...]
  transfers between devices with their start and end apart: 20 -> 30, of which waited for: 13 -> 19; matrix products, arithmetic and copies ran while one was open for 7% -> 4% of each run, Pallas kernels for 14% -> 43%
where the time goes in v2:
time: 549 us; the launch traced here: 547 us
  Pallas kernels  238 us (43%)
  waiting for transfers between devices  108 us (20%)
  blocking collectives  93.1 us (17%)
  starting transfers between devices  78.5 us (14%)
  local copies, waits for them, and re-layouts  15.3 us (3%)
  other arithmetic  13.1 us (2%)
    pallas_call x8, Pallas kernels, sweep(): pl.pallas_call(functools.partial(sweep_kernel, plan, at, upward, groups),...  112 us
    all_to_all x3, blocking collectives, exchange(): return lax.all_to_all(array, 'gx', split_axis=0, concat_axis=0, tiled=True)  93.1 us
    pallas_call x4, Pallas kernels, send(): pl.pallas_call(functools.partial(kernel, plan, len(aliases)), grid=(plan....  74.3 us
    all_to_all x10, waiting for transfers between devices, exchange(): return lax.all_to_all(array, 'gx', split_axis=0, concat_axis=0, tiled=True)  45.5 us
    all_to_all x10, starting transfers between devices, exchange(): return lax.all_to_all(array, 'gx', split_axis=0, concat_axis=0, tiled=True)  42.5 us
    ppermute x6, waiting for transfers between devices, spread_targets(): lax.ppermute(turned, 'ba', [(i, (i + shift) % groups) for i in range(grou...  36.6 us
    pallas_call x2, Pallas kernels, last(): pl.pallas_call(functools.partial(last_kernel, plan), grid=(plan.cells,),...  32.4 us
    ppermute x12, waiting for transfers between devices, body(): lax.ppermute(flux, 'ba', [(i, (i + shift) % groups) for i in range(groups)])  22 us
  transfers between devices with their start and end apart: 30, of which 19 were waited for; matrix products, arithmetic and copies ran while one was open for 4% of the time, Pallas kernels for 43%

profile of v2, /device:TPU:0, one launch (start us, length us, event | category | flops | bytes accessed | tf_op | source)
XLA Modules:
  0.0 547.1 jit_solution(12672238058224908482)
XLA Ops:
  0.6 4.9 mirrored.1
  5.6 3.3 collective-permute-start.1
  8.9 1.4 collective-permute-start
  10.3 12.0 %into_modes.2 = (f32[8,520,128]{2,1,0:T(8,128)}, f32[8,1024,128]{2,1,0:T(8,128)}) custom-call(f32[8,4,256,256]{3,2,1,0:T(8,128)} %phi.1, bf16[256,256]{1,0:T(8,128)(2,1)} %constant.161.clone.into_h.refs_3_, bf16[256,256]{1,0:T(8,128)(2,1)} %constant.162.clone.into_l.refs_4_, bf16[512,256]{1,0:T(8,128)(2,1)} %constant.163.clone.stacked_h.refs_5_, ...), custom_call_target="tpu_custom_call" | custom-call | bytes 44280000 | tf_op jit(solution)/shard_map/into_modes/pallas_call | solution.py:240
  22.3 4.9 all-to-all-start
  29.3 3.5 collective-permute-done.1
  34.1 2.3 collective-permute-start.2
  36.7 12.1 %into_modes.3 = (f32[8,520,128]{2,1,0:T(8,128)}, f32[8,1024,128]{2,1,0:T(8,128)}) custom-call(f32[8,4,256,256]{3,2,1,0:T(8,128)} %phi.1, bf16[256,256]{1,0:T(8,128)(2,1)} %constant.161.clone.into_h.refs_3_, bf16[256,256]{1,0:T(8,128)(2,1)} %constant.162.clone.into_l.refs_4_, ...), custom_call_target="tpu_custom_call", output_to_operand_aliasing={{1}: (5, {})} | custom-call | bytes 44280000 | tf_op jit(solution)/shard_map/into_modes/pallas_call | solution.py:240
  48.8 2.3 collective-permute-done.2
  51.1 4.9 all-to-all-done.refs_0_
  56.1 1.3 copy-done
  57.4 4.7 all-to-all-start.1
  62.6 4.0 collective-permute-start.4
  66.7 12.5 %collective-permute-done.4 = f32[2,16,32,128]{3,2,1,0:T(8,128)} collective-permute-done((f32[2,16,32,128]{3,2,1,0:T(8,128)}, f32[2,16,32,128]{3,2,1,0:T(8,128)}, u32[]{:S(2)}, u32[]{:S(2)}) %collective-permute-start.4) | collective-permute-done | bytes 524320 | tf_op jit(solution)/shard_map/ppermute | solution.py:609
  79.2 21.8 %collective-permute-done.3 = f32[2,16,32,128]{3,2,1,0:T(8,128)} collective-permute-done((f32[2,16,32,128]{3,2,1,0:T(8,128)}, f32[2,16,32,128]{3,2,1,0:T(8,128)}, u32[]{:S(2)}, u32[]{:S(2)}) %collective-permute-start.3) | collective-permute-done | bytes 524320 | tf_op jit(solution)/shard_map/ppermute | solution.py:609
  101.0 4.7 all-to-all-start.3
  109.0 3.4 collective-permute-start.9
  113.1 2.9 pad_maximum_fusion.other
  116.6 7.6 %targets.2 = (f32[64,2,5,8,128]{4,3,2,1,0:T(8,128)}, f32[64,2,4,8,128]{4,3,2,1,0:T(8,128)}) custom-call(s32[1]{0:T(128)} %bitcast.group, f32[2,2,64,32,256]{4,3,2,1,0:T(8,128)} %own.3, f32[4,2,16,32,128]{4,3,2,1,0:T(8,128)} %pad_maximum_fusion.other, f32[8,128]{1,0:T(8,128)} %broadcast_in_dim.180.keep.refs_10_.refs_8_), custom_call_target="tpu_custom_call" | custom-call | bytes 29520000 | tf_op jit(solution)/shard_map/targets/pallas_call | solution.py:537
  124.8 14.4 %downward.4 = (f32[8,520,128]{2,1,0:T(8,128)}, f32[8,520,128]{2,1,0:T(8,128)}, f32[2,5,8,128]{3,2,1,0:T(8,128)}, f32[3,6,64,8]{3,2,1,0:T(8,128)}, f32[64,2,8,128]{3,2,1,0:T(8,128)}) custom-call(f32[8,520,128]{2,1,0:T(8,128)} %copy-done, f32[8,520,128]{2,1,0:T(8,128)} %all-to-all-done.1.refs_1_, f32[64,2,5,8,128]{4,3,2,1,0:T(8,128)} %get-tuple-element.65.refs_2_, ...), custom_call_target="tpu_custom_call" | custom-call | bytes 47970000 | tf_op jit(solution)/shard_map/downward/pallas_call | solution.py:425
  139.2 2.0 collective-permute-start.5
  141.7 6.5 %collective-permute-done.5.refs_12_ = f32[2,5,8,128]{3,2,1,0:T(8,128)S(1)} collective-permute-done((f32[2,5,8,128]{3,2,1,0:T(8,128)}, f32[2,5,8,128]{3,2,1,0:T(8,128)S(1)}, u32[]{:S(2)}, u32[]{:S(2)}) %collective-permute-start.5) | collective-permute-done | bytes 40992 | tf_op jit(solution)/shard_map/ppermute | solution.py:662
  149.2 11.5 %collective-permute-done.6.refs_13_ = f32[2,5,8,128]{3,2,1,0:T(8,128)S(1)} collective-permute-done((f32[2,5,8,128]{3,2,1,0:T(8,128)}, f32[2,5,8,128]{3,2,1,0:T(8,128)S(1)}, u32[]{:S(2)}, u32[]{:S(2)}) %collective-permute-start.6) | collective-permute-done | bytes 40992 | tf_op jit(solution)/shard_map/ppermute | solution.py:662
  161.5 16.4 %upward.4 = (f32[8,1040,128]{2,1,0:T(8,128)}, f32[3,6,64,8]{3,2,1,0:T(8,128)}) custom-call(f32[8,520,128]{2,1,0:T(8,128)} %copy-done, f32[8,520,128]{2,1,0:T(8,128)} %all-to-all-done.1.refs_1_, f32[64,2,5,8,128]{4,3,2,1,0:T(8,128)} %get-tuple-element.65.refs_2_, f32[2,6,9,8,128]{4,3,2,1,0:T(8,128)} %get-tuple-element.121.refs_3_, ...), custom_call_target="tpu_custom_call" | custom-call | bytes 47970000 | tf_op jit(solution)/shard_map/upward/pallas_call | solution.py:425
  178.0 4.8 all-to-all-start.2
  184.0 11.9 %downward.5 = (f32[8,512,128]{2,1,0:T(8,128)}, f32[8,512,128]{2,1,0:T(8,128)}, f32[2,4,8,128]{3,2,1,0:T(8,128)}, f32[2,6,64,8]{3,2,1,0:T(8,128)}) custom-call(f32[8,1024,128]{2,1,0:T(8,128)} %all-to-all-done.3.refs_0_, f32[64,2,4,8,128]{4,3,2,1,0:T(8,128)} %get-tuple-element.74.refs_1_, f32[2,6,8,8,128]{4,3,2,1,0:T(8,128)} %get-tuple-element.122.refs_2_, ...), custom_call_target="tpu_custom_call" | custom-call | bytes 47970000 | tf_op jit(solution)/shard_map/downward/pallas_call | solution.py:425
  196.0 1.5 collective-permute-start.11
  197.5 1.5 collective-permute-start.12
  198.9 2.9 collective-permute-start.13
  201.8 1.6 pad_maximum_fusion.1.other
  203.5 7.5 %targets.3 = (f32[64,2,5,8,128]{4,3,2,1,0:T(8,128)}, f32[64,2,4,8,128]{4,3,2,1,0:T(8,128)}) custom-call(s32[1]{0:T(128)} %bitcast.group, f32[2,2,64,32,256]{4,3,2,1,0:T(8,128)} %own.3, f32[4,2,16,32,128]{4,3,2,1,0:T(8,128)} %pad_maximum_fusion.1.other, f32[8,128]{1,0:T(8,128)} %broadcast_in_dim.180.keep.refs_10_.refs_8_), custom_call_target="tpu_custom_call" | custom-call | bytes 29520000 | tf_op jit(solution)/shard_map/targets/pallas_call | solution.py:537
  211.6 13.1 %upward.5 = (f32[8,512,128]{2,1,0:T(8,128)}, f32[8,512,128]{2,1,0:T(8,128)}, f32[2,6,64,8]{3,2,1,0:T(8,128)}) custom-call(f32[8,1024,128]{2,1,0:T(8,128)} %all-to-all-done.3.refs_0_, f32[64,2,4,8,128]{4,3,2,1,0:T(8,128)} %get-tuple-element.74.refs_1_, f32[2,6,8,8,128]{4,3,2,1,0:T(8,128)} %get-tuple-element.123.refs_2_, ...), custom_call_target="tpu_custom_call" | custom-call | bytes 47970000 | tf_op jit(solution)/shard_map/upward/pallas_call | solution.py:425
  224.8 7.6 %all-to-all-done.2.refs_0_ = f32[8,1040,128]{2,1,0:T(8,128)} async-done(((f32[8,1040,128]{2,1,0:T(8,128)}), f32[8,1040,128]{2,1,0:T(8,128)}, u32[]{:S(2)}, u32[]{:S(2)}) %all-to-all-start.2) | async-done | bytes 4259872 | tf_op jit(solution)/shard_map/all_to_all | solution.py:613
  232.4 30.9 %all_to_all.69.refs_1_ = f32[8,512,128]{2,1,0:T(8,128)} all-to-all(f32[8,512,128]{2,1,0:T(8,128)} %get-tuple-element.82), channel_id=1, replica_groups=mesh['gx'=8,'ba'=4] {'gx'}, dimensions={0} | all-to-all | bytes 4194304 | tf_op jit(solution)/shard_map/all_to_all | solution.py:613
  263.3 3.6 all-to-all-start.6
  267.0 25.1 %between_steps.2 = (f32[8,520,128]{2,1,0:T(8,128)}, f32[8,1024,128]{2,1,0:T(8,128)}) custom-call(f32[8,1040,128]{2,1,0:T(8,128)} %all-to-all-done.2.refs_0_, f32[8,512,128]{2,1,0:T(8,128)} %all_to_all.69.refs_1_, f32[8,256,256]{2,1,0:T(8,128)} %refs_2_.7, bf16[256,256]{1,0:T(8,128)(2,1)} %constant.161.clone.into_h.refs_3_, ...), custom_call_target="tpu_custom_call" | custom-call | bytes 92250000 | tf_op jit(solution)/shard_map/between_steps/pallas_call | solution.py:240
  292.0 1.5 all-to-all-done.6.refs_1_
  293.5 1.3 copy-done.3
  294.9 3.6 all-to-all-start.5
  298.5 25.1 %between_steps.3 = (f32[8,520,128]{2,1,0:T(8,128)}, f32[8,1024,128]{2,1,0:T(8,128)}) custom-call(f32[8,1040,128]{2,1,0:T(8,128)} %all-to-all-done.2.refs_0_, f32[8,512,128]{2,1,0:T(8,128)} %copy-done.3, f32[8,256,256]{2,1,0:T(8,128)} %refs_2_.7, bf16[256,256]{1,0:T(8,128)(2,1)} %constant.161.clone.into_h.refs_3_, ...), custom_call_target="tpu_custom_call", output_to_operand_aliasing={{1}: (11, {})} | custom-call | bytes 92250000 | tf_op jit(solution)/shard_map/between_steps/pallas_call | solution.py:240
  323.6 1.8 all-to-all-done.5.refs_0_
  325.4 31.3 %all_to_all.70.refs_1_ = f32[8,520,128]{2,1,0:T(8,128)} all-to-all(f32[8,520,128]{2,1,0:T(8,128)} %get-tuple-element.88), channel_id=1, replica_groups=mesh['gx'=8,'ba'=4] {'gx'}, dimensions={0} | all-to-all | bytes 4259840 | tf_op jit(solution)/shard_map/all_to_all | solution.py:613
  356.7 4.6 all-to-all-start.9
  361.2 14.4 %downward.6 = (f32[8,520,128]{2,1,0:T(8,128)}, f32[8,520,128]{2,1,0:T(8,128)}, f32[2,5,8,128]{3,2,1,0:T(8,128)}, f32[3,6,64,8]{3,2,1,0:T(8,128)}, f32[64,2,8,128]{3,2,1,0:T(8,128)}) custom-call(f32[8,520,128]{2,1,0:T(8,128)} %copy-done.1, f32[8,520,128]{2,1,0:T(8,128)} %all_to_all.70.refs_1_, f32[64,2,5,8,128]{4,3,2,1,0:T(8,128)} %get-tuple-element.79.refs_2_, ...), custom_call_target="tpu_custom_call" | custom-call | bytes 47970000 | tf_op jit(solution)/shard_map/downward/pallas_call | solution.py:425
  375.6 1.5 collective-permute-start.14
  377.1 1.5 collective-permute-start.15
  378.6 2.9 collective-permute-start.16
  381.6 1.4 collective-permute-done.15.refs_13_
  384.1 16.4 %upward.6 = (f32[8,1040,128]{2,1,0:T(8,128)}, f32[3,6,64,8]{3,2,1,0:T(8,128)}) custom-call(f32[8,520,128]{2,1,0:T(8,128)} %copy-done.1, f32[8,520,128]{2,1,0:T(8,128)} %all_to_all.70.refs_1_, f32[64,2,5,8,128]{4,3,2,1,0:T(8,128)} %get-tuple-element.79.refs_2_, f32[2,6,9,8,128]{4,3,2,1,0:T(8,128)} %get-tuple-element.121.refs_3_, ...), custom_call_target="tpu_custom_call" | custom-call | bytes 47970000 | tf_op jit(solution)/shard_map/upward/pallas_call | solution.py:425
  400.5 9.8 %all-to-all-done.9.refs_0_ = f32[8,1024,128]{2,1,0:T(8,128)} async-done(((f32[8,1024,128]{2,1,0:T(8,128)}), f32[8,1024,128]{2,1,0:T(8,128)}, u32[]{:S(2)}, u32[]{:S(2)}) %all-to-all-start.9) | async-done | bytes 4194336 | tf_op jit(solution)/shard_map/all_to_all | solution.py:613
  410.4 4.6 all-to-all-start.8
  414.9 11.8 %downward.7 = (f32[8,512,128]{2,1,0:T(8,128)}, f32[8,512,128]{2,1,0:T(8,128)}, f32[2,4,8,128]{3,2,1,0:T(8,128)}, f32[2,6,64,8]{3,2,1,0:T(8,128)}) custom-call(f32[8,1024,128]{2,1,0:T(8,128)} %all-to-all-done.9.refs_0_, f32[64,2,4,8,128]{4,3,2,1,0:T(8,128)} %get-tuple-element.80.refs_1_, f32[2,6,8,8,128]{4,3,2,1,0:T(8,128)} %get-tuple-element.122.refs_2_, ...), custom_call_target="tpu_custom_call" | custom-call | bytes 47970000 | tf_op jit(solution)/shard_map/downward/pallas_call | solution.py:425
  426.7 1.5 collective-permute-start.17
  428.3 1.5 collective-permute-start.18
  429.7 2.9 collective-permute-start.19
  435.2 13.2 %upward.7 = (f32[8,512,128]{2,1,0:T(8,128)}, f32[8,512,128]{2,1,0:T(8,128)}, f32[2,6,64,8]{3,2,1,0:T(8,128)}) custom-call(f32[8,1024,128]{2,1,0:T(8,128)} %all-to-all-done.9.refs_0_, f32[64,2,4,8,128]{4,3,2,1,0:T(8,128)} %get-tuple-element.80.refs_1_, f32[2,6,8,8,128]{4,3,2,1,0:T(8,128)} %get-tuple-element.123.refs_2_, ...), custom_call_target="tpu_custom_call" | custom-call | bytes 47970000 | tf_op jit(solution)/shard_map/upward/pallas_call | solution.py:425
  448.4 16.4 %all-to-all-done.8.refs_0_ = f32[8,1040,128]{2,1,0:T(8,128)} async-done(((f32[8,1040,128]{2,1,0:T(8,128)}), f32[8,1040,128]{2,1,0:T(8,128)}, u32[]{:S(2)}, u32[]{:S(2)}) %all-to-all-start.8) | async-done | bytes 4259872 | tf_op jit(solution)/shard_map/all_to_all | solution.py:613
  464.8 30.9 %all_to_all.71.refs_1_ = f32[8,512,128]{2,1,0:T(8,128)} all-to-all(f32[8,512,128]{2,1,0:T(8,128)} %get-tuple-element.101), channel_id=1, replica_groups=mesh['gx'=8,'ba'=4] {'gx'}, dimensions={0} | all-to-all | bytes 4194304 | tf_op jit(solution)/shard_map/all_to_all | solution.py:613
  495.7 3.7 all-to-all-start.11
  503.2 1.4 add_add_fusion
  506.4 16.2 %out_of_modes.2.refs_7_ = f32[8,4,256,256]{3,2,1,0:T(8,128)} custom-call(f32[8,1040,128]{2,1,0:T(8,128)} %all-to-all-done.8.refs_0_, f32[8,512,128]{2,1,0:T(8,128)} %all_to_all.71.refs_1_, f32[8,256,256]{2,1,0:T(8,128)} %refs_2_.7, bf16[256,512]{1,0:T(8,128)(2,1)} %constant.165.clone.refs_7_.refs_3_, bf16[256,512]{1,0:T(8,128)(2,1)} %constant.166.clone.refs_8_.refs_4_, ...), custom_call_target="tpu_custom_call" | custom-call | bytes 59040000 | tf_op jit(solution)/shard_map/out_of_modes/pallas_call | solution.py:273
  522.6 3.4 all-to-all-done.11.refs_1_
  526.7 3.3 all-to-all-start.12
  530.0 16.2 %out_of_modes.3 = f32[8,4,256,256]{3,2,1,0:T(8,128)} custom-call(f32[8,1040,128]{2,1,0:T(8,128)} %all-to-all-done.8.refs_0_, f32[8,512,128]{2,1,0:T(8,128)} %copy-done.2, f32[8,256,256]{2,1,0:T(8,128)} %refs_2_.7, bf16[256,512]{1,0:T(8,128)(2,1)} %constant.165.clone.refs_7_.refs_3_, ...), custom_call_target="tpu_custom_call", output_to_operand_aliasing={{}: (7, {})} | custom-call | bytes 59040000 | tf_op jit(solution)/shard_map/out_of_modes/pallas_call | solution.py:273
  (178 shorter events, 24.3 us)
Async XLA Ops:
  5.6 27.2 %collective-permute-start.1 = (f32[2,2,16,32,128]{4,3,2,1,0:T(8,128)}, f32[2,2,16,32,128]{4,3,2,1,0:T(8,128)S(1)}, u32[]{:S(2)}, u32[]{:S(2)}) collective-permute-start(f32[2,2,16,32,128]{4,3,2,1,0:T(8,128)} %get-tuple-element.57), channel_id=1, source_target_pairs={{0,28},{4,24},{8,20},{12,16},{16,12},{20,8},{24,4},{28,0},{1,29},{... | collective-permute-start | bytes 3145736 | tf_op jit(solution)/shard_map/ppermute | solution.py:602
  8.9 20.4 %collective-permute-start = (f32[2,2,16,128]{3,2,1,0:T(8,128)}, f32[2,2,16,128]{3,2,1,0:T(8,128)S(1)}, u32[]{:S(2)}, u32[]{:S(2)}) collective-permute-start(f32[2,2,16,128]{3,2,1,0:T(8,128)} %get-tuple-element.58), channel_id=1, source_target_pairs={{0,0},{4,28},{8,24},{12,20},{16,16},{20,12},{24,8},{28,4},{1,1},{5... | collective-permute-start | bytes 98312 | tf_op jit(solution)/shard_map/ppermute | solution.py:603
  22.3 4.9 copy-start.20
  22.3 5.7 %copy-start.21 = (f32[4]{0:T(128)S(1)}, f32[4]{0:T(128)}, u32[]{:S(2)}) copy-start(f32[4]{0:T(128)} %param.26) | copy-start | bytes 52
  22.3 33.7 %all-to-all-start = ((f32[8,520,128]{2,1,0:T(8,128)}), f32[8,520,128]{2,1,0:T(8,128)S(1)}, u32[]{:S(2)}, u32[]{:S(2)}) async-start(f32[8,520,128]{2,1,0:T(8,128)} %get-tuple-element.60), calls=%async_computation | async-start | bytes 4259840 | tf_op jit(solution)/shard_map/all_to_all | solution.py:613
  34.1 14.7 %copy-start.6 = (f32[2,16,32,128]{3,2,1,0:T(8,128)}, f32[2,16,32,128]{3,2,1,0:T(8,128)S(1)}, u32[]{:S(2)}) copy-start(f32[2,16,32,128]{3,2,1,0:T(8,128)S(1)} %get-tuple-element.117) | copy-start | bytes 1572868
  34.1 17.0 %collective-permute-start.2 = (f32[2,16,32,128]{3,2,1,0:T(8,128)S(1)}, f32[2,16,32,128]{3,2,1,0:T(8,128)}, u32[]{:S(2)}, u32[]{:S(2)}) collective-permute-start(f32[2,16,32,128]{3,2,1,0:T(8,128)S(1)} %get-tuple-element.117), channel_id=1, source_target_pairs={{0,1},{1,2},{2,3},{3,0},{4,5},{5,6},{6,7},{7,4},{8,9},{9,10},{10,1... | collective-permute-start | bytes 1572872 | tf_op jit(solution)/shard_map/ppermute | solution.py:609
  56.1 1.3 copy-start
  57.4 43.5 %all-to-all-start.1 = ((f32[8,520,128]{2,1,0:T(8,128)}), f32[8,520,128]{2,1,0:T(8,128)}, u32[]{:S(2)}, u32[]{:S(2)}) async-start(f32[8,520,128]{2,1,0:T(8,128)} %get-tuple-element.64), calls=%async_computation.1 | async-start | bytes 4259840 | tf_op jit(solution)/shard_map/all_to_all | solution.py:613
  62.6 16.6 %collective-permute-start.4 = (f32[2,16,32,128]{3,2,1,0:T(8,128)}, f32[2,16,32,128]{3,2,1,0:T(8,128)}, u32[]{:S(2)}, u32[]{:S(2)}) collective-permute-start(f32[2,16,32,128]{3,2,1,0:T(8,128)} %copy-done.6), channel_id=1, source_target_pairs={{0,3},{1,0},{2,1},{3,2},{4,7},{5,4},{6,5},{7,6},{8,11},{9,8},{10,9... | collective-permute-start | bytes 1572872 | tf_op jit(solution)/shard_map/ppermute | solution.py:609
  66.6 34.4 %collective-permute-start.3 = (f32[2,16,32,128]{3,2,1,0:T(8,128)}, f32[2,16,32,128]{3,2,1,0:T(8,128)}, u32[]{:S(2)}, u32[]{:S(2)}) collective-permute-start(f32[2,16,32,128]{3,2,1,0:T(8,128)} %copy-done.6), channel_id=1, source_target_pairs={{0,2},{1,3},{2,0},{3,1},{4,6},{5,7},{6,4},{7,5},{8,10},{9,11},{10,... | collective-permute-start | bytes 1572872 | tf_op jit(solution)/shard_map/ppermute | solution.py:609
  101.0 5.9 %copy-start.22 = (f32[12]{0:T(128)S(1)}, f32[12]{0:T(128)}, u32[]{:S(2)}) copy-start(f32[12]{0:T(128)} %constant.177) | copy-start | bytes 148
  101.0 5.9 %copy-start.23 = (f32[12]{0:T(128)S(1)}, f32[12]{0:T(128)}, u32[]{:S(2)}) copy-start(f32[12]{0:T(128)} %constant.176) | copy-start | bytes 148
  101.0 5.9 %copy-start.24 = (f32[12]{0:T(128)S(1)}, f32[12]{0:T(128)}, u32[]{:S(2)}) copy-start(f32[12]{0:T(128)} %constant.175) | copy-start | bytes 148
  101.0 77.0 %all-to-all-start.3 = ((f32[8,1024,128]{2,1,0:T(8,128)}), f32[8,1024,128]{2,1,0:T(8,128)}, u32[]{:S(2)}, u32[]{:S(2)}) async-start(f32[8,1024,128]{2,1,0:T(8,128)} %get-tuple-element.73), calls=%async_computation.3 | async-start | bytes 8388608 | tf_op jit(solution)/shard_map/all_to_all | solution.py:613
  105.7 2.5 copy-start.5
  105.7 6.7 %copy-start.25 = (f32[6]{0:T(128)S(1)}, f32[6]{0:T(128)}, u32[]{:S(2)}) copy-start(f32[6]{0:T(128)} %constant.178) | copy-start | bytes 76
  108.1 69.8 %collective-permute-start.8 = (f32[2,16,32,128]{3,2,1,0:T(8,128)S(1)}, f32[2,16,32,128]{3,2,1,0:T(8,128)S(1)}, u32[]{:S(2)}, u32[]{:S(2)}) collective-permute-start(f32[2,16,32,128]{3,2,1,0:T(8,128)S(1)} %copy-done.5), channel_id=1, source_target_pairs={{0,1},{1,2},{2,3},{3,0},{4,5},{5,6},{6,7},{7,4},{8,9},{9,10},{10,1... | collective-permute-start | bytes 1572872 | tf_op jit(solution)/shard_map/ppermute | solution.py:609
  109.0 69.0 %collective-permute-start.9 = (f32[2,16,32,128]{3,2,1,0:T(8,128)S(1)}, f32[2,16,32,128]{3,2,1,0:T(8,128)S(1)}, u32[]{:S(2)}, u32[]{:S(2)}) collective-permute-start(f32[2,16,32,128]{3,2,1,0:T(8,128)S(1)} %copy-done.5), channel_id=1, source_target_pairs={{0,2},{1,3},{2,0},{3,1},{4,6},{5,7},{6,4},{7,5},{8,10},{9,11},{10,... | collective-permute-start | bytes 1572872 | tf_op jit(solution)/shard_map/ppermute | solution.py:609
  112.4 65.6 %collective-permute-start.10 = (f32[2,16,32,128]{3,2,1,0:T(8,128)S(1)}, f32[2,16,32,128]{3,2,1,0:T(8,128)S(1)}, u32[]{:S(2)}, u32[]{:S(2)}) collective-permute-start(f32[2,16,32,128]{3,2,1,0:T(8,128)S(1)} %copy-done.5), channel_id=1, source_target_pairs={{0,3},{1,0},{2,1},{3,2},{4,7},{5,4},{6,5},{7,6},{8,11},{9,8},{10,9... | collective-permute-start | bytes 1572872 | tf_op jit(solution)/shard_map/ppermute | solution.py:609
  124.8 16.4 %copy-start.26 = (f32[4]{0:T(128)S(1)}, f32[4]{0:T(128)}, u32[]{:S(2)}) copy-start(f32[4]{0:T(128)} %param.28) | copy-start | bytes 52
  139.2 9.0 %collective-permute-start.5 = (f32[2,5,8,128]{3,2,1,0:T(8,128)}, f32[2,5,8,128]{3,2,1,0:T(8,128)S(1)}, u32[]{:S(2)}, u32[]{:S(2)}) collective-permute-start(f32[2,5,8,128]{3,2,1,0:T(8,128)} %get-tuple-element.69.refs_11_), channel_id=1, source_target_pairs={{0,1},{1,2},{2,3},{3,0},{4,5},{5,6},{6,7},{7,4},{8,9},{9,10},{10,1... | collective-permute-start | bytes 122888 | tf_op jit(solution)/shard_map/ppermute | solution.py:662
  141.7 19.1 %collective-permute-start.6 = (f32[2,5,8,128]{3,2,1,0:T(8,128)}, f32[2,5,8,128]{3,2,1,0:T(8,128)S(1)}, u32[]{:S(2)}, u32[]{:S(2)}) collective-permute-start(f32[2,5,8,128]{3,2,1,0:T(8,128)} %get-tuple-element.69.refs_11_), channel_id=1, source_target_pairs={{0,2},{1,3},{2,0},{3,1},{4,6},{5,7},{6,4},{7,5},{8,10},{9,11},{10,... | collective-permute-start | bytes 122888 | tf_op jit(solution)/shard_map/ppermute | solution.py:662
  148.2 13.3 %copy-start.8 = (f32[2,5,8,128]{3,2,1,0:T(8,128)}, f32[2,5,8,128]{3,2,1,0:T(8,128)S(1)}, u32[]{:S(2)}) copy-start(f32[2,5,8,128]{3,2,1,0:T(8,128)S(1)} %collective-permute-done.5.refs_12_) | copy-start | bytes 122884
  148.2 12.7 %collective-permute-start.7 = (f32[2,5,8,128]{3,2,1,0:T(8,128)}, f32[2,5,8,128]{3,2,1,0:T(8,128)S(1)}, u32[]{:S(2)}, u32[]{:S(2)}) collective-permute-start(f32[2,5,8,128]{3,2,1,0:T(8,128)} %get-tuple-element.69.refs_11_), channel_id=1, source_target_pairs={{0,3},{1,0},{2,1},{3,2},{4,7},{5,4},{6,5},{7,6},{8,11},{9,8},{10,9... | collective-permute-start | bytes 122888 | tf_op jit(solution)/shard_map/ppermute | solution.py:662
  160.7 0.8 copy-start.9
  160.9 0.7 copy-start.12
  178.0 54.4 %all-to-all-start.2 = ((f32[8,1040,128]{2,1,0:T(8,128)}), f32[8,1040,128]{2,1,0:T(8,128)}, u32[]{:S(2)}, u32[]{:S(2)}) async-start(f32[8,1040,128]{2,1,0:T(8,128)} %get-tuple-element.71), calls=%async_computation.2 | async-start | bytes 8519680 | tf_op jit(solution)/shard_map/all_to_all | solution.py:613
  196.0 15.0 %collective-permute-start.11 = (f32[2,4,8,128]{3,2,1,0:T(8,128)}, f32[2,4,8,128]{3,2,1,0:T(8,128)S(1)}, u32[]{:S(2)}, u32[]{:S(2)}) collective-permute-start(f32[2,4,8,128]{3,2,1,0:T(8,128)} %get-tuple-element.77.refs_9_), channel_id=1, source_target_pairs={{0,1},{1,2},{2,3},{3,0},{4,5},{5,6},{6,7},{7,4},{8,9},{9,10},{10,1... | collective-permute-start | bytes 98312 | tf_op jit(solution)/shard_map/ppermute | solution.py:662
  197.5 13.5 %collective-permute-start.12 = (f32[2,4,8,128]{3,2,1,0:T(8,128)}, f32[2,4,8,128]{3,2,1,0:T(8,128)S(1)}, u32[]{:S(2)}, u32[]{:S(2)}) collective-permute-start(f32[2,4,8,128]{3,2,1,0:T(8,128)} %get-tuple-element.77.refs_9_), channel_id=1, source_target_pairs={{0,2},{1,3},{2,0},{3,1},{4,6},{5,7},{6,4},{7,5},{8,10},{9,11},{10,... | collective-permute-start | bytes 98312 | tf_op jit(solution)/shard_map/ppermute | solution.py:662
  198.9 12.1 %collective-permute-start.13 = (f32[2,4,8,128]{3,2,1,0:T(8,128)}, f32[2,4,8,128]{3,2,1,0:T(8,128)S(1)}, u32[]{:S(2)}, u32[]{:S(2)}) collective-permute-start(f32[2,4,8,128]{3,2,1,0:T(8,128)} %get-tuple-element.77.refs_9_), channel_id=1, source_target_pairs={{0,3},{1,0},{2,1},{3,2},{4,7},{5,4},{6,5},{7,6},{8,11},{9,8},{10,9... | collective-permute-start | bytes 98312 | tf_op jit(solution)/shard_map/ppermute | solution.py:662
  211.0 0.6 copy-start.14
  211.0 0.6 copy-start.15
  211.0 0.6 copy-start.16
  263.3 30.2 %all-to-all-start.6 = ((f32[8,512,128]{2,1,0:T(8,128)}), f32[8,512,128]{2,1,0:T(8,128)S(1)}, u32[]{:S(2)}, u32[]{:S(2)}) async-start(f32[8,512,128]{2,1,0:T(8,128)} %get-tuple-element.85), calls=%async_computation.6 | async-start | bytes 4194304 | tf_op jit(solution)/shard_map/all_to_all | solution.py:613
  293.5 1.3 copy-start.3
  294.9 30.5 %all-to-all-start.5 = ((f32[8,520,128]{2,1,0:T(8,128)}), f32[8,520,128]{2,1,0:T(8,128)S(1)}, u32[]{:S(2)}, u32[]{:S(2)}) async-start(f32[8,520,128]{2,1,0:T(8,128)} %get-tuple-element.83), calls=%async_computation.5 | async-start | bytes 4259840 | tf_op jit(solution)/shard_map/all_to_all | solution.py:613
  325.4 31.3 %copy-start.1 = (f32[8,520,128]{2,1,0:T(8,128)}, f32[8,520,128]{2,1,0:T(8,128)S(1)}, u32[]{:S(2)}) copy-start(f32[8,520,128]{2,1,0:T(8,128)S(1)} %all-to-all-done.5.refs_0_) | copy-start | bytes 6389764
  356.7 53.7 %all-to-all-start.9 = ((f32[8,1024,128]{2,1,0:T(8,128)}), f32[8,1024,128]{2,1,0:T(8,128)}, u32[]{:S(2)}, u32[]{:S(2)}) async-start(f32[8,1024,128]{2,1,0:T(8,128)} %get-tuple-element.95), calls=%async_computation.9 | async-start | bytes 8388608 | tf_op jit(solution)/shard_map/all_to_all | solution.py:613
  375.6 6.0 %collective-permute-start.14 = (f32[2,5,8,128]{3,2,1,0:T(8,128)}, f32[2,5,8,128]{3,2,1,0:T(8,128)S(1)}, u32[]{:S(2)}, u32[]{:S(2)}) collective-permute-start(f32[2,5,8,128]{3,2,1,0:T(8,128)} %get-tuple-element.92.refs_11_), channel_id=1, source_target_pairs={{0,1},{1,2},{2,3},{3,0},{4,5},{5,6},{6,7},{7,4},{8,9},{9,10},{10,1... | collective-permute-start | bytes 122888 | tf_op jit(solution)/shard_map/ppermute | solution.py:662
  377.1 5.9 %collective-permute-start.15 = (f32[2,5,8,128]{3,2,1,0:T(8,128)}, f32[2,5,8,128]{3,2,1,0:T(8,128)S(1)}, u32[]{:S(2)}, u32[]{:S(2)}) collective-permute-start(f32[2,5,8,128]{3,2,1,0:T(8,128)} %get-tuple-element.92.refs_11_), channel_id=1, source_target_pairs={{0,2},{1,3},{2,0},{3,1},{4,6},{5,7},{6,4},{7,5},{8,10},{9,11},{10,... | collective-permute-start | bytes 122888 | tf_op jit(solution)/shard_map/ppermute | solution.py:662
  378.6 4.9 collective-permute-start.16
  381.6 1.9 copy-start.10
  383.0 0.6 copy-start.11
  383.5 0.6 copy-start.13
  410.4 54.4 %all-to-all-start.8 = ((f32[8,1040,128]{2,1,0:T(8,128)}), f32[8,1040,128]{2,1,0:T(8,128)}, u32[]{:S(2)}, u32[]{:S(2)}) async-start(f32[8,1040,128]{2,1,0:T(8,128)} %get-tuple-element.93), calls=%async_computation.8 | async-start | bytes 8519680 | tf_op jit(solution)/shard_map/all_to_all | solution.py:613
  426.7 5.9 %collective-permute-start.17 = (f32[2,4,8,128]{3,2,1,0:T(8,128)}, f32[2,4,8,128]{3,2,1,0:T(8,128)S(1)}, u32[]{:S(2)}, u32[]{:S(2)}) collective-permute-start(f32[2,4,8,128]{3,2,1,0:T(8,128)} %get-tuple-element.98.refs_9_), channel_id=1, source_target_pairs={{0,1},{1,2},{2,3},{3,0},{4,5},{5,6},{6,7},{7,4},{8,9},{9,10},{10,1... | collective-permute-start | bytes 98312 | tf_op jit(solution)/shard_map/ppermute | solution.py:662
  428.3 5.1 collective-permute-start.18
  429.7 4.8 collective-permute-start.19
  432.7 1.9 copy-start.17
  433.4 1.2 copy-start.18
  434.6 0.6 copy-start.19
  495.7 3.7 copy-start.4
  495.7 6.0 %copy-start.7 = (f32[2,6,64,8]{3,2,1,0:T(8,128)S(1)}, f32[2,6,64,8]{3,2,1,0:T(8,128)}, u32[]{:S(2)}) copy-start(f32[2,6,64,8]{3,2,1,0:T(8,128)} %get-tuple-element.104) | copy-start | bytes 73732
  495.7 30.3 %all-to-all-start.11 = ((f32[8,512,128]{2,1,0:T(8,128)}), f32[8,512,128]{2,1,0:T(8,128)S(1)}, u32[]{:S(2)}, u32[]{:S(2)}) async-start(f32[8,512,128]{2,1,0:T(8,128)} %get-tuple-element.102), calls=%async_computation.11 | async-start | bytes 4194304 | tf_op jit(solution)/shard_map/all_to_all | solution.py:613
  526.0 4.0 copy-start.2
  526.7 19.6 %all-to-all-start.12 = ((f32[8,1,384]{2,1,0:T(1,128)}), f32[8,1,384]{2,1,0:T(1,128)S(1)}, u32[]{:S(2)}, u32[]{:S(2)}) async-start(f32[8,1,384]{2,1,0:T(1,128)} %copy.51), calls=%async_computation.12 | async-start | bytes 24576 | tf_op jit(solution)/shard_map/all_to_all | solution.py:613

commit v3 on v2

--- a/solution.py
+++ b/solution.py
@@ -147,6 +147,7 @@
     shifted = [pltpu.roll(turned, LANES - shard, 1) if shard else turned for shard in range(plan.shards)]
     sides = [jnp.concatenate([held[g * rows : (g + 1) * rows] for held in shifted], axis=0) for g in range(4)]
     first = lax.broadcasted_iota(jnp.int32, (width, half), 1) == 0
+    uppers, lowers = [], []
     for band in range(2):
         reals, imags = [], []
         for shard in range(plan.shards):
@@ -155,10 +156,13 @@
                 reals.append(ins[at][shard, pl.ds(base + band * chunk, chunk), :])
                 imags.append(ins[at][shard, pl.ds(base + (2 + band) * chunk, chunk), :])
         real, imag = jnp.concatenate(reals, axis=0), jnp.concatenate(imags, axis=0)
-        upper = jnp.concatenate([real, jnp.where(first, sides[band], imag)], axis=1)
-        lower = jnp.concatenate([-imag, jnp.where(first, -sides[band + 2], real)], axis=1)
-        mixed = dot3(beside, split(jnp.concatenate([upper, lower], axis=0)))
-        take(band, dot3(split(mixed), back))
+        uppers += [real, jnp.where(first, sides[band], imag)]
+        lowers += [-imag, jnp.where(first, -sides[band + 2], real)]
+    pairs = jnp.concatenate([jnp.concatenate(uppers, axis=1), jnp.concatenate(lowers, axis=1)], axis=0)
+    mixed = dot3(beside, split(pairs))
+    out = dot3(split(jnp.concatenate([mixed[:, :width], mixed[:, width:]], axis=0)), back)
+    for band in range(2):
+        take(band, out[band * width : (band + 1) * width])
 
 
 def first_kernel(plan, kept, phi, into_h, into_l, stacked_h, stacked_l, *refs):
@@ -487,59 +491,64 @@
     )(group, forward, lanes_turned, rows_turned)
 
 
-def aims_kernel(plan, group, own, other, keep, *refs):
-    outs, held = refs[:-1], refs[-1]
-    rows, half, chunk, tiles = plan.rows, plan.half, plan.chunk, plan.tiles
-    cells = own.shape[1]
-    owner = keep[...] > 0.0
-    row = lax.broadcasted_iota(jnp.int32, (rows, half), 0)
+def aims_kernel(plan, at, group, own, other, keep, out, held):
+    half, chunk, tiles = plan.half, plan.chunk, plan.tiles
+    cells, rows = own.shape[1:3]
+    row = lax.broadcasted_iota(jnp.int32, (chunk, half), 0)
     sub = lax.broadcasted_iota(jnp.int32, (8, LANES), 0)
     lane = lax.broadcasted_iota(jnp.int32, (1, LANES), 1)
     for part in range(2):
-        line = own[part, :, :, half:].reshape(cells * rows, half).T[:1]
-        if cells * rows < LANES:
-            line = jnp.concatenate([line, jnp.zeros((1, LANES - cells * rows), jnp.float32)], axis=1)
+        if at == 0:
+            owner = keep[...] > 0.0
+            line = own[part, :, :, half:].reshape(cells * rows, half).T[:1]
+            if cells * rows < LANES:
+                line = jnp.concatenate([line, jnp.zeros((1, LANES - cells * rows), jnp.float32)], axis=1)
         for cell in range(cells):
-            mine, theirs = own[part, cell, :, :half], other[part, cell]
-            held[...] = mine + jnp.where((row == 0) & owner[:1], 0.0, theirs)
-            for at in range(plan.chunks):
-                for tile in range(tiles):
-                    four = held[pl.ds(at * chunk + tile, 4, stride=tiles), :]
-                    outs[at][cell, part, tile] = jnp.concatenate([four, four], axis=0)
-            partner = jnp.where(owner, theirs[:1], 0.0)
-            start = cell * rows
-            piece = line[:, start // LANES * LANES : start // LANES * LANES + LANES]
-            at_zero = pltpu.roll(piece, LANES - start % LANES, 1) if start % LANES else piece
-            outs[0][cell, part, tiles] = jnp.where(sub % 4 < 2, partner, jnp.where(lane < rows, at_zero, 0.0))
-
-
-def make_aims(plan, own, other, keep, step):
+            mine, theirs = own[part, cell, :chunk, :half], other[part, cell]
+            if at == 0:
+                held[...] = mine + jnp.where((row == 0) & owner[:1], 0.0, theirs)
+            else:
+                held[...] = mine + theirs
+            for tile in range(tiles):
+                four = held[pl.ds(tile, 4, stride=tiles), :]
+                out[cell, part, tile] = jnp.concatenate([four, four], axis=0)
+            if at == 0:
+                partner = jnp.where(owner, theirs[:1], 0.0)
+                start = cell * rows
+                piece = line[:, start // LANES * LANES : start // LANES * LANES + LANES]
+                at_zero = pltpu.roll(piece, LANES - start % LANES, 1) if start % LANES else piece
+                out[cell, part, tiles] = jnp.where(sub % 4 < 2, partner, jnp.where(lane < rows, at_zero, 0.0))
+
+
+def make_aims(plan, at, own, parts, keep, step):
     cells = 8
-    rows, half = plan.rows, plan.half
+    half, chunk = plan.half, plan.chunk
+    other = jnp.stack(parts)
     groups = other.shape[0]
     blocks = other.shape[2] // cells
     group = lax.axis_index("ba").astype(jnp.int32).reshape(1)
-
-    def sender(z, at):
-        return (lax.rem(at[0] + groups - z // blocks, groups), 0, z % blocks, 0, 0)
+    own_rows = plan.rows if at == 0 else chunk
+
+    def sender(z, me):
+        return (lax.rem(me[0] + groups - z // blocks, groups), 0, z % blocks, 0, 0)
 
     spec = pltpu.PrefetchScalarGridSpec(
         num_scalar_prefetch=1,
         grid=(plan.depth // cells,),
         in_specs=[
-            pl.BlockSpec((None, 2, cells, rows, plan.width), lambda z, at: (step, 0, z, 0, 0)),
-            pl.BlockSpec((None, 2, cells, rows, half), sender),
-            pl.BlockSpec(keep.shape, lambda z, at: (0, 0)),
+            pl.BlockSpec((None, 2, cells, own_rows, plan.width), lambda z, me: (step, 0, z, at, 0)),
+            pl.BlockSpec((None, 2, cells, chunk, half), sender),
+            pl.BlockSpec(keep.shape, lambda z, me: (0, 0)),
         ],
-        out_specs=[pl.BlockSpec((cells, 2, plan.steps(at), 8, LANES), lambda z, at: (z, 0, 0, 0, 0)) for at in range(plan.chunks)],
-        scratch_shapes=[pltpu.VMEM((rows, half), jnp.float32)],
+        out_specs=pl.BlockSpec((cells, 2, plan.steps(at), 8, LANES), lambda z, me: (z, 0, 0, 0, 0)),
+        scratch_shapes=[pltpu.VMEM((chunk, half), jnp.float32)],
     )
     return pl.pallas_call(
-        functools.partial(aims_kernel, plan),
+        functools.partial(aims_kernel, plan, at),
         grid_spec=spec,
-        out_shape=[jax.ShapeDtypeStruct((plan.depth, 2, plan.steps(at), 8, LANES), jnp.float32) for at in range(plan.chunks)],
+        out_shape=jax.ShapeDtypeStruct((plan.depth, 2, plan.steps(at), 8, LANES), jnp.float32),
         compiler_params=PARAMS,
-        cost_estimate=cost(8),
+        cost_estimate=cost(4),
         name="targets",
     )(group, own, other, keep)
 
@@ -641,20 +650,18 @@
     swapped = swap_targets(*flipped)
     starts = [tie(phi_start, *flipped), tie(phi_start, swapped)]
     sent = into(lambda side, held: first(plan, side, starts[side], consts, held))
-    spread = [spread_targets(swapped[step]) for step in range(steps)]
-    aims = [None] * steps
+    chunk_rows = [slice(at * plan.chunk, (at + 1) * plan.chunk) for at in range(plan.chunks)]
+    spread = [[spread_targets(swapped[step][:, :, held]) for held in chunk_rows] for step in range(steps)]
     for step in range(steps):
         modes, after = [], None
         for at in range(plan.chunks):
-            besides = spread[0][1 : 2 if at == 0 and plan.chunks > 1 else groups] if step == 0 else ()
-            modes.append(in_order(sent[at], after, besides))
+            modes.append(in_order(sent[at], after, spread[0][at] if step == 0 else ()))
             after = modes[at][-1]
-        if step == 0:
-            aims[0] = make_aims(plan, forward, jnp.stack(spread[0]), keep, 0)
+        back = []
         back = []
         for at in range(plan.chunks):
             inv = inverse[at]
-            common = (*modes[at], aims[step][at])
+            common = (*modes[at], make_aims(plan, at, forward, spread[step][at], keep, step))
             part0, part1, flux, sums, *extras = sweep(plan, at, False, groups, *common, inv[:, :6], couple, rate)
             collect(sums, 0)
             fluxes = [flux]
@@ -663,11 +670,9 @@
             rest = (part0, part1, *extras, share, keep, *fluxes)
             *new, sums = sweep(plan, at, True, groups, *common, inv[:, 6:], couple, rate, *rest)
             collect(sums, 1)
-            if step + 1 < steps and at == 0:
-                new[0] = tie(new[0], *spread[step + 1])
             if step + 1 < steps and at == plan.chunks - 1:
-                aims[step + 1] = make_aims(plan, forward, jnp.stack(spread[step + 1]), keep, step + 1)
-                new[0] = tie(new[0], *aims[step + 1])
+                for part, parts in enumerate(spread[step + 1]):
+                    new[part % len(new)] = tie(new[part % len(new)], *parts)
             back.append(in_order(new, back[-1][-1] if back else None))
         ends = [[pieces[side % len(pieces)] for pieces in back] for side in range(2)]
         if step + 1 < steps:

time: 549 us -> 519 us (0.945)
  blocking collectives: 93.1 us -> 62.2 us
  starting transfers between devices: 78.5 us -> 89 us
  Pallas kernels: 238 us -> 231 us
  waiting for transfers between devices: 108 us -> 101 us
    all_to_all x3 -> x2, blocking collectives: 93.1 us -> 62.2 us  [exchange(): return lax.all_to_all(array, 'gx', split_axis=0, concat_axis=0, tiled=True)]
    pallas_call x2 -> x4, Pallas kernels: 15.1 us -> 26.3 us  [make_aims(): pl.pallas_call(functools.partial(aims_kernel, plan, at), grid_spec=spec,...]
    pallas_call x4, Pallas kernels: 74.3 us -> 64.3 us  [send(): pl.pallas_call(functools.partial(kernel, plan, len(aliases)), grid=(plan....]
    ppermute x6 -> x12, starting transfers between devices: 10.6 us -> 19.5 us  [spread_targets(): lax.ppermute(turned, 'ba', [(i, (i + shift) % groups) for i in range(grou...]
    pallas_call x2, Pallas kernels: 32.4 us -> 23.7 us  [last(): pl.pallas_call(functools.partial(last_kernel, plan), grid=(plan.cells,),...]
    all_to_all x10 -> x11, starting transfers between devices: 42.5 us -> 50.4 us  [exchange(): return lax.all_to_all(array, 'gx', split_axis=0, concat_axis=0, tiled=True)]
    ppermute x12, starting transfers between devices: 20.7 us -> 14.3 us  [body(): lax.ppermute(flux, 'ba', [(i, (i + shift) % groups) for i in range(groups)])]
    all_to_all x10 -> x11, waiting for transfers between devices: 45.5 us -> 41.9 us  [exchange(): return lax.all_to_all(array, 'gx', split_axis=0, concat_axis=0, tiled=True)]
  transfers between devices with their start and end apart: 30 -> 37, of which waited for: 19 -> 24; matrix products, arithmetic and copies ran while one was open for 4% -> 5% of each run, Pallas kernels for 43% -> 44%
where the time goes in v3:
time: 519 us; the launch traced here: 516 us
  Pallas kernels  231 us (45%)
  waiting for transfers between devices  101 us (19%)
  starting transfers between devices  89 us (17%)
  blocking collectives  62.2 us (12%)
  local copies, waits for them, and re-layouts  17.4 us (3%)
  other arithmetic  14.6 us (3%)
    pallas_call x8, Pallas kernels, sweep(): pl.pallas_call(functools.partial(sweep_kernel, plan, at, upward, groups),...  111 us
    pallas_call x4, Pallas kernels, send(): pl.pallas_call(functools.partial(kernel, plan, len(aliases)), grid=(plan....  64.3 us
    all_to_all x2, blocking collectives, exchange(): return lax.all_to_all(array, 'gx', split_axis=0, concat_axis=0, tiled=True)  62.2 us
    all_to_all x11, starting transfers between devices, exchange(): return lax.all_to_all(array, 'gx', split_axis=0, concat_axis=0, tiled=True)  50.4 us
    all_to_all x11, waiting for transfers between devices, exchange(): return lax.all_to_all(array, 'gx', split_axis=0, concat_axis=0, tiled=True)  41.9 us
    ppermute x12, waiting for transfers between devices, spread_targets(): lax.ppermute(turned, 'ba', [(i, (i + shift) % groups) for i in range(grou...  36.5 us
    pallas_call x4, Pallas kernels, make_aims(): pl.pallas_call(functools.partial(aims_kernel, plan, at), grid_spec=spec,...  26.3 us
    pallas_call x2, Pallas kernels, last(): pl.pallas_call(functools.partial(last_kernel, plan), grid=(plan.cells,),...  23.7 us
  transfers between devices with their start and end apart: 37, of which 24 were waited for; matrix products, arithmetic and copies ran while one was open for 5% of the time, Pallas kernels for 44%

profile of v3, /device:TPU:0, one launch (start us, length us, event | category | flops | bytes accessed | tf_op | source)
XLA Modules:
  0.0 516.3 jit_solution(9173604566550174492)
XLA Ops:
  0.6 4.9 mirrored.1
  5.6 3.3 collective-permute-start.1
  10.3 12.0 %into_modes.2 = (f32[8,520,128]{2,1,0:T(8,128)}, f32[8,1024,128]{2,1,0:T(8,128)}) custom-call(f32[8,4,256,256]{3,2,1,0:T(8,128)} %phi.1, bf16[256,256]{1,0:T(8,128)(2,1)} %constant.161.clone.into_h.refs_3_, bf16[256,256]{1,0:T(8,128)(2,1)} %constant.162.clone.into_l.refs_4_, bf16[512,256]{1,0:T(8,128)(2,1)} %constant.163.clone.stacked_h.refs_5_, ...), custom_call_target="tpu_custom_call" | custom-call | bytes 44280000 | tf_op jit(solution)/shard_map/into_modes/pallas_call | solution.py:244
  22.3 4.9 all-to-all-start
  28.8 4.0 collective-permute-done.1
  33.9 2.3 collective-permute-start.2
  36.3 2.6 collective-permute-start.3
  42.2 12.1 %into_modes.3 = (f32[8,520,128]{2,1,0:T(8,128)}, f32[8,1024,128]{2,1,0:T(8,128)}) custom-call(f32[8,4,256,256]{3,2,1,0:T(8,128)} %phi.1, bf16[256,256]{1,0:T(8,128)(2,1)} %constant.161.clone.into_h.refs_3_, bf16[256,256]{1,0:T(8,128)(2,1)} %constant.162.clone.into_l.refs_4_, ...), custom_call_target="tpu_custom_call", output_to_operand_aliasing={{1}: (5, {})} | custom-call | bytes 44280000 | tf_op jit(solution)/shard_map/into_modes/pallas_call | solution.py:244
  54.3 2.6 collective-permute-done.3
  58.2 7.8 %all-to-all-start.1 = ((f32[8,520,128]{2,1,0:T(8,128)}), f32[8,520,128]{2,1,0:T(8,128)}, u32[]{:S(2)}, u32[]{:S(2)}) async-start(f32[8,520,128]{2,1,0:T(8,128)} %get-tuple-element.60), calls=%async_computation.1 | async-start | bytes 4259840 | tf_op jit(solution)/shard_map/all_to_all | solution.py:622
  66.5 2.7 collective-permute-start.8
  69.3 1.6 collective-permute-start.9
  72.2 5.4 %collective-permute-done.8 = f32[2,16,16,128]{3,2,1,0:T(8,128)S(1)} collective-permute-done((f32[2,16,16,128]{3,2,1,0:T(8,128)S(1)}, f32[2,16,16,128]{3,2,1,0:T(8,128)S(1)}, u32[]{:S(2)}, u32[]{:S(2)}) %collective-permute-start.8) | collective-permute-done | bytes 262176 | tf_op jit(solution)/shard_map/ppermute | solution.py:618
  77.6 10.8 %collective-permute-done.9 = f32[2,16,16,128]{3,2,1,0:T(8,128)S(1)} collective-permute-done((f32[2,16,16,128]{3,2,1,0:T(8,128)S(1)}, f32[2,16,16,128]{3,2,1,0:T(8,128)S(1)}, u32[]{:S(2)}, u32[]{:S(2)}) %collective-permute-start.9) | collective-permute-done | bytes 262176 | tf_op jit(solution)/shard_map/ppermute | solution.py:618
  88.5 4.7 all-to-all-done.1.refs_1_
  93.1 4.7 all-to-all-start.3
  101.6 2.2 pad_maximum_fusion.other
  104.3 7.0 %targets.4.refs_2_ = f32[64,2,5,8,128]{4,3,2,1,0:T(8,128)} custom-call(s32[1]{0:T(128)} %bitcast.group, f32[2,2,64,32,256]{4,3,2,1,0:T(8,128)} %own.7, f32[4,2,16,16,128]{4,3,2,1,0:T(8,128)} %pad_maximum_fusion.other, f32[8,128]{1,0:T(8,128)} %broadcast_in_dim.180.keep.refs_10_.refs_8_), custom_call_target="tpu_custom_call" | custom-call | bytes 14760000 | tf_op jit(solution)/shard_map/targets/pallas_call | solution.py:546
  112.0 14.3 %downward.4 = (f32[8,520,128]{2,1,0:T(8,128)}, f32[8,520,128]{2,1,0:T(8,128)}, f32[2,5,8,128]{3,2,1,0:T(8,128)}, f32[3,6,64,8]{3,2,1,0:T(8,128)}, f32[64,2,8,128]{3,2,1,0:T(8,128)}) custom-call(f32[8,520,128]{2,1,0:T(8,128)} %copy-done, f32[8,520,128]{2,1,0:T(8,128)} %all-to-all-done.1.refs_1_, f32[64,2,5,8,128]{4,3,2,1,0:T(8,128)} %targets.4.refs_2_, ...), custom_call_target="tpu_custom_call" | custom-call | bytes 47970000 | tf_op jit(solution)/shard_map/downward/pallas_call | solution.py:429
  126.3 2.6 collective-permute-start.5
  128.9 1.6 collective-permute-start.6
  132.3 2.1 collective-permute-done.6.refs_13_
  135.5 16.4 %upward.4 = (f32[8,1040,128]{2,1,0:T(8,128)}, f32[3,6,64,8]{3,2,1,0:T(8,128)}) custom-call(f32[8,520,128]{2,1,0:T(8,128)} %copy-done, f32[8,520,128]{2,1,0:T(8,128)} %all-to-all-done.1.refs_1_, f32[64,2,5,8,128]{4,3,2,1,0:T(8,128)} %targets.4.refs_2_, f32[2,6,9,8,128]{4,3,2,1,0:T(8,128)} %get-tuple-element.111.refs_3_, ...), custom_call_target="tpu_custom_call" | custom-call | bytes 47970000 | tf_op jit(solution)/shard_map/upward/pallas_call | solution.py:429
  151.8 4.6 all-to-all-start.2
  158.3 2.3 collective-permute-start.15
  163.7 6.2 %targets.5.refs_1_ = f32[64,2,4,8,128]{4,3,2,1,0:T(8,128)} custom-call(s32[1]{0:T(128)} %bitcast.group, f32[2,2,64,32,256]{4,3,2,1,0:T(8,128)} %own.7, f32[4,2,16,16,128]{4,3,2,1,0:T(8,128)} %pad_maximum_fusion.1.other, f32[8,128]{1,0:T(8,128)} %broadcast_in_dim.180.keep.refs_10_.refs_8_), custom_call_target="tpu_custom_call" | custom-call | bytes 14760000 | tf_op jit(solution)/shard_map/targets/pallas_call | solution.py:546
  169.9 11.8 %downward.5 = (f32[8,512,128]{2,1,0:T(8,128)}, f32[8,512,128]{2,1,0:T(8,128)}, f32[2,4,8,128]{3,2,1,0:T(8,128)}, f32[2,6,64,8]{3,2,1,0:T(8,128)}) custom-call(f32[8,1024,128]{2,1,0:T(8,128)} %all-to-all-done.3.refs_0_, f32[64,2,4,8,128]{4,3,2,1,0:T(8,128)} %targets.5.refs_1_, f32[2,6,8,8,128]{4,3,2,1,0:T(8,128)} %get-tuple-element.112.refs_2_, ...), custom_call_target="tpu_custom_call" | custom-call | bytes 47970000 | tf_op jit(solution)/shard_map/downward/pallas_call | solution.py:429
  183.4 4.3 collective-permute-done.11.refs_10_
  188.6 3.2 collective-permute-done.13.refs_12_
  192.4 13.2 %upward.5 = (f32[8,512,128]{2,1,0:T(8,128)}, f32[8,512,128]{2,1,0:T(8,128)}, f32[2,6,64,8]{3,2,1,0:T(8,128)}) custom-call(f32[8,1024,128]{2,1,0:T(8,128)} %all-to-all-done.3.refs_0_, f32[64,2,4,8,128]{4,3,2,1,0:T(8,128)} %targets.5.refs_1_, f32[2,6,8,8,128]{4,3,2,1,0:T(8,128)} %get-tuple-element.113.refs_2_, ...), custom_call_target="tpu_custom_call" | custom-call | bytes 47970000 | tf_op jit(solution)/shard_map/upward/pallas_call | solution.py:429
  206.4 4.1 all-to-all-start.4
  210.7 2.3 collective-permute-start.18
  212.9 1.4 collective-permute-start.19
  214.4 7.2 %collective-permute-done.17 = f32[2,16,16,128]{3,2,1,0:T(8,128)S(1)} collective-permute-done((f32[2,16,16,128]{3,2,1,0:T(8,128)S(1)}, f32[2,16,16,128]{3,2,1,0:T(8,128)S(1)}, u32[]{:S(2)}, u32[]{:S(2)}) %collective-permute-start.17) | collective-permute-done | bytes 262176 | tf_op jit(solution)/shard_map/ppermute | solution.py:618
  221.6 10.4 %collective-permute-done.18 = f32[2,16,16,128]{3,2,1,0:T(8,128)S(1)} collective-permute-done((f32[2,16,16,128]{3,2,1,0:T(8,128)S(1)}, f32[2,16,16,128]{3,2,1,0:T(8,128)S(1)}, u32[]{:S(2)}, u32[]{:S(2)}) %collective-permute-start.18) | collective-permute-done | bytes 262176 | tf_op jit(solution)/shard_map/ppermute | solution.py:618
  233.4 3.7 all-to-all-done.4.refs_1_
  237.1 4.3 all-to-all-start.6
  241.5 20.1 %between_steps.2 = (f32[8,520,128]{2,1,0:T(8,128)}, f32[8,1024,128]{2,1,0:T(8,128)}) custom-call(f32[8,1040,128]{2,1,0:T(8,128)} %all-to-all-done.2.refs_0_, f32[8,512,128]{2,1,0:T(8,128)} %copy-done.3, f32[8,256,256]{2,1,0:T(8,128)} %refs_2_.7, bf16[256,256]{1,0:T(8,128)(2,1)} %constant.161.clone.into_h.refs_3_, ...), custom_call_target="tpu_custom_call" | custom-call | bytes 92250000 | tf_op jit(solution)/shard_map/between_steps/pallas_call | solution.py:244
  261.6 6.6 %all-to-all-done.6.refs_1_ = f32[8,512,128]{2,1,0:T(8,128)} async-done(((f32[8,512,128]{2,1,0:T(8,128)}), f32[8,512,128]{2,1,0:T(8,128)}, u32[]{:S(2)}, u32[]{:S(2)}) %all-to-all-start.6) | async-done | bytes 2097184 | tf_op jit(solution)/shard_map/all_to_all | solution.py:622
  268.2 3.6 all-to-all-start.5
  271.8 20.1 %between_steps.3 = (f32[8,520,128]{2,1,0:T(8,128)}, f32[8,1024,128]{2,1,0:T(8,128)}) custom-call(f32[8,1040,128]{2,1,0:T(8,128)} %all-to-all-done.2.refs_0_, f32[8,512,128]{2,1,0:T(8,128)} %all-to-all-done.6.refs_1_, f32[8,256,256]{2,1,0:T(8,128)} %refs_2_.7, bf16[256,256]{1,0:T(8,128)(2,1)} %constant.161.clone.into_h.refs_3_, ...), custom_call_target="tpu_custom_call", output_to_operand_aliasing={{1}: (11, {})} | custom-call | bytes 92250000 | tf_op jit(solution)/shard_map/between_steps/pallas_call | solution.py:244
  291.9 6.8 %all-to-all-done.5.refs_0_ = f32[8,520,128]{2,1,0:T(8,128)S(1)} async-done(((f32[8,520,128]{2,1,0:T(8,128)}), f32[8,520,128]{2,1,0:T(8,128)S(1)}, u32[]{:S(2)}, u32[]{:S(2)}) %all-to-all-start.5) | async-done | bytes 2129952 | tf_op jit(solution)/shard_map/all_to_all | solution.py:622
  298.7 31.3 %all_to_all.69.refs_1_ = f32[8,520,128]{2,1,0:T(8,128)} all-to-all(f32[8,520,128]{2,1,0:T(8,128)} %get-tuple-element.80), channel_id=1, replica_groups=mesh['gx'=8,'ba'=4] {'gx'}, dimensions={0} | all-to-all | bytes 4259840 | tf_op jit(solution)/shard_map/all_to_all | solution.py:622
  330.0 4.7 all-to-all-start.9
  335.8 7.0 %targets.6.refs_2_ = f32[64,2,5,8,128]{4,3,2,1,0:T(8,128)} custom-call(s32[1]{0:T(128)} %bitcast.group, f32[2,2,64,32,256]{4,3,2,1,0:T(8,128)} %own.7, f32[4,2,16,16,128]{4,3,2,1,0:T(8,128)} %pad_maximum_fusion.2.other, f32[8,128]{1,0:T(8,128)} %broadcast_in_dim.180.keep.refs_10_.refs_8_), custom_call_target="tpu_custom_call" | custom-call | bytes 14760000 | tf_op jit(solution)/shard_map/targets/pallas_call | solution.py:546
  342.8 14.3 %downward.6 = (f32[8,520,128]{2,1,0:T(8,128)}, f32[8,520,128]{2,1,0:T(8,128)}, f32[2,5,8,128]{3,2,1,0:T(8,128)}, f32[3,6,64,8]{3,2,1,0:T(8,128)}, f32[64,2,8,128]{3,2,1,0:T(8,128)}) custom-call(f32[8,520,128]{2,1,0:T(8,128)} %copy-done.1, f32[8,520,128]{2,1,0:T(8,128)} %all_to_all.69.refs_1_, f32[64,2,5,8,128]{4,3,2,1,0:T(8,128)} %targets.6.refs_2_, ...), custom_call_target="tpu_custom_call" | custom-call | bytes 47970000 | tf_op jit(solution)/shard_map/downward/pallas_call | solution.py:429
  359.5 1.5 collective-permute-start.22
  360.9 2.6 collective-permute-done.20.refs_12_
  365.4 16.4 %upward.6 = (f32[8,1040,128]{2,1,0:T(8,128)}, f32[3,6,64,8]{3,2,1,0:T(8,128)}) custom-call(f32[8,520,128]{2,1,0:T(8,128)} %copy-done.1, f32[8,520,128]{2,1,0:T(8,128)} %all_to_all.69.refs_1_, f32[64,2,5,8,128]{4,3,2,1,0:T(8,128)} %targets.6.refs_2_, f32[2,6,9,8,128]{4,3,2,1,0:T(8,128)} %get-tuple-element.111.refs_3_, ...), custom_call_target="tpu_custom_call" | custom-call | bytes 47970000 | tf_op jit(solution)/shard_map/upward/pallas_call | solution.py:429
  381.8 2.0 all-to-all-done.9.refs_0_
  383.8 4.7 all-to-all-start.8
  389.6 6.2 %targets.7.refs_1_ = f32[64,2,4,8,128]{4,3,2,1,0:T(8,128)} custom-call(s32[1]{0:T(128)} %bitcast.group, f32[2,2,64,32,256]{4,3,2,1,0:T(8,128)} %own.7, f32[4,2,16,16,128]{4,3,2,1,0:T(8,128)} %pad_maximum_fusion.3.other, f32[8,128]{1,0:T(8,128)} %broadcast_in_dim.180.keep.refs_10_.refs_8_), custom_call_target="tpu_custom_call" | custom-call | bytes 14760000 | tf_op jit(solution)/shard_map/targets/pallas_call | solution.py:546
  395.8 11.8 %downward.7 = (f32[8,512,128]{2,1,0:T(8,128)}, f32[8,512,128]{2,1,0:T(8,128)}, f32[2,4,8,128]{3,2,1,0:T(8,128)}, f32[2,6,64,8]{3,2,1,0:T(8,128)}) custom-call(f32[8,1024,128]{2,1,0:T(8,128)} %all-to-all-done.9.refs_0_, f32[64,2,4,8,128]{4,3,2,1,0:T(8,128)} %targets.7.refs_1_, f32[2,6,8,8,128]{4,3,2,1,0:T(8,128)} %get-tuple-element.112.refs_2_, ...), custom_call_target="tpu_custom_call" | custom-call | bytes 47970000 | tf_op jit(solution)/shard_map/downward/pallas_call | solution.py:429
  410.0 1.5 collective-permute-start.25
  411.5 2.3 collective-permute-done.23.refs_10_
  415.4 13.1 %upward.7 = (f32[8,512,128]{2,1,0:T(8,128)}, f32[8,512,128]{2,1,0:T(8,128)}, f32[2,6,64,8]{3,2,1,0:T(8,128)}) custom-call(f32[8,1024,128]{2,1,0:T(8,128)} %all-to-all-done.9.refs_0_, f32[64,2,4,8,128]{4,3,2,1,0:T(8,128)} %targets.7.refs_1_, f32[2,6,8,8,128]{4,3,2,1,0:T(8,128)} %get-tuple-element.113.refs_2_, ...), custom_call_target="tpu_custom_call" | custom-call | bytes 47970000 | tf_op jit(solution)/shard_map/upward/pallas_call | solution.py:429
  428.6 9.8 %all-to-all-done.8.refs_0_ = f32[8,1040,128]{2,1,0:T(8,128)} async-done(((f32[8,1040,128]{2,1,0:T(8,128)}), f32[8,1040,128]{2,1,0:T(8,128)}, u32[]{:S(2)}, u32[]{:S(2)}) %all-to-all-start.8) | async-done | bytes 4259872 | tf_op jit(solution)/shard_map/all_to_all | solution.py:622
  438.3 30.9 %all_to_all.70.refs_1_ = f32[8,512,128]{2,1,0:T(8,128)} all-to-all(f32[8,512,128]{2,1,0:T(8,128)} %get-tuple-element.93), channel_id=1, replica_groups=mesh['gx'=8,'ba'=4] {'gx'}, dimensions={0} | all-to-all | bytes 4194304 | tf_op jit(solution)/shard_map/all_to_all | solution.py:622
  469.3 3.7 all-to-all-start.11
  476.7 1.4 add_add_fusion
  480.0 11.8 %out_of_modes.2.refs_7_ = f32[8,4,256,256]{3,2,1,0:T(8,128)} custom-call(f32[8,1040,128]{2,1,0:T(8,128)} %all-to-all-done.8.refs_0_, f32[8,512,128]{2,1,0:T(8,128)} %all_to_all.70.refs_1_, f32[8,256,256]{2,1,0:T(8,128)} %refs_2_.7, bf16[256,512]{1,0:T(8,128)(2,1)} %constant.165.clone.refs_7_.refs_3_, bf16[256,512]{1,0:T(8,128)(2,1)} %constant.166.clone.refs_8_.refs_4_, ...), custom_call_target="tpu_custom_call" | custom-call | bytes 59040000 | tf_op jit(solution)/shard_map/out_of_modes/pallas_call | solution.py:277
  491.8 7.8 %all-to-all-done.11.refs_1_ = f32[8,512,128]{2,1,0:T(8,128)S(1)} async-done(((f32[8,512,128]{2,1,0:T(8,128)}), f32[8,512,128]{2,1,0:T(8,128)S(1)}, u32[]{:S(2)}, u32[]{:S(2)}) %all-to-all-start.11) | async-done | bytes 2097184 | tf_op jit(solution)/shard_map/all_to_all | solution.py:622
  500.3 3.3 all-to-all-start.12
  503.6 11.8 %out_of_modes.3 = f32[8,4,256,256]{3,2,1,0:T(8,128)} custom-call(f32[8,1040,128]{2,1,0:T(8,128)} %all-to-all-done.8.refs_0_, f32[8,512,128]{2,1,0:T(8,128)} %copy-done.2, f32[8,256,256]{2,1,0:T(8,128)} %refs_2_.7, bf16[256,512]{1,0:T(8,128)(2,1)} %constant.165.clone.refs_7_.refs_3_, ...), custom_call_target="tpu_custom_call", output_to_operand_aliasing={{}: (7, {})} | custom-call | bytes 59040000 | tf_op jit(solution)/shard_map/out_of_modes/pallas_call | solution.py:277
  (217 shorter events, 46.6 us)
Async XLA Ops:
  5.6 27.2 %collective-permute-start.1 = (f32[2,2,16,32,128]{4,3,2,1,0:T(8,128)}, f32[2,2,16,32,128]{4,3,2,1,0:T(8,128)S(1)}, u32[]{:S(2)}, u32[]{:S(2)}) collective-permute-start(f32[2,2,16,32,128]{4,3,2,1,0:T(8,128)} %get-tuple-element.53), channel_id=1, source_target_pairs={{0,28},{4,24},{8,20},{12,16},{16,12},{20,8},{24,4},{28,0},{1,29},{... | collective-permute-start | bytes 3145736 | tf_op jit(solution)/shard_map/ppermute | solution.py:611
  8.9 19.9 %collective-permute-start = (f32[2,2,16,128]{3,2,1,0:T(8,128)}, f32[2,2,16,128]{3,2,1,0:T(8,128)S(1)}, u32[]{:S(2)}, u32[]{:S(2)}) collective-permute-start(f32[2,2,16,128]{3,2,1,0:T(8,128)} %get-tuple-element.54), channel_id=1, source_target_pairs={{0,0},{4,28},{8,24},{12,20},{16,16},{20,12},{24,8},{28,4},{1,1},{5... | collective-permute-start | bytes 98312 | tf_op jit(solution)/shard_map/ppermute | solution.py:612
  22.3 4.9 copy-start.29
  22.3 6.2 %copy-start.30 = (f32[4]{0:T(128)S(1)}, f32[4]{0:T(128)}, u32[]{:S(2)}) copy-start(f32[4]{0:T(128)} %param.26) | copy-start | bytes 52
  22.3 34.6 %all-to-all-start = ((f32[8,520,128]{2,1,0:T(8,128)}), f32[8,520,128]{2,1,0:T(8,128)S(1)}, u32[]{:S(2)}, u32[]{:S(2)}) async-start(f32[8,520,128]{2,1,0:T(8,128)} %get-tuple-element.56), calls=%async_computation | async-start | bytes 4259840 | tf_op jit(solution)/shard_map/all_to_all | solution.py:622
  33.9 20.4 %collective-permute-start.2 = (f32[2,16,16,128]{3,2,1,0:T(8,128)}, f32[2,16,16,128]{3,2,1,0:T(8,128)}, u32[]{:S(2)}, u32[]{:S(2)}) collective-permute-start(f32[2,16,16,128]{3,2,1,0:T(8,128)} %get-tuple-element.121), channel_id=1, source_target_pairs={{0,1},{1,2},{2,3},{3,0},{4,5},{5,6},{6,7},{7,4},{8,9},{9,10},{10,1... | collective-permute-start | bytes 786440 | tf_op jit(solution)/shard_map/ppermute | solution.py:618
  36.3 20.6 %collective-permute-start.3 = (f32[2,16,16,128]{3,2,1,0:T(8,128)}, f32[2,16,16,128]{3,2,1,0:T(8,128)}, u32[]{:S(2)}, u32[]{:S(2)}) collective-permute-start(f32[2,16,16,128]{3,2,1,0:T(8,128)} %get-tuple-element.121), channel_id=1, source_target_pairs={{0,2},{1,3},{2,0},{3,1},{4,6},{5,7},{6,4},{7,5},{8,10},{9,11},{10,... | collective-permute-start | bytes 786440 | tf_op jit(solution)/shard_map/ppermute | solution.py:618
  38.9 18.0 %collective-permute-start.4 = (f32[2,16,16,128]{3,2,1,0:T(8,128)}, f32[2,16,16,128]{3,2,1,0:T(8,128)}, u32[]{:S(2)}, u32[]{:S(2)}) collective-permute-start(f32[2,16,16,128]{3,2,1,0:T(8,128)} %get-tuple-element.121), channel_id=1, source_target_pairs={{0,3},{1,0},{2,1},{3,2},{4,7},{5,4},{6,5},{7,6},{8,11},{9,8},{10,9... | collective-permute-start | bytes 786440 | tf_op jit(solution)/shard_map/ppermute | solution.py:618
  56.9 1.3 copy-start
  56.9 9.5 %copy-start.35 = (s32[4]{0:T(128)S(1)}, s32[4]{0:T(128)}, u32[]{:S(2)}) copy-start(s32[4]{0:T(128)} %iota_add_fusion) | copy-start | bytes 52
  58.2 34.9 %all-to-all-start.1 = ((f32[8,520,128]{2,1,0:T(8,128)}), f32[8,520,128]{2,1,0:T(8,128)}, u32[]{:S(2)}, u32[]{:S(2)}) async-start(f32[8,520,128]{2,1,0:T(8,128)} %get-tuple-element.60), calls=%async_computation.1 | async-start | bytes 4259840 | tf_op jit(solution)/shard_map/all_to_all | solution.py:622
  66.5 11.1 %collective-permute-start.8 = (f32[2,16,16,128]{3,2,1,0:T(8,128)S(1)}, f32[2,16,16,128]{3,2,1,0:T(8,128)S(1)}, u32[]{:S(2)}, u32[]{:S(2)}) collective-permute-start(f32[2,16,16,128]{3,2,1,0:T(8,128)S(1)} %get-tuple-element.120), channel_id=1, source_target_pairs={{0,1},{1,2},{2,3},{3,0},{4,5},{5,6},{6,7},{7,4},{8,9},{9,10},{10,1... | collective-permute-start | bytes 786440 | tf_op jit(solution)/shard_map/ppermute | solution.py:618
  69.3 19.2 %collective-permute-start.9 = (f32[2,16,16,128]{3,2,1,0:T(8,128)S(1)}, f32[2,16,16,128]{3,2,1,0:T(8,128)S(1)}, u32[]{:S(2)}, u32[]{:S(2)}) collective-permute-start(f32[2,16,16,128]{3,2,1,0:T(8,128)S(1)} %get-tuple-element.120), channel_id=1, source_target_pairs={{0,2},{1,3},{2,0},{3,1},{4,6},{5,7},{6,4},{7,5},{8,10},{9,11},{10,... | collective-permute-start | bytes 786440 | tf_op jit(solution)/shard_map/ppermute | solution.py:618
  70.8 17.6 %collective-permute-start.10 = (f32[2,16,16,128]{3,2,1,0:T(8,128)S(1)}, f32[2,16,16,128]{3,2,1,0:T(8,128)S(1)}, u32[]{:S(2)}, u32[]{:S(2)}) collective-permute-start(f32[2,16,16,128]{3,2,1,0:T(8,128)S(1)} %get-tuple-element.120), channel_id=1, source_target_pairs={{0,3},{1,0},{2,1},{3,2},{4,7},{5,4},{6,5},{7,6},{8,11},{9,8},{10,9... | collective-permute-start | bytes 786440 | tf_op jit(solution)/shard_map/ppermute | solution.py:618
  93.1 5.1 copy-start.36
  93.1 6.5 %copy-start.31 = (f32[12]{0:T(128)S(1)}, f32[12]{0:T(128)}, u32[]{:S(2)}) copy-start(f32[12]{0:T(128)} %constant.177) | copy-start | bytes 148
  93.1 6.5 %copy-start.32 = (f32[12]{0:T(128)S(1)}, f32[12]{0:T(128)}, u32[]{:S(2)}) copy-start(f32[12]{0:T(128)} %constant.176) | copy-start | bytes 148
  93.1 6.5 %copy-start.33 = (f32[12]{0:T(128)S(1)}, f32[12]{0:T(128)}, u32[]{:S(2)}) copy-start(f32[12]{0:T(128)} %constant.175) | copy-start | bytes 148
  93.1 58.7 %all-to-all-start.3 = ((f32[8,1024,128]{2,1,0:T(8,128)}), f32[8,1024,128]{2,1,0:T(8,128)}, u32[]{:S(2)}, u32[]{:S(2)}) async-start(f32[8,1024,128]{2,1,0:T(8,128)} %get-tuple-element.67), calls=%async_computation.3 | async-start | bytes 8388608 | tf_op jit(solution)/shard_map/all_to_all | solution.py:622
  97.9 3.0 copy-start.34
  126.3 6.0 %collective-permute-start.5 = (f32[2,5,8,128]{3,2,1,0:T(8,128)}, f32[2,5,8,128]{3,2,1,0:T(8,128)S(1)}, u32[]{:S(2)}, u32[]{:S(2)}) collective-permute-start(f32[2,5,8,128]{3,2,1,0:T(8,128)} %get-tuple-element.64.refs_11_), channel_id=1, source_target_pairs={{0,1},{1,2},{2,3},{3,0},{4,5},{5,6},{6,7},{7,4},{8,9},{9,10},{10,1... | collective-permute-start | bytes 122888 | tf_op jit(solution)/shard_map/ppermute | solution.py:669
  128.9 5.6 %collective-permute-start.6 = (f32[2,5,8,128]{3,2,1,0:T(8,128)}, f32[2,5,8,128]{3,2,1,0:T(8,128)S(1)}, u32[]{:S(2)}, u32[]{:S(2)}) collective-permute-start(f32[2,5,8,128]{3,2,1,0:T(8,128)} %get-tuple-element.64.refs_11_), channel_id=1, source_target_pairs={{0,2},{1,3},{2,0},{3,1},{4,6},{5,7},{6,4},{7,5},{8,10},{9,11},{10,... | collective-permute-start | bytes 122888 | tf_op jit(solution)/shard_map/ppermute | solution.py:669
  130.5 4.3 collective-permute-start.7
  132.3 3.1 copy-start.17
  134.4 1.0 copy-start.18
  151.8 54.4 %all-to-all-start.2 = ((f32[8,1040,128]{2,1,0:T(8,128)}), f32[8,1040,128]{2,1,0:T(8,128)}, u32[]{:S(2)}, u32[]{:S(2)}) async-start(f32[8,1040,128]{2,1,0:T(8,128)} %get-tuple-element.65), calls=%async_computation.2 | async-start | bytes 8519680 | tf_op jit(solution)/shard_map/all_to_all | solution.py:622
  157.5 48.1 %collective-permute-start.14 = (f32[2,16,16,128]{3,2,1,0:T(8,128)S(1)}, f32[2,16,16,128]{3,2,1,0:T(8,128)S(1)}, u32[]{:S(2)}, u32[]{:S(2)}) collective-permute-start(f32[2,16,16,128]{3,2,1,0:T(8,128)S(1)} %get-tuple-element.117), channel_id=1, source_target_pairs={{0,1},{1,2},{2,3},{3,0},{4,5},{5,6},{6,7},{7,4},{8,9},{9,10},{10,1... | collective-permute-start | bytes 786440 | tf_op jit(solution)/shard_map/ppermute | solution.py:618
  158.3 47.3 %collective-permute-start.15 = (f32[2,16,16,128]{3,2,1,0:T(8,128)S(1)}, f32[2,16,16,128]{3,2,1,0:T(8,128)S(1)}, u32[]{:S(2)}, u32[]{:S(2)}) collective-permute-start(f32[2,16,16,128]{3,2,1,0:T(8,128)S(1)} %get-tuple-element.117), channel_id=1, source_target_pairs={{0,2},{1,3},{2,0},{3,1},{4,6},{5,7},{6,4},{7,5},{8,10},{9,11},{10,... | collective-permute-start | bytes 786440 | tf_op jit(solution)/shard_map/ppermute | solution.py:618
  160.5 45.1 %collective-permute-start.16 = (f32[2,16,16,128]{3,2,1,0:T(8,128)S(1)}, f32[2,16,16,128]{3,2,1,0:T(8,128)S(1)}, u32[]{:S(2)}, u32[]{:S(2)}) collective-permute-start(f32[2,16,16,128]{3,2,1,0:T(8,128)S(1)} %get-tuple-element.117), channel_id=1, source_target_pairs={{0,3},{1,0},{2,1},{3,2},{4,7},{5,4},{6,5},{7,6},{8,11},{9,8},{10,9... | collective-permute-start | bytes 786440 | tf_op jit(solution)/shard_map/ppermute | solution.py:618
  181.7 6.0 %collective-permute-start.11 = (f32[2,4,8,128]{3,2,1,0:T(8,128)}, f32[2,4,8,128]{3,2,1,0:T(8,128)S(1)}, u32[]{:S(2)}, u32[]{:S(2)}) collective-permute-start(f32[2,4,8,128]{3,2,1,0:T(8,128)} %get-tuple-element.70.refs_9_), channel_id=1, source_target_pairs={{0,1},{1,2},{2,3},{3,0},{4,5},{5,6},{6,7},{7,4},{8,9},{9,10},{10,1... | collective-permute-start | bytes 98312 | tf_op jit(solution)/shard_map/ppermute | solution.py:669
  182.6 6.0 %collective-permute-start.12 = (f32[2,4,8,128]{3,2,1,0:T(8,128)}, f32[2,4,8,128]{3,2,1,0:T(8,128)S(1)}, u32[]{:S(2)}, u32[]{:S(2)}) collective-permute-start(f32[2,4,8,128]{3,2,1,0:T(8,128)} %get-tuple-element.70.refs_9_), channel_id=1, source_target_pairs={{0,2},{1,3},{2,0},{3,1},{4,6},{5,7},{6,4},{7,5},{8,10},{9,11},{10,... | collective-permute-start | bytes 98312 | tf_op jit(solution)/shard_map/ppermute | solution.py:669
  187.7 4.1 copy-start.25
  187.7 4.1 collective-permute-start.13
  188.6 3.2 copy-start.27
  205.6 4.9 copy-start.6
  206.4 30.7 %all-to-all-start.4 = ((f32[8,512,128]{2,1,0:T(8,128)}), f32[8,512,128]{2,1,0:T(8,128)S(1)}, u32[]{:S(2)}, u32[]{:S(2)}) async-start(f32[8,512,128]{2,1,0:T(8,128)} %get-tuple-element.73), calls=%async_computation.4 | async-start | bytes 4194304 | tf_op jit(solution)/shard_map/all_to_all | solution.py:622
  210.5 11.1 %collective-permute-start.17 = (f32[2,16,16,128]{3,2,1,0:T(8,128)S(1)}, f32[2,16,16,128]{3,2,1,0:T(8,128)S(1)}, u32[]{:S(2)}, u32[]{:S(2)}) collective-permute-start(f32[2,16,16,128]{3,2,1,0:T(8,128)S(1)} %copy-done.6), channel_id=1, source_target_pairs={{0,1},{1,2},{2,3},{3,0},{4,5},{5,6},{6,7},{7,4},{8,9},{9,10},{10,1... | collective-permute-start | bytes 786440 | tf_op jit(solution)/shard_map/ppermute | solution.py:618
  210.7 21.3 %collective-permute-start.18 = (f32[2,16,16,128]{3,2,1,0:T(8,128)S(1)}, f32[2,16,16,128]{3,2,1,0:T(8,128)S(1)}, u32[]{:S(2)}, u32[]{:S(2)}) collective-permute-start(f32[2,16,16,128]{3,2,1,0:T(8,128)S(1)} %copy-done.6), channel_id=1, source_target_pairs={{0,2},{1,3},{2,0},{3,1},{4,6},{5,7},{6,4},{7,5},{8,10},{9,11},{10,... | collective-permute-start | bytes 786440 | tf_op jit(solution)/shard_map/ppermute | solution.py:618
  212.9 19.1 %collective-permute-start.19 = (f32[2,16,16,128]{3,2,1,0:T(8,128)S(1)}, f32[2,16,16,128]{3,2,1,0:T(8,128)S(1)}, u32[]{:S(2)}, u32[]{:S(2)}) collective-permute-start(f32[2,16,16,128]{3,2,1,0:T(8,128)S(1)} %copy-done.6), channel_id=1, source_target_pairs={{0,3},{1,0},{2,1},{3,2},{4,7},{5,4},{6,5},{7,6},{8,11},{9,8},{10,9... | collective-permute-start | bytes 786440 | tf_op jit(solution)/shard_map/ppermute | solution.py:618
  221.6 40.0 %copy-start.11 = (f32[2,16,16,128]{3,2,1,0:T(8,128)}, f32[2,16,16,128]{3,2,1,0:T(8,128)S(1)}, u32[]{:S(2)}) copy-start(f32[2,16,16,128]{3,2,1,0:T(8,128)S(1)} %collective-permute-done.17) | copy-start | bytes 786436
  237.1 4.4 copy-start.3
  237.1 31.0 %all-to-all-start.6 = ((f32[8,512,128]{2,1,0:T(8,128)}), f32[8,512,128]{2,1,0:T(8,128)}, u32[]{:S(2)}, u32[]{:S(2)}) async-start(f32[8,512,128]{2,1,0:T(8,128)} %get-tuple-element.77), calls=%async_computation.6 | async-start | bytes 4194304 | tf_op jit(solution)/shard_map/all_to_all | solution.py:622
  268.2 30.5 %all-to-all-start.5 = ((f32[8,520,128]{2,1,0:T(8,128)}), f32[8,520,128]{2,1,0:T(8,128)S(1)}, u32[]{:S(2)}, u32[]{:S(2)}) async-start(f32[8,520,128]{2,1,0:T(8,128)} %get-tuple-element.74), calls=%async_computation.5 | async-start | bytes 4259840 | tf_op jit(solution)/shard_map/all_to_all | solution.py:622
  298.7 31.3 %copy-start.1 = (f32[8,520,128]{2,1,0:T(8,128)}, f32[8,520,128]{2,1,0:T(8,128)S(1)}, u32[]{:S(2)}) copy-start(f32[8,520,128]{2,1,0:T(8,128)S(1)} %all-to-all-done.5.refs_0_) | copy-start | bytes 6389764
  330.0 4.7 copy-start.8
  330.0 4.7 copy-start.10
  330.0 53.8 %all-to-all-start.9 = ((f32[8,1024,128]{2,1,0:T(8,128)}), f32[8,1024,128]{2,1,0:T(8,128)}, u32[]{:S(2)}, u32[]{:S(2)}) async-start(f32[8,1024,128]{2,1,0:T(8,128)} %get-tuple-element.87), calls=%async_computation.9 | async-start | bytes 8388608 | tf_op jit(solution)/shard_map/all_to_all | solution.py:622
  357.1 6.4 %collective-permute-start.20 = (f32[2,5,8,128]{3,2,1,0:T(8,128)}, f32[2,5,8,128]{3,2,1,0:T(8,128)S(1)}, u32[]{:S(2)}, u32[]{:S(2)}) collective-permute-start(f32[2,5,8,128]{3,2,1,0:T(8,128)} %get-tuple-element.84.refs_11_), channel_id=1, source_target_pairs={{0,1},{1,2},{2,3},{3,0},{4,5},{5,6},{6,7},{7,4},{8,9},{9,10},{10,1... | collective-permute-start | bytes 122888 | tf_op jit(solution)/shard_map/ppermute | solution.py:669
  358.3 6.5 %collective-permute-start.21 = (f32[2,5,8,128]{3,2,1,0:T(8,128)}, f32[2,5,8,128]{3,2,1,0:T(8,128)S(1)}, u32[]{:S(2)}, u32[]{:S(2)}) collective-permute-start(f32[2,5,8,128]{3,2,1,0:T(8,128)} %get-tuple-element.84.refs_11_), channel_id=1, source_target_pairs={{0,2},{1,3},{2,0},{3,1},{4,6},{5,7},{6,4},{7,5},{8,10},{9,11},{10,... | collective-permute-start | bytes 122888 | tf_op jit(solution)/shard_map/ppermute | solution.py:669
  359.5 5.3 %collective-permute-start.22 = (f32[2,5,8,128]{3,2,1,0:T(8,128)}, f32[2,5,8,128]{3,2,1,0:T(8,128)S(1)}, u32[]{:S(2)}, u32[]{:S(2)}) collective-permute-start(f32[2,5,8,128]{3,2,1,0:T(8,128)} %get-tuple-element.84.refs_11_), channel_id=1, source_target_pairs={{0,3},{1,0},{2,1},{3,2},{4,7},{5,4},{6,5},{7,6},{8,11},{9,8},{10,9... | collective-permute-start | bytes 122888 | tf_op jit(solution)/shard_map/ppermute | solution.py:669
  363.5 1.3 copy-start.19
  383.8 4.7 copy-start.12
  383.8 4.7 copy-start.14
  383.8 4.7 copy-start.16
  383.8 54.5 %all-to-all-start.8 = ((f32[8,1040,128]{2,1,0:T(8,128)}), f32[8,1040,128]{2,1,0:T(8,128)}, u32[]{:S(2)}, u32[]{:S(2)}) async-start(f32[8,1040,128]{2,1,0:T(8,128)} %get-tuple-element.85), calls=%async_computation.8 | async-start | bytes 8519680 | tf_op jit(solution)/shard_map/all_to_all | solution.py:622
  407.6 6.1 %collective-permute-start.23 = (f32[2,4,8,128]{3,2,1,0:T(8,128)}, f32[2,4,8,128]{3,2,1,0:T(8,128)S(1)}, u32[]{:S(2)}, u32[]{:S(2)}) collective-permute-start(f32[2,4,8,128]{3,2,1,0:T(8,128)} %get-tuple-element.90.refs_9_), channel_id=1, source_target_pairs={{0,1},{1,2},{2,3},{3,0},{4,5},{5,6},{6,7},{7,4},{8,9},{9,10},{10,1... | collective-permute-start | bytes 98312 | tf_op jit(solution)/shard_map/ppermute | solution.py:669
  408.9 5.9 %collective-permute-start.24 = (f32[2,4,8,128]{3,2,1,0:T(8,128)}, f32[2,4,8,128]{3,2,1,0:T(8,128)S(1)}, u32[]{:S(2)}, u32[]{:S(2)}) collective-permute-start(f32[2,4,8,128]{3,2,1,0:T(8,128)} %get-tuple-element.90.refs_9_), channel_id=1, source_target_pairs={{0,2},{1,3},{2,0},{3,1},{4,6},{5,7},{6,4},{7,5},{8,10},{9,11},{10,... | collective-permute-start | bytes 98312 | tf_op jit(solution)/shard_map/ppermute | solution.py:669
  410.0 4.8 collective-permute-start.25
  413.8 1.0 copy-start.23
  469.3 3.7 copy-start.4
  469.3 6.0 %copy-start.5 = (f32[2,6,64,8]{3,2,1,0:T(8,128)S(1)}, f32[2,6,64,8]{3,2,1,0:T(8,128)}, u32[]{:S(2)}) copy-start(f32[2,6,64,8]{3,2,1,0:T(8,128)} %get-tuple-element.96) | copy-start | bytes 73732
  469.3 30.3 %all-to-all-start.11 = ((f32[8,512,128]{2,1,0:T(8,128)}), f32[8,512,128]{2,1,0:T(8,128)S(1)}, u32[]{:S(2)}, u32[]{:S(2)}) async-start(f32[8,512,128]{2,1,0:T(8,128)} %get-tuple-element.94), calls=%async_computation.11 | async-start | bytes 4194304 | tf_op jit(solution)/shard_map/all_to_all | solution.py:622
  499.6 4.0 copy-start.2
  500.3 15.2 %all-to-all-start.12 = ((f32[8,1,384]{2,1,0:T(1,128)}), f32[8,1,384]{2,1,0:T(1,128)S(1)}, u32[]{:S(2)}, u32[]{:S(2)}) async-start(f32[8,1,384]{2,1,0:T(1,128)} %copy.51), calls=%async_computation.12 | async-start | bytes 24576 | tf_op jit(solution)/shard_map/all_to_all | solution.py:622
  (10 other events, 6.6 us)

commit v4 on v3

--- a/solution.py
+++ b/solution.py
@@ -68,6 +68,7 @@
         self.main = 4 * self.chunk
         self.depth = shards * cells
         self.edge = cells * self.main
+        self.batch = 4 if cells % 4 == 0 else 2 if cells % 2 == 0 else 1
         self.pad = (cells + 7) // 8 * 8
 
     def height(self, chunk):
@@ -106,7 +107,12 @@
     return [View(refs[0], side * plan.height(at)) for side in range(2)]
 
 
-def forward_slabs(plan, cell, phis, into, stacked, outs):
+def forward_slabs(plan, step, phis, into, stacked, outs):
+    for sub in range(plan.batch):
+        forward_cell(plan, step * plan.batch + sub, sub, functools.partial(phis, sub), into, stacked, outs)
+
+
+def forward_cell(plan, cell, sub, phis, into, stacked, outs):
     width, half, rows, chunk = plan.width, plan.half, plan.rows, plan.chunk
     lane = lax.broadcasted_iota(jnp.int32, (width, half), 1)
     first = lane == 0
@@ -119,7 +125,7 @@
         real = cos_re + jnp.where(first, 0.0, sin_im)
         imag = jnp.where(first, 0.0, cos_im) - sin_re
         for at in range(plan.chunks):
-            base = pl.multiple_of(cell * plan.main, 8) if at == 0 else 0
+            base = pl.multiple_of(cell * plan.main, 8) if at == 0 else sub * plan.main
             for shard in range(plan.shards):
                 start = shard * rows + at * chunk
                 outs[at][shard, pl.ds(base + band * chunk, chunk), :] = real[start : start + chunk]
@@ -139,7 +145,22 @@
         outs[0][shard, pl.ds(plan.edge + cell, 1), :] = row
 
 
-def inverse_slabs(plan, cell, ins, beside, back, take):
+def inverse_slabs(plan, step, ins, beside, back, take):
+    width = plan.width
+    uppers, lowers = [], []
+    for sub in range(plan.batch):
+        inverse_cell(plan, step * plan.batch + sub, sub, ins, uppers, lowers)
+    pairs = jnp.concatenate([jnp.concatenate(uppers, axis=1), jnp.concatenate(lowers, axis=1)], axis=0)
+    mixed = dot3(beside, split(pairs))
+    slabs = [mixed[:, i * width : (i + 1) * width] for i in range(2 * plan.batch)]
+    out = dot3(split(jnp.concatenate(slabs, axis=0)), back)
+    for sub in range(plan.batch):
+        for band in range(2):
+            start = (2 * sub + band) * width
+            take(sub, band, out[start : start + width])
+
+
+def inverse_cell(plan, cell, sub, ins, uppers, lowers):
     width, half, rows, chunk = plan.width, plan.half, plan.rows, plan.chunk
     lines = [ins[0][shard, pl.ds(plan.edge + cell, 1), :] for shard in range(plan.shards)]
     lines.append(jnp.zeros((LANES - plan.shards, LANES), jnp.float32))
@@ -147,29 +168,23 @@
     shifted = [pltpu.roll(turned, LANES - shard, 1) if shard else turned for shard in range(plan.shards)]
     sides = [jnp.concatenate([held[g * rows : (g + 1) * rows] for held in shifted], axis=0) for g in range(4)]
     first = lax.broadcasted_iota(jnp.int32, (width, half), 1) == 0
-    uppers, lowers = [], []
     for band in range(2):
         reals, imags = [], []
         for shard in range(plan.shards):
             for at in range(plan.chunks):
-                base = pl.multiple_of(cell * plan.main, 8) if at == 0 else 0
+                base = pl.multiple_of(cell * plan.main, 8) if at == 0 else sub * plan.main
                 reals.append(ins[at][shard, pl.ds(base + band * chunk, chunk), :])
                 imags.append(ins[at][shard, pl.ds(base + (2 + band) * chunk, chunk), :])
         real, imag = jnp.concatenate(reals, axis=0), jnp.concatenate(imags, axis=0)
         uppers += [real, jnp.where(first, sides[band], imag)]
         lowers += [-imag, jnp.where(first, -sides[band + 2], real)]
-    pairs = jnp.concatenate([jnp.concatenate(uppers, axis=1), jnp.concatenate(lowers, axis=1)], axis=0)
-    mixed = dot3(beside, split(pairs))
-    out = dot3(split(jnp.concatenate([mixed[:, :width], mixed[:, width:]], axis=0)), back)
-    for band in range(2):
-        take(band, out[band * width : (band + 1) * width])
 
 
 def first_kernel(plan, kept, phi, into_h, into_l, stacked_h, stacked_l, *refs):
     cell = pl.program_id(0)
     outs = refs[kept:]
     into, stacked = (into_h[...], into_l[...]), (stacked_h[...], stacked_l[...])
-    forward_slabs(plan, cell, lambda band: phi[0, band], into, stacked, outs)
+    forward_slabs(plan, cell, lambda sub, band: phi[sub, band], into, stacked, outs)
 
 
 def middle_kernel(plan, kept, *refs):
@@ -179,12 +194,12 @@
     into_h, into_l, stacked_h, stacked_l, beside_h, beside_l, back_h, back_l = refs[plan.chunks + 1 : plan.chunks + 9]
     outs, held = refs[plan.chunks + 9 + kept : -1], refs[-1]
 
-    def take(band, value):
-        held[band] = value * coeff[0]
+    def take(sub, band, value):
+        held[sub, band] = value * coeff[sub]
 
     inverse_slabs(plan, cell, ins, (beside_h[...], beside_l[...]), (back_h[...], back_l[...]), take)
     into, stacked = (into_h[...], into_l[...]), (stacked_h[...], stacked_l[...])
-    forward_slabs(plan, cell, lambda band: held[band], into, stacked, outs)
+    forward_slabs(plan, cell, lambda sub, band: held[sub, band], into, stacked, outs)
 
 
 def last_kernel(plan, *refs):
@@ -192,8 +207,8 @@
     coeff, beside_h, beside_l, back_h, back_l = refs[plan.chunks : plan.chunks + 5]
     out = refs[-1]
 
-    def take(band, value):
-        out[0, band] = value * coeff[0]
+    def take(sub, band, value):
+        out[sub, band] = value * coeff[sub]
 
     inverse_slabs(plan, pl.program_id(0), ins, (beside_h[...], beside_l[...]), (back_h[...], back_l[...]), take)
 
@@ -211,8 +226,9 @@
             shape = (plan.shards, plan.height(0), LANES)
             specs.append(pl.BlockSpec(shape, lambda cell, first=side if merged else 0: (0, first, 0)))
         else:
-            shape = (plan.shards, plan.main, LANES)
-            specs.append(pl.BlockSpec(shape, lambda cell, first=side * plan.cells if merged else 0: (0, first + cell, 0)))
+            shape = (plan.shards, plan.batch * plan.main, LANES)
+            first = side * plan.cells // plan.batch if merged else 0
+            specs.append(pl.BlockSpec(shape, lambda cell, first=first: (0, first + cell, 0)))
     return specs
 
 
@@ -221,11 +237,11 @@
 
 
 def slab_spec(plan, side):
-    return pl.BlockSpec((1, 2, plan.width, plan.width), lambda cell: (cell, side, 0, 0))
+    return pl.BlockSpec((plan.batch, 2, plan.width, plan.width), lambda cell: (cell, side, 0, 0))
 
 
 def coeff_spec(plan):
-    return pl.BlockSpec((1, plan.width, plan.width), lambda cell: (cell, 0, 0))
+    return pl.BlockSpec((plan.batch, plan.width, plan.width), lambda cell: (cell, 0, 0))
 
 
 def cost(microseconds):
@@ -243,7 +259,7 @@
             operands, in_specs = operands + [held[at]], in_specs + [pl.BlockSpec(memory_space=pl.ANY)]
     return pl.pallas_call(
         functools.partial(kernel, plan, len(aliases)),
-        grid=(plan.cells,),
+        grid=(plan.cells // plan.batch,),
         in_specs=in_specs,
         out_specs=piece_specs(plan, side, plan.sides_sent),
         out_shape=sent_shapes(plan),
@@ -262,7 +278,7 @@
 
 def middle(plan, side, ins, coeff, consts, held):
     in_specs = piece_specs(plan, side, plan.sides_back) + [coeff_spec(plan)] + [whole(c) for c in consts]
-    scratch = [pltpu.VMEM((2, plan.width, plan.width), jnp.float32)]
+    scratch = [pltpu.VMEM((plan.batch, 2, plan.width, plan.width), jnp.float32)]
     return send(middle_kernel, plan, side, [*ins, coeff, *consts], in_specs, held, 25, scratch, "between_steps")
 
 
@@ -276,7 +292,7 @@
         in_specs.append(pl.BlockSpec(memory_space=pl.ANY))
     return pl.pallas_call(
         functools.partial(last_kernel, plan),
-        grid=(plan.cells,),
+        grid=(plan.cells // plan.batch,),
         in_specs=in_specs,
         out_specs=slab_spec(plan, side),
         out_shape=jax.ShapeDtypeStruct((plan.cells, 4, plan.width, plan.width), jnp.float32),
@@ -440,15 +456,16 @@
 
 def mirror_kernel(plan, group, upper, lanes_turned, rows_turned, turned, lead):
     rows, half = plan.rows, plan.half
-    cells = upper.shape[1]
+    cells = rows_turned.shape[0] // rows
     for part in range(2):
         sign = 1.0 if part == 0 else -1.0
-        pairs = split(sign * upper[part].reshape(cells * rows, half))
-        value = dot(pairs[0], lanes_turned[...]) + dot(pairs[1], lanes_turned[...])
-        lead[part] = value.reshape(cells, rows, half)[:, 0, :]
-        pairs = split(value)
-        value = dot(rows_turned[...], pairs[0]) + dot(rows_turned[...], pairs[1])
-        turned[part] = value.reshape(cells, rows, half)
+        for at in range(0, upper.shape[1], cells):
+            pairs = split(sign * upper[part, at : at + cells].reshape(cells * rows, half))
+            value = dot(pairs[0], lanes_turned[...]) + dot(pairs[1], lanes_turned[...])
+            lead[part, at : at + cells] = value.reshape(cells, rows, half)[:, 0, :]
+            pairs = split(value)
+            value = dot(rows_turned[...], pairs[0]) + dot(rows_turned[...], pairs[1])
+            turned[part, at : at + cells] = value.reshape(cells, rows, half)
 
 
 def mirror(plan, forward, groups):
@@ -463,19 +480,18 @@
         for r in range(1, rows):
             rows_turned[c * rows + r, c * rows + rows - r] = 1
     lanes_turned, rows_turned = jnp.asarray(lanes_turned), jnp.asarray(rows_turned)
-    blocks = share // cells
     group = lax.axis_index("ba").astype(jnp.int32).reshape(1)
     spec = pltpu.PrefetchScalarGridSpec(
         num_scalar_prefetch=1,
-        grid=(forward.shape[0], blocks),
+        grid=(forward.shape[0],),
         in_specs=[
-            pl.BlockSpec((None, 2, cells, rows, half), lambda step, z, at: (step, 0, at[0] * blocks + z, 0, 1)),
-            pl.BlockSpec(lanes_turned.shape, lambda step, z, at: (0, 0)),
-            pl.BlockSpec(rows_turned.shape, lambda step, z, at: (0, 0)),
+            pl.BlockSpec((None, 2, share, rows, half), lambda step, at: (step, 0, at[0], 0, 1)),
+            pl.BlockSpec(lanes_turned.shape, lambda step, at: (0, 0)),
+            pl.BlockSpec(rows_turned.shape, lambda step, at: (0, 0)),
         ],
         out_specs=[
-            pl.BlockSpec((None, 2, cells, rows, half), lambda step, z, at: (step, 0, z, 0, 0)),
-            pl.BlockSpec((None, 2, cells, half), lambda step, z, at: (step, 0, z, 0)),
+            pl.BlockSpec((None, 2, share, rows, half), lambda step, at: (step, 0, 0, 0, 0)),
+            pl.BlockSpec((None, 2, share, half), lambda step, at: (step, 0, 0, 0)),
         ],
     )
     return pl.pallas_call(
@@ -652,16 +668,23 @@
     sent = into(lambda side, held: first(plan, side, starts[side], consts, held))
     chunk_rows = [slice(at * plan.chunk, (at + 1) * plan.chunk) for at in range(plan.chunks)]
     spread = [[spread_targets(swapped[step][:, :, held]) for held in chunk_rows] for step in range(steps)]
+    early = make_aims(plan, 0, forward, spread[0][0], keep, 0)
     for step in range(steps):
         modes, after = [], None
         for at in range(plan.chunks):
-            modes.append(in_order(sent[at], after, spread[0][at] if step == 0 else ()))
+            besides = ()
+            if step == 0:
+                besides = spread[0][at]
+                if at == 1:
+                    besides = [*besides, early]
+            modes.append(in_order(sent[at], after, besides))
             after = modes[at][-1]
         back = []
         back = []
         for at in range(plan.chunks):
             inv = inverse[at]
-            common = (*modes[at], make_aims(plan, at, forward, spread[step][at], keep, step))
+            aims = early if step == 0 and at == 0 else make_aims(plan, at, forward, spread[step][at], keep, step)
+            common = (*modes[at], aims)
             part0, part1, flux, sums, *extras = sweep(plan, at, False, groups, *common, inv[:, :6], couple, rate)
             collect(sums, 0)
             fluxes = [flux]

time: 519 us -> 520 us (level); the launches traced: 516 us -> 510 us
  Pallas kernels: 231 us -> 219 us
  starting transfers between devices: 89 us -> 95.5 us
    pallas_call x4, Pallas kernels: 64.3 us -> 56.7 us  [send(): pl.pallas_call(functools.partial(kernel, plan, len(aliases)), grid=(plan....]
    ppermute x12, waiting for transfers between devices: 36.5 us -> 31.3 us  [spread_targets(): lax.ppermute(turned, 'ba', [(i, (i + shift) % groups) for i in range(grou...]
  transfers between devices with their start and end apart: 37 -> 37, of which waited for: 24 -> 25; matrix products, arithmetic and copies ran while one was open for 5% -> 5% of each run, Pallas kernels for 44% -> 42%
where the time goes in v4:
time: 520 us; the launch traced here: 510 us
  Pallas kernels  219 us (42%)
  waiting for transfers between devices  101 us (19%)
  starting transfers between devices  95.5 us (18%)
  blocking collectives  62.2 us (12%)
  local copies, waits for them, and re-layouts  16.8 us (3%)
  other arithmetic  14 us (3%)
    pallas_call x8, Pallas kernels, sweep(): pl.pallas_call(functools.partial(sweep_kernel, plan, at, upward, groups),...  111 us
    all_to_all x2, blocking collectives, exchange(): return lax.all_to_all(array, 'gx', split_axis=0, concat_axis=0, tiled=True)  62.2 us
    pallas_call x4, Pallas kernels, send(): pl.pallas_call(functools.partial(kernel, plan, len(aliases)), grid=(plan....  56.7 us
    all_to_all x11, starting transfers between devices, exchange(): return lax.all_to_all(array, 'gx', split_axis=0, concat_axis=0, tiled=True)  48.9 us
    all_to_all x11, waiting for transfers between devices, exchange(): return lax.all_to_all(array, 'gx', split_axis=0, concat_axis=0, tiled=True)  45.4 us
    ppermute x12, waiting for transfers between devices, spread_targets(): lax.ppermute(turned, 'ba', [(i, (i + shift) % groups) for i in range(grou...  31.3 us
    pallas_call x4, Pallas kernels, make_aims(): pl.pallas_call(functools.partial(aims_kernel, plan, at), grid_spec=spec,...  26.3 us
    ppermute x12, starting transfers between devices, spread_targets(): lax.ppermute(turned, 'ba', [(i, (i + shift) % groups) for i in range(grou...  23.5 us
  transfers between devices with their start and end apart: 37, of which 25 were waited for; matrix products, arithmetic and copies ran while one was open for 5% of the time, Pallas kernels for 42%

profile of v4, /device:TPU:0, one launch (start us, length us, event | category | flops | bytes accessed | tf_op | source)
XLA Modules:
  0.0 510.3 jit_solution(13099767614300546016)
XLA Ops:
  0.6 4.4 mirrored.1
  5.0 3.3 collective-permute-start.1
  9.8 10.2 %into_modes.2 = (f32[8,520,128]{2,1,0:T(8,128)}, f32[8,1024,128]{2,1,0:T(8,128)}) custom-call(f32[8,4,256,256]{3,2,1,0:T(8,128)} %phi.1, bf16[256,256]{1,0:T(8,128)(2,1)} %constant.161.clone.into_h.refs_3_, bf16[256,256]{1,0:T(8,128)(2,1)} %constant.162.clone.into_l.refs_4_, bf16[512,256]{1,0:T(8,128)(2,1)} %constant.163.clone.stacked_h.refs_5_, ...), custom_call_target="tpu_custom_call" | custom-call | bytes 44280000 | tf_op jit(solution)/shard_map/into_modes/pallas_call | solution.py:260
  19.9 4.9 all-to-all-start
  26.0 6.3 %collective-permute-done.1 = f32[2,2,16,32,128]{4,3,2,1,0:T(8,128)S(1)} collective-permute-done((f32[2,2,16,32,128]{4,3,2,1,0:T(8,128)}, f32[2,2,16,32,128]{4,3,2,1,0:T(8,128)S(1)}, u32[]{:S(2)}, u32[]{:S(2)}) %collective-permute-start.1) | collective-permute-done | bytes 1048608 | tf_op jit(solution)/shard_map/ppermute | solution.py:627
  32.7 2.4 collective-permute-start.2
  35.1 2.6 collective-permute-start.3
  39.1 10.1 %into_modes.3 = (f32[8,520,128]{2,1,0:T(8,128)}, f32[8,1024,128]{2,1,0:T(8,128)}) custom-call(f32[8,4,256,256]{3,2,1,0:T(8,128)} %phi.1, bf16[256,256]{1,0:T(8,128)(2,1)} %constant.161.clone.into_h.refs_3_, bf16[256,256]{1,0:T(8,128)(2,1)} %constant.162.clone.into_l.refs_4_, ...), custom_call_target="tpu_custom_call", output_to_operand_aliasing={{1}: (5, {})} | custom-call | bytes 44280000 | tf_op jit(solution)/shard_map/into_modes/pallas_call | solution.py:260
  49.2 6.2 %collective-permute-done.3 = f32[2,16,16,128]{3,2,1,0:T(8,128)S(1)} collective-permute-done((f32[2,16,16,128]{3,2,1,0:T(8,128)S(1)}, f32[2,16,16,128]{3,2,1,0:T(8,128)S(1)}, u32[]{:S(2)}, u32[]{:S(2)}) %collective-permute-start.3) | collective-permute-done | bytes 262176 | tf_op jit(solution)/shard_map/ppermute | solution.py:634
  57.5 5.6 %all-to-all-start.1 = ((f32[8,520,128]{2,1,0:T(8,128)}), f32[8,520,128]{2,1,0:T(8,128)}, u32[]{:S(2)}, u32[]{:S(2)}) async-start(f32[8,520,128]{2,1,0:T(8,128)} %get-tuple-element.60), calls=%async_computation.1 | async-start | bytes 4259840 | tf_op jit(solution)/shard_map/all_to_all | solution.py:638
  64.1 4.3 collective-permute-start.8
  68.4 2.2 collective-permute-start.9
  71.3 2.2 pad_maximum_fusion.other
  74.1 7.0 %targets.4.refs_2_ = f32[64,2,5,8,128]{4,3,2,1,0:T(8,128)} custom-call(s32[1]{0:T(128)} %bitcast.group, f32[2,2,64,32,256]{4,3,2,1,0:T(8,128)} %own.7, f32[4,2,16,16,128]{4,3,2,1,0:T(8,128)} %pad_maximum_fusion.other, f32[8,128]{1,0:T(8,128)} %broadcast_in_dim.180.keep.refs_10_.refs_8_), custom_call_target="tpu_custom_call" | custom-call | bytes 14760000 | tf_op jit(solution)/shard_map/targets/pallas_call | solution.py:562
  81.1 7.1 %collective-permute-done.9 = f32[2,16,16,128]{3,2,1,0:T(8,128)S(1)} collective-permute-done((f32[2,16,16,128]{3,2,1,0:T(8,128)S(1)}, f32[2,16,16,128]{3,2,1,0:T(8,128)S(1)}, u32[]{:S(2)}, u32[]{:S(2)}) %collective-permute-start.9) | collective-permute-done | bytes 262176 | tf_op jit(solution)/shard_map/ppermute | solution.py:634
  88.1 2.0 all-to-all-done.1.refs_1_
  90.1 4.7 all-to-all-start.3
  99.2 14.3 %downward.4 = (f32[8,520,128]{2,1,0:T(8,128)}, f32[8,520,128]{2,1,0:T(8,128)}, f32[2,5,8,128]{3,2,1,0:T(8,128)}, f32[3,6,64,8]{3,2,1,0:T(8,128)}, f32[64,2,8,128]{3,2,1,0:T(8,128)}) custom-call(f32[8,520,128]{2,1,0:T(8,128)} %copy-done, f32[8,520,128]{2,1,0:T(8,128)} %all-to-all-done.1.refs_1_, f32[64,2,5,8,128]{4,3,2,1,0:T(8,128)} %targets.4.refs_2_, ...), custom_call_target="tpu_custom_call" | custom-call | bytes 47970000 | tf_op jit(solution)/shard_map/downward/pallas_call | solution.py:445
  113.6 4.2 collective-permute-start.5
  117.8 2.2 collective-permute-start.6
  122.0 1.5 collective-permute-done.6.refs_13_
  125.3 16.4 %upward.4 = (f32[8,1040,128]{2,1,0:T(8,128)}, f32[3,6,64,8]{3,2,1,0:T(8,128)}) custom-call(f32[8,520,128]{2,1,0:T(8,128)} %copy-done, f32[8,520,128]{2,1,0:T(8,128)} %all-to-all-done.1.refs_1_, f32[64,2,5,8,128]{4,3,2,1,0:T(8,128)} %targets.4.refs_2_, f32[2,6,9,8,128]{4,3,2,1,0:T(8,128)} %get-tuple-element.111.refs_3_, ...), custom_call_target="tpu_custom_call" | custom-call | bytes 47970000 | tf_op jit(solution)/shard_map/upward/pallas_call | solution.py:445
  141.6 2.4 all-to-all-done.3.refs_0_
  144.0 4.6 all-to-all-start.2
  149.7 4.2 collective-permute-start.14
  153.9 2.2 collective-permute-start.15
  158.3 6.2 %targets.5.refs_1_ = f32[64,2,4,8,128]{4,3,2,1,0:T(8,128)} custom-call(s32[1]{0:T(128)} %bitcast.group, f32[2,2,64,32,256]{4,3,2,1,0:T(8,128)} %own.7, f32[4,2,16,16,128]{4,3,2,1,0:T(8,128)} %pad_maximum_fusion.1.other, f32[8,128]{1,0:T(8,128)} %broadcast_in_dim.180.keep.refs_10_.refs_8_), custom_call_target="tpu_custom_call" | custom-call | bytes 14760000 | tf_op jit(solution)/shard_map/targets/pallas_call | solution.py:562
  164.5 11.8 %downward.5 = (f32[8,512,128]{2,1,0:T(8,128)}, f32[8,512,128]{2,1,0:T(8,128)}, f32[2,4,8,128]{3,2,1,0:T(8,128)}, f32[2,6,64,8]{3,2,1,0:T(8,128)}) custom-call(f32[8,1024,128]{2,1,0:T(8,128)} %all-to-all-done.3.refs_0_, f32[64,2,4,8,128]{4,3,2,1,0:T(8,128)} %targets.5.refs_1_, f32[2,6,8,8,128]{4,3,2,1,0:T(8,128)} %get-tuple-element.112.refs_2_, ...), custom_call_target="tpu_custom_call" | custom-call | bytes 47970000 | tf_op jit(solution)/shard_map/downward/pallas_call | solution.py:445
  176.4 1.8 collective-permute-start.11
  178.9 3.3 collective-permute-done.11.refs_10_
  183.2 3.2 collective-permute-done.13.refs_12_
  187.0 13.2 %upward.5 = (f32[8,512,128]{2,1,0:T(8,128)}, f32[8,512,128]{2,1,0:T(8,128)}, f32[2,6,64,8]{3,2,1,0:T(8,128)}) custom-call(f32[8,1024,128]{2,1,0:T(8,128)} %all-to-all-done.3.refs_0_, f32[64,2,4,8,128]{4,3,2,1,0:T(8,128)} %targets.5.refs_1_, f32[2,6,8,8,128]{4,3,2,1,0:T(8,128)} %get-tuple-element.113.refs_2_, ...), custom_call_target="tpu_custom_call" | custom-call | bytes 47970000 | tf_op jit(solution)/shard_map/upward/pallas_call | solution.py:445
  201.0 4.1 all-to-all-start.4
  206.3 2.2 collective-permute-start.18
  209.0 7.2 %collective-permute-done.17 = f32[2,16,16,128]{3,2,1,0:T(8,128)S(1)} collective-permute-done((f32[2,16,16,128]{3,2,1,0:T(8,128)S(1)}, f32[2,16,16,128]{3,2,1,0:T(8,128)S(1)}, u32[]{:S(2)}, u32[]{:S(2)}) %collective-permute-start.17) | collective-permute-done | bytes 262176 | tf_op jit(solution)/shard_map/ppermute | solution.py:634
  216.2 10.8 %collective-permute-done.18 = f32[2,16,16,128]{3,2,1,0:T(8,128)S(1)} collective-permute-done((f32[2,16,16,128]{3,2,1,0:T(8,128)S(1)}, f32[2,16,16,128]{3,2,1,0:T(8,128)S(1)}, u32[]{:S(2)}, u32[]{:S(2)}) %collective-permute-start.18) | collective-permute-done | bytes 262176 | tf_op jit(solution)/shard_map/ppermute | solution.py:634
  228.4 3.3 all-to-all-done.4.refs_1_
  231.7 4.5 all-to-all-start.6
  236.3 18.2 %between_steps.2 = (f32[8,520,128]{2,1,0:T(8,128)}, f32[8,1024,128]{2,1,0:T(8,128)}) custom-call(f32[8,1040,128]{2,1,0:T(8,128)} %all-to-all-done.2.refs_0_, f32[8,512,128]{2,1,0:T(8,128)} %copy-done.3, f32[8,256,256]{2,1,0:T(8,128)} %refs_2_.7, bf16[256,256]{1,0:T(8,128)(2,1)} %constant.161.clone.into_h.refs_3_, ...), custom_call_target="tpu_custom_call" | custom-call | bytes 92250000 | tf_op jit(solution)/shard_map/between_steps/pallas_call | solution.py:260
  254.5 8.4 %all-to-all-done.6.refs_1_ = f32[8,512,128]{2,1,0:T(8,128)} async-done(((f32[8,512,128]{2,1,0:T(8,128)}), f32[8,512,128]{2,1,0:T(8,128)}, u32[]{:S(2)}, u32[]{:S(2)}) %all-to-all-start.6) | async-done | bytes 2097184 | tf_op jit(solution)/shard_map/all_to_all | solution.py:638
  262.9 3.6 all-to-all-start.5
  266.6 18.2 %between_steps.3 = (f32[8,520,128]{2,1,0:T(8,128)}, f32[8,1024,128]{2,1,0:T(8,128)}) custom-call(f32[8,1040,128]{2,1,0:T(8,128)} %all-to-all-done.2.refs_0_, f32[8,512,128]{2,1,0:T(8,128)} %all-to-all-done.6.refs_1_, f32[8,256,256]{2,1,0:T(8,128)} %refs_2_.7, bf16[256,256]{1,0:T(8,128)(2,1)} %constant.161.clone.into_h.refs_3_, ...), custom_call_target="tpu_custom_call", output_to_operand_aliasing={{1}: (11, {})} | custom-call | bytes 92250000 | tf_op jit(solution)/shard_map/between_steps/pallas_call | solution.py:260
  284.8 8.7 %all-to-all-done.5.refs_0_ = f32[8,520,128]{2,1,0:T(8,128)S(1)} async-done(((f32[8,520,128]{2,1,0:T(8,128)}), f32[8,520,128]{2,1,0:T(8,128)S(1)}, u32[]{:S(2)}, u32[]{:S(2)}) %all-to-all-start.5) | async-done | bytes 2129952 | tf_op jit(solution)/shard_map/all_to_all | solution.py:638
  293.5 31.3 %all_to_all.69.refs_1_ = f32[8,520,128]{2,1,0:T(8,128)} all-to-all(f32[8,520,128]{2,1,0:T(8,128)} %get-tuple-element.80), channel_id=1, replica_groups=mesh['gx'=8,'ba'=4] {'gx'}, dimensions={0} | all-to-all | bytes 4259840 | tf_op jit(solution)/shard_map/all_to_all | solution.py:638
  324.8 4.9 all-to-all-start.9
  330.8 7.0 %targets.6.refs_2_ = f32[64,2,5,8,128]{4,3,2,1,0:T(8,128)} custom-call(s32[1]{0:T(128)} %bitcast.group, f32[2,2,64,32,256]{4,3,2,1,0:T(8,128)} %own.7, f32[4,2,16,16,128]{4,3,2,1,0:T(8,128)} %pad_maximum_fusion.2.other, f32[8,128]{1,0:T(8,128)} %broadcast_in_dim.180.keep.refs_10_.refs_8_), custom_call_target="tpu_custom_call" | custom-call | bytes 14760000 | tf_op jit(solution)/shard_map/targets/pallas_call | solution.py:562
  337.8 14.3 %downward.6 = (f32[8,520,128]{2,1,0:T(8,128)}, f32[8,520,128]{2,1,0:T(8,128)}, f32[2,5,8,128]{3,2,1,0:T(8,128)}, f32[3,6,64,8]{3,2,1,0:T(8,128)}, f32[64,2,8,128]{3,2,1,0:T(8,128)}) custom-call(f32[8,520,128]{2,1,0:T(8,128)} %copy-done.1, f32[8,520,128]{2,1,0:T(8,128)} %all_to_all.69.refs_1_, f32[64,2,5,8,128]{4,3,2,1,0:T(8,128)} %targets.6.refs_2_, ...), custom_call_target="tpu_custom_call" | custom-call | bytes 47970000 | tf_op jit(solution)/shard_map/downward/pallas_call | solution.py:445
  352.1 1.9 collective-permute-start.20
  356.4 2.2 collective-permute-done.20.refs_12_
  360.8 16.4 %upward.6 = (f32[8,1040,128]{2,1,0:T(8,128)}, f32[3,6,64,8]{3,2,1,0:T(8,128)}) custom-call(f32[8,520,128]{2,1,0:T(8,128)} %copy-done.1, f32[8,520,128]{2,1,0:T(8,128)} %all_to_all.69.refs_1_, f32[64,2,5,8,128]{4,3,2,1,0:T(8,128)} %targets.6.refs_2_, f32[2,6,9,8,128]{4,3,2,1,0:T(8,128)} %get-tuple-element.111.refs_3_, ...), custom_call_target="tpu_custom_call" | custom-call | bytes 47970000 | tf_op jit(solution)/shard_map/upward/pallas_call | solution.py:445
  377.2 1.6 all-to-all-done.9.refs_0_
  378.8 4.7 all-to-all-start.8
  384.7 6.2 %targets.7.refs_1_ = f32[64,2,4,8,128]{4,3,2,1,0:T(8,128)} custom-call(s32[1]{0:T(128)} %bitcast.group, f32[2,2,64,32,256]{4,3,2,1,0:T(8,128)} %own.7, f32[4,2,16,16,128]{4,3,2,1,0:T(8,128)} %pad_maximum_fusion.3.other, f32[8,128]{1,0:T(8,128)} %broadcast_in_dim.180.keep.refs_10_.refs_8_), custom_call_target="tpu_custom_call" | custom-call | bytes 14760000 | tf_op jit(solution)/shard_map/targets/pallas_call | solution.py:562
  390.8 11.9 %downward.7 = (f32[8,512,128]{2,1,0:T(8,128)}, f32[8,512,128]{2,1,0:T(8,128)}, f32[2,4,8,128]{3,2,1,0:T(8,128)}, f32[2,6,64,8]{3,2,1,0:T(8,128)}) custom-call(f32[8,1024,128]{2,1,0:T(8,128)} %all-to-all-done.9.refs_0_, f32[64,2,4,8,128]{4,3,2,1,0:T(8,128)} %targets.7.refs_1_, f32[2,6,8,8,128]{4,3,2,1,0:T(8,128)} %get-tuple-element.112.refs_2_, ...), custom_call_target="tpu_custom_call" | custom-call | bytes 47970000 | tf_op jit(solution)/shard_map/downward/pallas_call | solution.py:445
  402.7 1.9 collective-permute-start.23
  407.0 1.9 collective-permute-done.23.refs_10_
  410.8 13.1 %upward.7 = (f32[8,512,128]{2,1,0:T(8,128)}, f32[8,512,128]{2,1,0:T(8,128)}, f32[2,6,64,8]{3,2,1,0:T(8,128)}) custom-call(f32[8,1024,128]{2,1,0:T(8,128)} %all-to-all-done.9.refs_0_, f32[64,2,4,8,128]{4,3,2,1,0:T(8,128)} %targets.7.refs_1_, f32[2,6,8,8,128]{4,3,2,1,0:T(8,128)} %get-tuple-element.113.refs_2_, ...), custom_call_target="tpu_custom_call" | custom-call | bytes 47970000 | tf_op jit(solution)/shard_map/upward/pallas_call | solution.py:445
  423.9 9.4 %all-to-all-done.8.refs_0_ = f32[8,1040,128]{2,1,0:T(8,128)} async-done(((f32[8,1040,128]{2,1,0:T(8,128)}), f32[8,1040,128]{2,1,0:T(8,128)}, u32[]{:S(2)}, u32[]{:S(2)}) %all-to-all-start.8) | async-done | bytes 4259872 | tf_op jit(solution)/shard_map/all_to_all | solution.py:638
  433.3 30.9 %all_to_all.70.refs_1_ = f32[8,512,128]{2,1,0:T(8,128)} all-to-all(f32[8,512,128]{2,1,0:T(8,128)} %get-tuple-element.93), channel_id=1, replica_groups=mesh['gx'=8,'ba'=4] {'gx'}, dimensions={0} | all-to-all | bytes 4194304 | tf_op jit(solution)/shard_map/all_to_all | solution.py:638
  464.3 4.0 all-to-all-start.11
  475.3 10.1 %out_of_modes.2.refs_7_ = f32[8,4,256,256]{3,2,1,0:T(8,128)} custom-call(f32[8,1040,128]{2,1,0:T(8,128)} %all-to-all-done.8.refs_0_, f32[8,512,128]{2,1,0:T(8,128)} %all_to_all.70.refs_1_, f32[8,256,256]{2,1,0:T(8,128)} %refs_2_.7, bf16[256,512]{1,0:T(8,128)(2,1)} %constant.165.clone.refs_7_.refs_3_, bf16[256,512]{1,0:T(8,128)(2,1)} %constant.166.clone.refs_8_.refs_4_, ...), custom_call_target="tpu_custom_call" | custom-call | bytes 59040000 | tf_op jit(solution)/shard_map/out_of_modes/pallas_call | solution.py:293
  485.4 9.5 %all-to-all-done.11.refs_1_ = f32[8,512,128]{2,1,0:T(8,128)S(1)} async-done(((f32[8,512,128]{2,1,0:T(8,128)}), f32[8,512,128]{2,1,0:T(8,128)S(1)}, u32[]{:S(2)}, u32[]{:S(2)}) %all-to-all-start.11) | async-done | bytes 2097184 | tf_op jit(solution)/shard_map/all_to_all | solution.py:638
  495.5 3.3 all-to-all-start.12
  498.9 10.1 %out_of_modes.3 = f32[8,4,256,256]{3,2,1,0:T(8,128)} custom-call(f32[8,1040,128]{2,1,0:T(8,128)} %all-to-all-done.8.refs_0_, f32[8,512,128]{2,1,0:T(8,128)} %copy-done.2, f32[8,256,256]{2,1,0:T(8,128)} %refs_2_.7, bf16[256,512]{1,0:T(8,128)(2,1)} %constant.165.clone.refs_7_.refs_3_, ...), custom_call_target="tpu_custom_call", output_to_operand_aliasing={{}: (7, {})} | custom-call | bytes 59040000 | tf_op jit(solution)/shard_map/out_of_modes/pallas_call | solution.py:293
  (219 shorter events, 46.1 us)
Async XLA Ops:
  5.0 27.2 %collective-permute-start.1 = (f32[2,2,16,32,128]{4,3,2,1,0:T(8,128)}, f32[2,2,16,32,128]{4,3,2,1,0:T(8,128)S(1)}, u32[]{:S(2)}, u32[]{:S(2)}) collective-permute-start(f32[2,2,16,32,128]{4,3,2,1,0:T(8,128)} %get-tuple-element.53), channel_id=1, source_target_pairs={{0,28},{4,24},{8,20},{12,16},{16,12},{20,8},{24,4},{28,0},{1,29},{... | collective-permute-start | bytes 3145736 | tf_op jit(solution)/shard_map/ppermute | solution.py:627
  8.4 17.6 %collective-permute-start = (f32[2,2,16,128]{3,2,1,0:T(8,128)}, f32[2,2,16,128]{3,2,1,0:T(8,128)S(1)}, u32[]{:S(2)}, u32[]{:S(2)}) collective-permute-start(f32[2,2,16,128]{3,2,1,0:T(8,128)} %get-tuple-element.54), channel_id=1, source_target_pairs={{0,0},{4,28},{8,24},{12,20},{16,16},{20,12},{24,8},{28,4},{1,1},{5... | collective-permute-start | bytes 98312 | tf_op jit(solution)/shard_map/ppermute | solution.py:628
  19.9 4.9 copy-start.31
  19.9 5.9 %copy-start.32 = (f32[4]{0:T(128)S(1)}, f32[4]{0:T(128)}, u32[]{:S(2)}) copy-start(f32[4]{0:T(128)} %param.26) | copy-start | bytes 52
  19.9 36.2 %all-to-all-start = ((f32[8,520,128]{2,1,0:T(8,128)}), f32[8,520,128]{2,1,0:T(8,128)S(1)}, u32[]{:S(2)}, u32[]{:S(2)}) async-start(f32[8,520,128]{2,1,0:T(8,128)} %get-tuple-element.56), calls=%async_computation | async-start | bytes 4259840 | tf_op jit(solution)/shard_map/all_to_all | solution.py:638
  32.7 16.5 %collective-permute-start.2 = (f32[2,16,16,128]{3,2,1,0:T(8,128)S(1)}, f32[2,16,16,128]{3,2,1,0:T(8,128)S(1)}, u32[]{:S(2)}, u32[]{:S(2)}) collective-permute-start(f32[2,16,16,128]{3,2,1,0:T(8,128)S(1)} %get-tuple-element.121), channel_id=1, source_target_pairs={{0,1},{1,2},{2,3},{3,0},{4,5},{5,6},{6,7},{7,4},{8,9},{9,10},{10,1... | collective-permute-start | bytes 786440 | tf_op jit(solution)/shard_map/ppermute | solution.py:634
  35.1 20.3 %collective-permute-start.3 = (f32[2,16,16,128]{3,2,1,0:T(8,128)S(1)}, f32[2,16,16,128]{3,2,1,0:T(8,128)S(1)}, u32[]{:S(2)}, u32[]{:S(2)}) collective-permute-start(f32[2,16,16,128]{3,2,1,0:T(8,128)S(1)} %get-tuple-element.121), channel_id=1, source_target_pairs={{0,2},{1,3},{2,0},{3,1},{4,6},{5,7},{6,4},{7,5},{8,10},{9,11},{10,... | collective-permute-start | bytes 786440 | tf_op jit(solution)/shard_map/ppermute | solution.py:634
  37.7 18.4 %collective-permute-start.4 = (f32[2,16,16,128]{3,2,1,0:T(8,128)S(1)}, f32[2,16,16,128]{3,2,1,0:T(8,128)}, u32[]{:S(2)}, u32[]{:S(2)}) collective-permute-start(f32[2,16,16,128]{3,2,1,0:T(8,128)S(1)} %get-tuple-element.121), channel_id=1, source_target_pairs={{0,3},{1,0},{2,1},{3,2},{4,7},{5,4},{6,5},{7,6},{8,11},{9,8},{10,9... | collective-permute-start | bytes 786440 | tf_op jit(solution)/shard_map/ppermute | solution.py:634
  49.2 6.2 %copy-start.7 = (f32[2,16,16,128]{3,2,1,0:T(8,128)}, f32[2,16,16,128]{3,2,1,0:T(8,128)S(1)}, u32[]{:S(2)}) copy-start(f32[2,16,16,128]{3,2,1,0:T(8,128)S(1)} %collective-permute-done.2) | copy-start | bytes 786436
  56.1 1.3 copy-start
  57.5 32.7 %all-to-all-start.1 = ((f32[8,520,128]{2,1,0:T(8,128)}), f32[8,520,128]{2,1,0:T(8,128)}, u32[]{:S(2)}, u32[]{:S(2)}) async-start(f32[8,520,128]{2,1,0:T(8,128)} %get-tuple-element.60), calls=%async_computation.1 | async-start | bytes 4259840 | tf_op jit(solution)/shard_map/all_to_all | solution.py:638
  64.1 17.0 %collective-permute-start.8 = (f32[2,16,16,128]{3,2,1,0:T(8,128)S(1)}, f32[2,16,16,128]{3,2,1,0:T(8,128)S(1)}, u32[]{:S(2)}, u32[]{:S(2)}) collective-permute-start(f32[2,16,16,128]{3,2,1,0:T(8,128)S(1)} %get-tuple-element.120), channel_id=1, source_target_pairs={{0,1},{1,2},{2,3},{3,0},{4,5},{5,6},{6,7},{7,4},{8,9},{9,10},{10,1... | collective-permute-start | bytes 786440 | tf_op jit(solution)/shard_map/ppermute | solution.py:634
  68.4 19.8 %collective-permute-start.9 = (f32[2,16,16,128]{3,2,1,0:T(8,128)S(1)}, f32[2,16,16,128]{3,2,1,0:T(8,128)S(1)}, u32[]{:S(2)}, u32[]{:S(2)}) collective-permute-start(f32[2,16,16,128]{3,2,1,0:T(8,128)S(1)} %get-tuple-element.120), channel_id=1, source_target_pairs={{0,2},{1,3},{2,0},{3,1},{4,6},{5,7},{6,4},{7,5},{8,10},{9,11},{10,... | collective-permute-start | bytes 786440 | tf_op jit(solution)/shard_map/ppermute | solution.py:634
  70.5 17.6 %collective-permute-start.10 = (f32[2,16,16,128]{3,2,1,0:T(8,128)S(1)}, f32[2,16,16,128]{3,2,1,0:T(8,128)S(1)}, u32[]{:S(2)}, u32[]{:S(2)}) collective-permute-start(f32[2,16,16,128]{3,2,1,0:T(8,128)S(1)} %get-tuple-element.120), channel_id=1, source_target_pairs={{0,3},{1,0},{2,1},{3,2},{4,7},{5,4},{6,5},{7,6},{8,11},{9,8},{10,9... | collective-permute-start | bytes 786440 | tf_op jit(solution)/shard_map/ppermute | solution.py:634
  90.1 5.1 %copy-start.37 = (f32[4]{0:T(128)S(1)}, f32[4]{0:T(128)}, u32[]{:S(2)}) copy-start(f32[4]{0:T(128)} %param.28) | copy-start | bytes 52
  90.1 6.4 %copy-start.33 = (f32[12]{0:T(128)S(1)}, f32[12]{0:T(128)}, u32[]{:S(2)}) copy-start(f32[12]{0:T(128)} %constant.177) | copy-start | bytes 148
  90.1 6.4 %copy-start.34 = (f32[12]{0:T(128)S(1)}, f32[12]{0:T(128)}, u32[]{:S(2)}) copy-start(f32[12]{0:T(128)} %constant.176) | copy-start | bytes 148
  90.1 6.4 %copy-start.35 = (f32[12]{0:T(128)S(1)}, f32[12]{0:T(128)}, u32[]{:S(2)}) copy-start(f32[12]{0:T(128)} %constant.175) | copy-start | bytes 148
  90.1 53.9 %all-to-all-start.3 = ((f32[8,1024,128]{2,1,0:T(8,128)}), f32[8,1024,128]{2,1,0:T(8,128)}, u32[]{:S(2)}, u32[]{:S(2)}) async-start(f32[8,1024,128]{2,1,0:T(8,128)} %get-tuple-element.67), calls=%async_computation.3 | async-start | bytes 8388608 | tf_op jit(solution)/shard_map/all_to_all | solution.py:638
  94.9 3.0 copy-start.36
  113.6 8.5 %collective-permute-start.5 = (f32[2,5,8,128]{3,2,1,0:T(8,128)}, f32[2,5,8,128]{3,2,1,0:T(8,128)S(1)}, u32[]{:S(2)}, u32[]{:S(2)}) collective-permute-start(f32[2,5,8,128]{3,2,1,0:T(8,128)} %get-tuple-element.64.refs_11_), channel_id=1, source_target_pairs={{0,1},{1,2},{2,3},{3,0},{4,5},{5,6},{6,7},{7,4},{8,9},{9,10},{10,1... | collective-permute-start | bytes 122888 | tf_op jit(solution)/shard_map/ppermute | solution.py:692
  117.8 5.7 %collective-permute-start.6 = (f32[2,5,8,128]{3,2,1,0:T(8,128)}, f32[2,5,8,128]{3,2,1,0:T(8,128)S(1)}, u32[]{:S(2)}, u32[]{:S(2)}) collective-permute-start(f32[2,5,8,128]{3,2,1,0:T(8,128)} %get-tuple-element.64.refs_11_), channel_id=1, source_target_pairs={{0,2},{1,3},{2,0},{3,1},{4,6},{5,7},{6,4},{7,5},{8,10},{9,11},{10,... | collective-permute-start | bytes 122888 | tf_op jit(solution)/shard_map/ppermute | solution.py:692
  119.9 4.7 collective-permute-start.7
  122.0 3.2 copy-start.19
  123.5 1.8 copy-start.20
  144.0 56.2 %all-to-all-start.2 = ((f32[8,1040,128]{2,1,0:T(8,128)}), f32[8,1040,128]{2,1,0:T(8,128)}, u32[]{:S(2)}, u32[]{:S(2)}) async-start(f32[8,1040,128]{2,1,0:T(8,128)} %get-tuple-element.65), calls=%async_computation.2 | async-start | bytes 8519680 | tf_op jit(solution)/shard_map/all_to_all | solution.py:638
  149.7 50.5 %collective-permute-start.14 = (f32[2,16,16,128]{3,2,1,0:T(8,128)S(1)}, f32[2,16,16,128]{3,2,1,0:T(8,128)S(1)}, u32[]{:S(2)}, u32[]{:S(2)}) collective-permute-start(f32[2,16,16,128]{3,2,1,0:T(8,128)S(1)} %get-tuple-element.117), channel_id=1, source_target_pairs={{0,1},{1,2},{2,3},{3,0},{4,5},{5,6},{6,7},{7,4},{8,9},{9,10},{10,1... | collective-permute-start | bytes 786440 | tf_op jit(solution)/shard_map/ppermute | solution.py:634
  153.9 46.3 %collective-permute-start.15 = (f32[2,16,16,128]{3,2,1,0:T(8,128)S(1)}, f32[2,16,16,128]{3,2,1,0:T(8,128)S(1)}, u32[]{:S(2)}, u32[]{:S(2)}) collective-permute-start(f32[2,16,16,128]{3,2,1,0:T(8,128)S(1)} %get-tuple-element.117), channel_id=1, source_target_pairs={{0,2},{1,3},{2,0},{3,1},{4,6},{5,7},{6,4},{7,5},{8,10},{9,11},{10,... | collective-permute-start | bytes 786440 | tf_op jit(solution)/shard_map/ppermute | solution.py:634
  156.0 44.2 %collective-permute-start.16 = (f32[2,16,16,128]{3,2,1,0:T(8,128)S(1)}, f32[2,16,16,128]{3,2,1,0:T(8,128)S(1)}, u32[]{:S(2)}, u32[]{:S(2)}) collective-permute-start(f32[2,16,16,128]{3,2,1,0:T(8,128)S(1)} %get-tuple-element.117), channel_id=1, source_target_pairs={{0,3},{1,0},{2,1},{3,2},{4,7},{5,4},{6,5},{7,6},{8,11},{9,8},{10,9... | collective-permute-start | bytes 786440 | tf_op jit(solution)/shard_map/ppermute | solution.py:634
  176.4 5.9 %collective-permute-start.11 = (f32[2,4,8,128]{3,2,1,0:T(8,128)}, f32[2,4,8,128]{3,2,1,0:T(8,128)S(1)}, u32[]{:S(2)}, u32[]{:S(2)}) collective-permute-start(f32[2,4,8,128]{3,2,1,0:T(8,128)} %get-tuple-element.70.refs_9_), channel_id=1, source_target_pairs={{0,1},{1,2},{2,3},{3,0},{4,5},{5,6},{6,7},{7,4},{8,9},{9,10},{10,1... | collective-permute-start | bytes 98312 | tf_op jit(solution)/shard_map/ppermute | solution.py:692
  178.2 5.0 collective-permute-start.12
  182.3 4.1 copy-start.27
  182.3 4.1 collective-permute-start.13
  183.2 3.2 copy-start.29
  200.2 4.9 copy-start.6
  201.0 30.7 %all-to-all-start.4 = ((f32[8,512,128]{2,1,0:T(8,128)}), f32[8,512,128]{2,1,0:T(8,128)S(1)}, u32[]{:S(2)}, u32[]{:S(2)}) async-start(f32[8,512,128]{2,1,0:T(8,128)} %get-tuple-element.73), calls=%async_computation.4 | async-start | bytes 4194304 | tf_op jit(solution)/shard_map/all_to_all | solution.py:638
  205.1 11.1 %collective-permute-start.17 = (f32[2,16,16,128]{3,2,1,0:T(8,128)S(1)}, f32[2,16,16,128]{3,2,1,0:T(8,128)S(1)}, u32[]{:S(2)}, u32[]{:S(2)}) collective-permute-start(f32[2,16,16,128]{3,2,1,0:T(8,128)S(1)} %copy-done.6), channel_id=1, source_target_pairs={{0,1},{1,2},{2,3},{3,0},{4,5},{5,6},{6,7},{7,4},{8,9},{9,10},{10,1... | collective-permute-start | bytes 786440 | tf_op jit(solution)/shard_map/ppermute | solution.py:634
  206.3 20.7 %collective-permute-start.18 = (f32[2,16,16,128]{3,2,1,0:T(8,128)S(1)}, f32[2,16,16,128]{3,2,1,0:T(8,128)S(1)}, u32[]{:S(2)}, u32[]{:S(2)}) collective-permute-start(f32[2,16,16,128]{3,2,1,0:T(8,128)S(1)} %copy-done.6), channel_id=1, source_target_pairs={{0,2},{1,3},{2,0},{3,1},{4,6},{5,7},{6,4},{7,5},{8,10},{9,11},{10,... | collective-permute-start | bytes 786440 | tf_op jit(solution)/shard_map/ppermute | solution.py:634
  208.4 18.5 %collective-permute-start.19 = (f32[2,16,16,128]{3,2,1,0:T(8,128)S(1)}, f32[2,16,16,128]{3,2,1,0:T(8,128)S(1)}, u32[]{:S(2)}, u32[]{:S(2)}) collective-permute-start(f32[2,16,16,128]{3,2,1,0:T(8,128)S(1)} %copy-done.6), channel_id=1, source_target_pairs={{0,3},{1,0},{2,1},{3,2},{4,7},{5,4},{6,5},{7,6},{8,11},{9,8},{10,9... | collective-permute-start | bytes 786440 | tf_op jit(solution)/shard_map/ppermute | solution.py:634
  216.2 38.3 %copy-start.13 = (f32[2,16,16,128]{3,2,1,0:T(8,128)}, f32[2,16,16,128]{3,2,1,0:T(8,128)S(1)}, u32[]{:S(2)}) copy-start(f32[2,16,16,128]{3,2,1,0:T(8,128)S(1)} %collective-permute-done.17) | copy-start | bytes 786436
  231.7 4.6 copy-start.3
  231.7 31.2 %all-to-all-start.6 = ((f32[8,512,128]{2,1,0:T(8,128)}), f32[8,512,128]{2,1,0:T(8,128)}, u32[]{:S(2)}, u32[]{:S(2)}) async-start(f32[8,512,128]{2,1,0:T(8,128)} %get-tuple-element.77), calls=%async_computation.6 | async-start | bytes 4194304 | tf_op jit(solution)/shard_map/all_to_all | solution.py:638
  262.9 30.5 %all-to-all-start.5 = ((f32[8,520,128]{2,1,0:T(8,128)}), f32[8,520,128]{2,1,0:T(8,128)S(1)}, u32[]{:S(2)}, u32[]{:S(2)}) async-start(f32[8,520,128]{2,1,0:T(8,128)} %get-tuple-element.74), calls=%async_computation.5 | async-start | bytes 4259840 | tf_op jit(solution)/shard_map/all_to_all | solution.py:638
  293.5 31.3 %copy-start.1 = (f32[8,520,128]{2,1,0:T(8,128)}, f32[8,520,128]{2,1,0:T(8,128)S(1)}, u32[]{:S(2)}) copy-start(f32[8,520,128]{2,1,0:T(8,128)S(1)} %all-to-all-done.5.refs_0_) | copy-start | bytes 6389764
  324.8 4.9 copy-start.10
  324.8 4.9 copy-start.12
  324.8 54.0 %all-to-all-start.9 = ((f32[8,1024,128]{2,1,0:T(8,128)}), f32[8,1024,128]{2,1,0:T(8,128)}, u32[]{:S(2)}, u32[]{:S(2)}) async-start(f32[8,1024,128]{2,1,0:T(8,128)} %get-tuple-element.87), calls=%async_computation.9 | async-start | bytes 8388608 | tf_op jit(solution)/shard_map/all_to_all | solution.py:638
  352.1 6.4 %collective-permute-start.20 = (f32[2,5,8,128]{3,2,1,0:T(8,128)}, f32[2,5,8,128]{3,2,1,0:T(8,128)S(1)}, u32[]{:S(2)}, u32[]{:S(2)}) collective-permute-start(f32[2,5,8,128]{3,2,1,0:T(8,128)} %get-tuple-element.84.refs_11_), channel_id=1, source_target_pairs={{0,1},{1,2},{2,3},{3,0},{4,5},{5,6},{6,7},{7,4},{8,9},{9,10},{10,1... | collective-permute-start | bytes 122888 | tf_op jit(solution)/shard_map/ppermute | solution.py:692
  354.0 5.9 %collective-permute-start.21 = (f32[2,5,8,128]{3,2,1,0:T(8,128)}, f32[2,5,8,128]{3,2,1,0:T(8,128)S(1)}, u32[]{:S(2)}, u32[]{:S(2)}) collective-permute-start(f32[2,5,8,128]{3,2,1,0:T(8,128)} %get-tuple-element.84.refs_11_), channel_id=1, source_target_pairs={{0,2},{1,3},{2,0},{3,1},{4,6},{5,7},{6,4},{7,5},{8,10},{9,11},{10,... | collective-permute-start | bytes 122888 | tf_op jit(solution)/shard_map/ppermute | solution.py:692
  355.3 4.9 collective-permute-start.22
  358.5 1.7 copy-start.21
  378.8 4.7 copy-start.14
  378.8 4.7 copy-start.16
  378.8 4.7 copy-start.18
  378.8 54.5 %all-to-all-start.8 = ((f32[8,1040,128]{2,1,0:T(8,128)}), f32[8,1040,128]{2,1,0:T(8,128)}, u32[]{:S(2)}, u32[]{:S(2)}) async-start(f32[8,1040,128]{2,1,0:T(8,128)} %get-tuple-element.85), calls=%async_computation.8 | async-start | bytes 8519680 | tf_op jit(solution)/shard_map/all_to_all | solution.py:638
  402.7 6.2 %collective-permute-start.23 = (f32[2,4,8,128]{3,2,1,0:T(8,128)}, f32[2,4,8,128]{3,2,1,0:T(8,128)S(1)}, u32[]{:S(2)}, u32[]{:S(2)}) collective-permute-start(f32[2,4,8,128]{3,2,1,0:T(8,128)} %get-tuple-element.90.refs_9_), channel_id=1, source_target_pairs={{0,1},{1,2},{2,3},{3,0},{4,5},{5,6},{6,7},{7,4},{8,9},{9,10},{10,1... | collective-permute-start | bytes 98312 | tf_op jit(solution)/shard_map/ppermute | solution.py:692
  404.6 5.4 %collective-permute-start.24 = (f32[2,4,8,128]{3,2,1,0:T(8,128)}, f32[2,4,8,128]{3,2,1,0:T(8,128)S(1)}, u32[]{:S(2)}, u32[]{:S(2)}) collective-permute-start(f32[2,4,8,128]{3,2,1,0:T(8,128)} %get-tuple-element.90.refs_9_), channel_id=1, source_target_pairs={{0,2},{1,3},{2,0},{3,1},{4,6},{5,7},{6,4},{7,5},{8,10},{9,11},{10,... | collective-permute-start | bytes 98312 | tf_op jit(solution)/shard_map/ppermute | solution.py:692
  405.9 4.3 collective-permute-start.25
  408.9 1.3 copy-start.25
  464.3 4.0 copy-start.4
  464.3 6.3 %copy-start.5 = (f32[2,6,64,8]{3,2,1,0:T(8,128)S(1)}, f32[2,6,64,8]{3,2,1,0:T(8,128)}, u32[]{:S(2)}) copy-start(f32[2,6,64,8]{3,2,1,0:T(8,128)} %get-tuple-element.96) | copy-start | bytes 73732
  464.3 30.6 %all-to-all-start.11 = ((f32[8,512,128]{2,1,0:T(8,128)}), f32[8,512,128]{2,1,0:T(8,128)S(1)}, u32[]{:S(2)}, u32[]{:S(2)}) async-start(f32[8,512,128]{2,1,0:T(8,128)} %get-tuple-element.94), calls=%async_computation.11 | async-start | bytes 4194304 | tf_op jit(solution)/shard_map/all_to_all | solution.py:638
  494.9 4.0 copy-start.2
  495.5 13.5 %all-to-all-start.12 = ((f32[8,1,384]{2,1,0:T(1,128)}), f32[8,1,384]{2,1,0:T(1,128)S(1)}, u32[]{:S(2)}, u32[]{:S(2)}) async-start(f32[8,1,384]{2,1,0:T(1,128)} %copy.51), calls=%async_computation.12 | async-start | bytes 24576 | tf_op jit(solution)/shard_map/all_to_all | solution.py:638
  (11 other events, 7.3 us)

commit v5 on v4

--- a/solution.py
+++ b/solution.py
@@ -68,7 +68,7 @@
         self.main = 4 * self.chunk
         self.depth = shards * cells
         self.edge = cells * self.main
-        self.batch = 4 if cells % 4 == 0 else 2 if cells % 2 == 0 else 1
+        self.batch = 2 if cells % 2 == 0 else 1
         self.pad = (cells + 7) // 8 * 8
 
     def height(self, chunk):

time: 520 us -> 520 us (level)
  transfers between devices with their start and end apart: 37 -> 37, of which waited for: 25 -> 25; matrix products, arithmetic and copies ran while one was open for 5% -> 5% of each run, Pallas kernels for 42% -> 43%
where the time goes in v5:
time: 520 us; the launch traced here: 510 us
  Pallas kernels  223 us (43%)
  waiting for transfers between devices  97.6 us (19%)
  starting transfers between devices  95 us (18%)
  blocking collectives  62.2 us (12%)
  local copies, waits for them, and re-layouts  16.8 us (3%)
  other arithmetic  14 us (3%)
    pallas_call x8, Pallas kernels, sweep(): pl.pallas_call(functools.partial(sweep_kernel, plan, at, upward, groups),...  111 us
    all_to_all x2, blocking collectives, exchange(): return lax.all_to_all(array, 'gx', split_axis=0, concat_axis=0, tiled=True)  62.2 us
    pallas_call x4, Pallas kernels, send(): pl.pallas_call(functools.partial(kernel, plan, len(aliases)), grid=(plan....  61 us
    all_to_all x11, starting transfers between devices, exchange(): return lax.all_to_all(array, 'gx', split_axis=0, concat_axis=0, tiled=True)  48.9 us
    all_to_all x11, waiting for transfers between devices, exchange(): return lax.all_to_all(array, 'gx', split_axis=0, concat_axis=0, tiled=True)  42.6 us
    ppermute x12, waiting for transfers between devices, spread_targets(): lax.ppermute(turned, 'ba', [(i, (i + shift) % groups) for i in range(grou...  30.8 us
    pallas_call x4, Pallas kernels, make_aims(): pl.pallas_call(functools.partial(aims_kernel, plan, at), grid_spec=spec,...  26.3 us
    ppermute x12, starting transfers between devices, spread_targets(): lax.ppermute(turned, 'ba', [(i, (i + shift) % groups) for i in range(grou...  23.5 us
  transfers between devices with their start and end apart: 37, of which 25 were waited for; matrix products, arithmetic and copies ran while one was open for 5% of the time, Pallas kernels for 43%

profile of v5, /device:TPU:0, one launch (start us, length us, event | category | flops | bytes accessed | tf_op | source)
XLA Modules:
  0.0 510.1 jit_solution(4156436283586681302)
XLA Ops:
  0.6 4.4 mirrored.1
  5.0 3.3 collective-permute-start.1
  9.8 10.5 %into_modes.2 = (f32[8,520,128]{2,1,0:T(8,128)}, f32[8,1024,128]{2,1,0:T(8,128)}) custom-call(f32[8,4,256,256]{3,2,1,0:T(8,128)} %phi.1, bf16[256,256]{1,0:T(8,128)(2,1)} %constant.161.clone.into_h.refs_3_, bf16[256,256]{1,0:T(8,128)(2,1)} %constant.162.clone.into_l.refs_4_, bf16[512,256]{1,0:T(8,128)(2,1)} %constant.163.clone.stacked_h.refs_5_, ...), custom_call_target="tpu_custom_call" | custom-call | bytes 44280000 | tf_op jit(solution)/shard_map/into_modes/pallas_call | solution.py:260
  20.3 4.9 all-to-all-start
  26.4 5.9 %collective-permute-done.1 = f32[2,2,16,32,128]{4,3,2,1,0:T(8,128)S(1)} collective-permute-done((f32[2,2,16,32,128]{4,3,2,1,0:T(8,128)}, f32[2,2,16,32,128]{4,3,2,1,0:T(8,128)S(1)}, u32[]{:S(2)}, u32[]{:S(2)}) %collective-permute-start.1) | collective-permute-done | bytes 1048608 | tf_op jit(solution)/shard_map/ppermute | solution.py:627
  32.7 2.4 collective-permute-start.2
  35.1 2.6 collective-permute-start.3
  39.1 10.6 %into_modes.3 = (f32[8,520,128]{2,1,0:T(8,128)}, f32[8,1024,128]{2,1,0:T(8,128)}) custom-call(f32[8,4,256,256]{3,2,1,0:T(8,128)} %phi.1, bf16[256,256]{1,0:T(8,128)(2,1)} %constant.161.clone.into_h.refs_3_, bf16[256,256]{1,0:T(8,128)(2,1)} %constant.162.clone.into_l.refs_4_, ...), custom_call_target="tpu_custom_call", output_to_operand_aliasing={{1}: (5, {})} | custom-call | bytes 44280000 | tf_op jit(solution)/shard_map/into_modes/pallas_call | solution.py:260
  49.7 5.7 %collective-permute-done.3 = f32[2,16,16,128]{3,2,1,0:T(8,128)S(1)} collective-permute-done((f32[2,16,16,128]{3,2,1,0:T(8,128)S(1)}, f32[2,16,16,128]{3,2,1,0:T(8,128)S(1)}, u32[]{:S(2)}, u32[]{:S(2)}) %collective-permute-start.3) | collective-permute-done | bytes 262176 | tf_op jit(solution)/shard_map/ppermute | solution.py:634
  57.4 5.6 %all-to-all-start.1 = ((f32[8,520,128]{2,1,0:T(8,128)}), f32[8,520,128]{2,1,0:T(8,128)}, u32[]{:S(2)}, u32[]{:S(2)}) async-start(f32[8,520,128]{2,1,0:T(8,128)} %get-tuple-element.60), calls=%async_computation.1 | async-start | bytes 4259840 | tf_op jit(solution)/shard_map/all_to_all | solution.py:638
  64.1 4.3 collective-permute-start.8
  68.3 2.2 collective-permute-start.9
  71.3 2.2 pad_maximum_fusion.other
  74.1 7.0 %targets.4.refs_2_ = f32[64,2,5,8,128]{4,3,2,1,0:T(8,128)} custom-call(s32[1]{0:T(128)} %bitcast.group, f32[2,2,64,32,256]{4,3,2,1,0:T(8,128)} %own.7, f32[4,2,16,16,128]{4,3,2,1,0:T(8,128)} %pad_maximum_fusion.other, f32[8,128]{1,0:T(8,128)} %broadcast_in_dim.180.keep.refs_10_.refs_8_), custom_call_target="tpu_custom_call" | custom-call | bytes 14760000 | tf_op jit(solution)/shard_map/targets/pallas_call | solution.py:562
  81.0 7.1 %collective-permute-done.9 = f32[2,16,16,128]{3,2,1,0:T(8,128)S(1)} collective-permute-done((f32[2,16,16,128]{3,2,1,0:T(8,128)S(1)}, f32[2,16,16,128]{3,2,1,0:T(8,128)S(1)}, u32[]{:S(2)}, u32[]{:S(2)}) %collective-permute-start.9) | collective-permute-done | bytes 262176 | tf_op jit(solution)/shard_map/ppermute | solution.py:634
  88.1 2.0 all-to-all-done.1.refs_1_
  90.1 4.7 all-to-all-start.3
  99.2 14.3 %downward.4 = (f32[8,520,128]{2,1,0:T(8,128)}, f32[8,520,128]{2,1,0:T(8,128)}, f32[2,5,8,128]{3,2,1,0:T(8,128)}, f32[3,6,64,8]{3,2,1,0:T(8,128)}, f32[64,2,8,128]{3,2,1,0:T(8,128)}) custom-call(f32[8,520,128]{2,1,0:T(8,128)} %copy-done, f32[8,520,128]{2,1,0:T(8,128)} %all-to-all-done.1.refs_1_, f32[64,2,5,8,128]{4,3,2,1,0:T(8,128)} %targets.4.refs_2_, ...), custom_call_target="tpu_custom_call" | custom-call | bytes 47970000 | tf_op jit(solution)/shard_map/downward/pallas_call | solution.py:445
  113.6 4.2 collective-permute-start.5
  117.7 2.2 collective-permute-start.6
  120.1 1.9 collective-permute-done.5.refs_12_
  124.8 16.4 %upward.4 = (f32[8,1040,128]{2,1,0:T(8,128)}, f32[3,6,64,8]{3,2,1,0:T(8,128)}) custom-call(f32[8,520,128]{2,1,0:T(8,128)} %copy-done, f32[8,520,128]{2,1,0:T(8,128)} %all-to-all-done.1.refs_1_, f32[64,2,5,8,128]{4,3,2,1,0:T(8,128)} %targets.4.refs_2_, f32[2,6,9,8,128]{4,3,2,1,0:T(8,128)} %get-tuple-element.111.refs_3_, ...), custom_call_target="tpu_custom_call" | custom-call | bytes 47970000 | tf_op jit(solution)/shard_map/upward/pallas_call | solution.py:445
  141.2 2.8 all-to-all-done.3.refs_0_
  144.0 4.7 all-to-all-start.2
  149.8 4.2 collective-permute-start.14
  154.0 2.2 collective-permute-start.15
  158.5 6.2 %targets.5.refs_1_ = f32[64,2,4,8,128]{4,3,2,1,0:T(8,128)} custom-call(s32[1]{0:T(128)} %bitcast.group, f32[2,2,64,32,256]{4,3,2,1,0:T(8,128)} %own.7, f32[4,2,16,16,128]{4,3,2,1,0:T(8,128)} %pad_maximum_fusion.1.other, f32[8,128]{1,0:T(8,128)} %broadcast_in_dim.180.keep.refs_10_.refs_8_), custom_call_target="tpu_custom_call" | custom-call | bytes 14760000 | tf_op jit(solution)/shard_map/targets/pallas_call | solution.py:562
  164.7 11.8 %downward.5 = (f32[8,512,128]{2,1,0:T(8,128)}, f32[8,512,128]{2,1,0:T(8,128)}, f32[2,4,8,128]{3,2,1,0:T(8,128)}, f32[2,6,64,8]{3,2,1,0:T(8,128)}) custom-call(f32[8,1024,128]{2,1,0:T(8,128)} %all-to-all-done.3.refs_0_, f32[64,2,4,8,128]{4,3,2,1,0:T(8,128)} %targets.5.refs_1_, f32[2,6,8,8,128]{4,3,2,1,0:T(8,128)} %get-tuple-element.112.refs_2_, ...), custom_call_target="tpu_custom_call" | custom-call | bytes 47970000 | tf_op jit(solution)/shard_map/downward/pallas_call | solution.py:445
  176.5 1.8 collective-permute-start.11
  179.1 3.3 collective-permute-done.11.refs_10_
  183.4 3.2 collective-permute-done.13.refs_12_
  187.2 13.2 %upward.5 = (f32[8,512,128]{2,1,0:T(8,128)}, f32[8,512,128]{2,1,0:T(8,128)}, f32[2,6,64,8]{3,2,1,0:T(8,128)}) custom-call(f32[8,1024,128]{2,1,0:T(8,128)} %all-to-all-done.3.refs_0_, f32[64,2,4,8,128]{4,3,2,1,0:T(8,128)} %targets.5.refs_1_, f32[2,6,8,8,128]{4,3,2,1,0:T(8,128)} %get-tuple-element.113.refs_2_, ...), custom_call_target="tpu_custom_call" | custom-call | bytes 47970000 | tf_op jit(solution)/shard_map/upward/pallas_call | solution.py:445
  201.2 4.1 all-to-all-start.4
  206.4 2.2 collective-permute-start.18
  209.1 7.2 %collective-permute-done.17 = f32[2,16,16,128]{3,2,1,0:T(8,128)S(1)} collective-permute-done((f32[2,16,16,128]{3,2,1,0:T(8,128)S(1)}, f32[2,16,16,128]{3,2,1,0:T(8,128)S(1)}, u32[]{:S(2)}, u32[]{:S(2)}) %collective-permute-start.17) | collective-permute-done | bytes 262176 | tf_op jit(solution)/shard_map/ppermute | solution.py:634
  216.3 10.8 %collective-permute-done.18 = f32[2,16,16,128]{3,2,1,0:T(8,128)S(1)} collective-permute-done((f32[2,16,16,128]{3,2,1,0:T(8,128)S(1)}, f32[2,16,16,128]{3,2,1,0:T(8,128)S(1)}, u32[]{:S(2)}, u32[]{:S(2)}) %collective-permute-start.18) | collective-permute-done | bytes 262176 | tf_op jit(solution)/shard_map/ppermute | solution.py:634
  228.5 3.3 all-to-all-done.4.refs_1_
  231.9 4.4 all-to-all-start.6
  236.3 19.9 %between_steps.2 = (f32[8,520,128]{2,1,0:T(8,128)}, f32[8,1024,128]{2,1,0:T(8,128)}) custom-call(f32[8,1040,128]{2,1,0:T(8,128)} %all-to-all-done.2.refs_0_, f32[8,512,128]{2,1,0:T(8,128)} %copy-done.3, f32[8,256,256]{2,1,0:T(8,128)} %refs_2_.7, bf16[256,256]{1,0:T(8,128)(2,1)} %constant.161.clone.into_h.refs_3_, ...), custom_call_target="tpu_custom_call" | custom-call | bytes 92250000 | tf_op jit(solution)/shard_map/between_steps/pallas_call | solution.py:260
  256.2 6.7 %all-to-all-done.6.refs_1_ = f32[8,512,128]{2,1,0:T(8,128)} async-done(((f32[8,512,128]{2,1,0:T(8,128)}), f32[8,512,128]{2,1,0:T(8,128)}, u32[]{:S(2)}, u32[]{:S(2)}) %all-to-all-start.6) | async-done | bytes 2097184 | tf_op jit(solution)/shard_map/all_to_all | solution.py:638
  262.9 3.6 all-to-all-start.5
  266.5 19.9 %between_steps.3 = (f32[8,520,128]{2,1,0:T(8,128)}, f32[8,1024,128]{2,1,0:T(8,128)}) custom-call(f32[8,1040,128]{2,1,0:T(8,128)} %all-to-all-done.2.refs_0_, f32[8,512,128]{2,1,0:T(8,128)} %all-to-all-done.6.refs_1_, f32[8,256,256]{2,1,0:T(8,128)} %refs_2_.7, bf16[256,256]{1,0:T(8,128)(2,1)} %constant.161.clone.into_h.refs_3_, ...), custom_call_target="tpu_custom_call", output_to_operand_aliasing={{1}: (11, {})} | custom-call | bytes 92250000 | tf_op jit(solution)/shard_map/between_steps/pallas_call | solution.py:260
  286.5 7.0 %all-to-all-done.5.refs_0_ = f32[8,520,128]{2,1,0:T(8,128)S(1)} async-done(((f32[8,520,128]{2,1,0:T(8,128)}), f32[8,520,128]{2,1,0:T(8,128)S(1)}, u32[]{:S(2)}, u32[]{:S(2)}) %all-to-all-start.5) | async-done | bytes 2129952 | tf_op jit(solution)/shard_map/all_to_all | solution.py:638
  293.5 31.3 %all_to_all.69.refs_1_ = f32[8,520,128]{2,1,0:T(8,128)} all-to-all(f32[8,520,128]{2,1,0:T(8,128)} %get-tuple-element.80), channel_id=1, replica_groups=mesh['gx'=8,'ba'=4] {'gx'}, dimensions={0} | all-to-all | bytes 4259840 | tf_op jit(solution)/shard_map/all_to_all | solution.py:638
  324.8 4.9 all-to-all-start.9
  330.8 7.0 %targets.6.refs_2_ = f32[64,2,5,8,128]{4,3,2,1,0:T(8,128)} custom-call(s32[1]{0:T(128)} %bitcast.group, f32[2,2,64,32,256]{4,3,2,1,0:T(8,128)} %own.7, f32[4,2,16,16,128]{4,3,2,1,0:T(8,128)} %pad_maximum_fusion.2.other, f32[8,128]{1,0:T(8,128)} %broadcast_in_dim.180.keep.refs_10_.refs_8_), custom_call_target="tpu_custom_call" | custom-call | bytes 14760000 | tf_op jit(solution)/shard_map/targets/pallas_call | solution.py:562
  337.8 14.3 %downward.6 = (f32[8,520,128]{2,1,0:T(8,128)}, f32[8,520,128]{2,1,0:T(8,128)}, f32[2,5,8,128]{3,2,1,0:T(8,128)}, f32[3,6,64,8]{3,2,1,0:T(8,128)}, f32[64,2,8,128]{3,2,1,0:T(8,128)}) custom-call(f32[8,520,128]{2,1,0:T(8,128)} %copy-done.1, f32[8,520,128]{2,1,0:T(8,128)} %all_to_all.69.refs_1_, f32[64,2,5,8,128]{4,3,2,1,0:T(8,128)} %targets.6.refs_2_, ...), custom_call_target="tpu_custom_call" | custom-call | bytes 47970000 | tf_op jit(solution)/shard_map/downward/pallas_call | solution.py:445
  352.1 1.9 collective-permute-start.20
  356.4 2.1 collective-permute-done.20.refs_12_
  360.7 16.4 %upward.6 = (f32[8,1040,128]{2,1,0:T(8,128)}, f32[3,6,64,8]{3,2,1,0:T(8,128)}) custom-call(f32[8,520,128]{2,1,0:T(8,128)} %copy-done.1, f32[8,520,128]{2,1,0:T(8,128)} %all_to_all.69.refs_1_, f32[64,2,5,8,128]{4,3,2,1,0:T(8,128)} %targets.6.refs_2_, f32[2,6,9,8,128]{4,3,2,1,0:T(8,128)} %get-tuple-element.111.refs_3_, ...), custom_call_target="tpu_custom_call" | custom-call | bytes 47970000 | tf_op jit(solution)/shard_map/upward/pallas_call | solution.py:445
  377.1 1.7 all-to-all-done.9.refs_0_
  378.8 4.7 all-to-all-start.8
  384.6 6.2 %targets.7.refs_1_ = f32[64,2,4,8,128]{4,3,2,1,0:T(8,128)} custom-call(s32[1]{0:T(128)} %bitcast.group, f32[2,2,64,32,256]{4,3,2,1,0:T(8,128)} %own.7, f32[4,2,16,16,128]{4,3,2,1,0:T(8,128)} %pad_maximum_fusion.3.other, f32[8,128]{1,0:T(8,128)} %broadcast_in_dim.180.keep.refs_10_.refs_8_), custom_call_target="tpu_custom_call" | custom-call | bytes 14760000 | tf_op jit(solution)/shard_map/targets/pallas_call | solution.py:562
  390.8 11.9 %downward.7 = (f32[8,512,128]{2,1,0:T(8,128)}, f32[8,512,128]{2,1,0:T(8,128)}, f32[2,4,8,128]{3,2,1,0:T(8,128)}, f32[2,6,64,8]{3,2,1,0:T(8,128)}) custom-call(f32[8,1024,128]{2,1,0:T(8,128)} %all-to-all-done.9.refs_0_, f32[64,2,4,8,128]{4,3,2,1,0:T(8,128)} %targets.7.refs_1_, f32[2,6,8,8,128]{4,3,2,1,0:T(8,128)} %get-tuple-element.112.refs_2_, ...), custom_call_target="tpu_custom_call" | custom-call | bytes 47970000 | tf_op jit(solution)/shard_map/downward/pallas_call | solution.py:445
  402.7 1.9 collective-permute-start.23
  406.9 2.0 collective-permute-done.23.refs_10_
  410.8 13.1 %upward.7 = (f32[8,512,128]{2,1,0:T(8,128)}, f32[8,512,128]{2,1,0:T(8,128)}, f32[2,6,64,8]{3,2,1,0:T(8,128)}) custom-call(f32[8,1024,128]{2,1,0:T(8,128)} %all-to-all-done.9.refs_0_, f32[64,2,4,8,128]{4,3,2,1,0:T(8,128)} %targets.7.refs_1_, f32[2,6,8,8,128]{4,3,2,1,0:T(8,128)} %get-tuple-element.113.refs_2_, ...), custom_call_target="tpu_custom_call" | custom-call | bytes 47970000 | tf_op jit(solution)/shard_map/upward/pallas_call | solution.py:445
  423.9 9.4 %all-to-all-done.8.refs_0_ = f32[8,1040,128]{2,1,0:T(8,128)} async-done(((f32[8,1040,128]{2,1,0:T(8,128)}), f32[8,1040,128]{2,1,0:T(8,128)}, u32[]{:S(2)}, u32[]{:S(2)}) %all-to-all-start.8) | async-done | bytes 4259872 | tf_op jit(solution)/shard_map/all_to_all | solution.py:638
  433.3 30.9 %all_to_all.70.refs_1_ = f32[8,512,128]{2,1,0:T(8,128)} all-to-all(f32[8,512,128]{2,1,0:T(8,128)} %get-tuple-element.93), channel_id=1, replica_groups=mesh['gx'=8,'ba'=4] {'gx'}, dimensions={0} | all-to-all | bytes 4194304 | tf_op jit(solution)/shard_map/all_to_all | solution.py:638
  464.3 4.0 all-to-all-start.11
  475.2 10.0 %out_of_modes.2.refs_7_ = f32[8,4,256,256]{3,2,1,0:T(8,128)} custom-call(f32[8,1040,128]{2,1,0:T(8,128)} %all-to-all-done.8.refs_0_, f32[8,512,128]{2,1,0:T(8,128)} %all_to_all.70.refs_1_, f32[8,256,256]{2,1,0:T(8,128)} %refs_2_.7, bf16[256,512]{1,0:T(8,128)(2,1)} %constant.165.clone.refs_7_.refs_3_, bf16[256,512]{1,0:T(8,128)(2,1)} %constant.166.clone.refs_8_.refs_4_, ...), custom_call_target="tpu_custom_call" | custom-call | bytes 59040000 | tf_op jit(solution)/shard_map/out_of_modes/pallas_call | solution.py:293
  485.2 9.6 %all-to-all-done.11.refs_1_ = f32[8,512,128]{2,1,0:T(8,128)S(1)} async-done(((f32[8,512,128]{2,1,0:T(8,128)}), f32[8,512,128]{2,1,0:T(8,128)S(1)}, u32[]{:S(2)}, u32[]{:S(2)}) %all-to-all-start.11) | async-done | bytes 2097184 | tf_op jit(solution)/shard_map/all_to_all | solution.py:638
  495.5 3.3 all-to-all-start.12
  498.9 10.0 %out_of_modes.3 = f32[8,4,256,256]{3,2,1,0:T(8,128)} custom-call(f32[8,1040,128]{2,1,0:T(8,128)} %all-to-all-done.8.refs_0_, f32[8,512,128]{2,1,0:T(8,128)} %copy-done.2, f32[8,256,256]{2,1,0:T(8,128)} %refs_2_.7, bf16[256,512]{1,0:T(8,128)(2,1)} %constant.165.clone.refs_7_.refs_3_, ...), custom_call_target="tpu_custom_call", output_to_operand_aliasing={{}: (7, {})} | custom-call | bytes 59040000 | tf_op jit(solution)/shard_map/out_of_modes/pallas_call | solution.py:293
  (219 shorter events, 45.2 us)
Async XLA Ops:
  5.0 27.2 %collective-permute-start.1 = (f32[2,2,16,32,128]{4,3,2,1,0:T(8,128)}, f32[2,2,16,32,128]{4,3,2,1,0:T(8,128)S(1)}, u32[]{:S(2)}, u32[]{:S(2)}) collective-permute-start(f32[2,2,16,32,128]{4,3,2,1,0:T(8,128)} %get-tuple-element.53), channel_id=1, source_target_pairs={{0,28},{4,24},{8,20},{12,16},{16,12},{20,8},{24,4},{28,0},{1,29},{... | collective-permute-start | bytes 3145736 | tf_op jit(solution)/shard_map/ppermute | solution.py:627
  8.4 18.0 %collective-permute-start = (f32[2,2,16,128]{3,2,1,0:T(8,128)}, f32[2,2,16,128]{3,2,1,0:T(8,128)S(1)}, u32[]{:S(2)}, u32[]{:S(2)}) collective-permute-start(f32[2,2,16,128]{3,2,1,0:T(8,128)} %get-tuple-element.54), channel_id=1, source_target_pairs={{0,0},{4,28},{8,24},{12,20},{16,16},{20,12},{24,8},{28,4},{1,1},{5... | collective-permute-start | bytes 98312 | tf_op jit(solution)/shard_map/ppermute | solution.py:628
  20.3 4.9 copy-start.31
  20.3 5.8 %copy-start.32 = (f32[4]{0:T(128)S(1)}, f32[4]{0:T(128)}, u32[]{:S(2)}) copy-start(f32[4]{0:T(128)} %param.26) | copy-start | bytes 52
  20.3 35.8 %all-to-all-start = ((f32[8,520,128]{2,1,0:T(8,128)}), f32[8,520,128]{2,1,0:T(8,128)S(1)}, u32[]{:S(2)}, u32[]{:S(2)}) async-start(f32[8,520,128]{2,1,0:T(8,128)} %get-tuple-element.56), calls=%async_computation | async-start | bytes 4259840 | tf_op jit(solution)/shard_map/all_to_all | solution.py:638
  32.7 17.0 %collective-permute-start.2 = (f32[2,16,16,128]{3,2,1,0:T(8,128)S(1)}, f32[2,16,16,128]{3,2,1,0:T(8,128)S(1)}, u32[]{:S(2)}, u32[]{:S(2)}) collective-permute-start(f32[2,16,16,128]{3,2,1,0:T(8,128)S(1)} %get-tuple-element.121), channel_id=1, source_target_pairs={{0,1},{1,2},{2,3},{3,0},{4,5},{5,6},{6,7},{7,4},{8,9},{9,10},{10,1... | collective-permute-start | bytes 786440 | tf_op jit(solution)/shard_map/ppermute | solution.py:634
  35.1 20.3 %collective-permute-start.3 = (f32[2,16,16,128]{3,2,1,0:T(8,128)S(1)}, f32[2,16,16,128]{3,2,1,0:T(8,128)S(1)}, u32[]{:S(2)}, u32[]{:S(2)}) collective-permute-start(f32[2,16,16,128]{3,2,1,0:T(8,128)S(1)} %get-tuple-element.121), channel_id=1, source_target_pairs={{0,2},{1,3},{2,0},{3,1},{4,6},{5,7},{6,4},{7,5},{8,10},{9,11},{10,... | collective-permute-start | bytes 786440 | tf_op jit(solution)/shard_map/ppermute | solution.py:634
  37.7 18.4 %collective-permute-start.4 = (f32[2,16,16,128]{3,2,1,0:T(8,128)S(1)}, f32[2,16,16,128]{3,2,1,0:T(8,128)}, u32[]{:S(2)}, u32[]{:S(2)}) collective-permute-start(f32[2,16,16,128]{3,2,1,0:T(8,128)S(1)} %get-tuple-element.121), channel_id=1, source_target_pairs={{0,3},{1,0},{2,1},{3,2},{4,7},{5,4},{6,5},{7,6},{8,11},{9,8},{10,9... | collective-permute-start | bytes 786440 | tf_op jit(solution)/shard_map/ppermute | solution.py:634
  49.7 5.7 %copy-start.7 = (f32[2,16,16,128]{3,2,1,0:T(8,128)}, f32[2,16,16,128]{3,2,1,0:T(8,128)S(1)}, u32[]{:S(2)}) copy-start(f32[2,16,16,128]{3,2,1,0:T(8,128)S(1)} %collective-permute-done.2) | copy-start | bytes 786436
  56.1 1.3 copy-start
  57.4 32.7 %all-to-all-start.1 = ((f32[8,520,128]{2,1,0:T(8,128)}), f32[8,520,128]{2,1,0:T(8,128)}, u32[]{:S(2)}, u32[]{:S(2)}) async-start(f32[8,520,128]{2,1,0:T(8,128)} %get-tuple-element.60), calls=%async_computation.1 | async-start | bytes 4259840 | tf_op jit(solution)/shard_map/all_to_all | solution.py:638
  64.1 17.0 %collective-permute-start.8 = (f32[2,16,16,128]{3,2,1,0:T(8,128)S(1)}, f32[2,16,16,128]{3,2,1,0:T(8,128)S(1)}, u32[]{:S(2)}, u32[]{:S(2)}) collective-permute-start(f32[2,16,16,128]{3,2,1,0:T(8,128)S(1)} %get-tuple-element.120), channel_id=1, source_target_pairs={{0,1},{1,2},{2,3},{3,0},{4,5},{5,6},{6,7},{7,4},{8,9},{9,10},{10,1... | collective-permute-start | bytes 786440 | tf_op jit(solution)/shard_map/ppermute | solution.py:634
  68.3 19.8 %collective-permute-start.9 = (f32[2,16,16,128]{3,2,1,0:T(8,128)S(1)}, f32[2,16,16,128]{3,2,1,0:T(8,128)S(1)}, u32[]{:S(2)}, u32[]{:S(2)}) collective-permute-start(f32[2,16,16,128]{3,2,1,0:T(8,128)S(1)} %get-tuple-element.120), channel_id=1, source_target_pairs={{0,2},{1,3},{2,0},{3,1},{4,6},{5,7},{6,4},{7,5},{8,10},{9,11},{10,... | collective-permute-start | bytes 786440 | tf_op jit(solution)/shard_map/ppermute | solution.py:634
  70.5 17.6 %collective-permute-start.10 = (f32[2,16,16,128]{3,2,1,0:T(8,128)S(1)}, f32[2,16,16,128]{3,2,1,0:T(8,128)S(1)}, u32[]{:S(2)}, u32[]{:S(2)}) collective-permute-start(f32[2,16,16,128]{3,2,1,0:T(8,128)S(1)} %get-tuple-element.120), channel_id=1, source_target_pairs={{0,3},{1,0},{2,1},{3,2},{4,7},{5,4},{6,5},{7,6},{8,11},{9,8},{10,9... | collective-permute-start | bytes 786440 | tf_op jit(solution)/shard_map/ppermute | solution.py:634
  90.1 5.1 %copy-start.37 = (f32[4]{0:T(128)S(1)}, f32[4]{0:T(128)}, u32[]{:S(2)}) copy-start(f32[4]{0:T(128)} %param.28) | copy-start | bytes 52
  90.1 6.4 %copy-start.33 = (f32[12]{0:T(128)S(1)}, f32[12]{0:T(128)}, u32[]{:S(2)}) copy-start(f32[12]{0:T(128)} %constant.177) | copy-start | bytes 148
  90.1 6.4 %copy-start.34 = (f32[12]{0:T(128)S(1)}, f32[12]{0:T(128)}, u32[]{:S(2)}) copy-start(f32[12]{0:T(128)} %constant.176) | copy-start | bytes 148
  90.1 6.4 %copy-start.35 = (f32[12]{0:T(128)S(1)}, f32[12]{0:T(128)}, u32[]{:S(2)}) copy-start(f32[12]{0:T(128)} %constant.175) | copy-start | bytes 148
  90.1 53.9 %all-to-all-start.3 = ((f32[8,1024,128]{2,1,0:T(8,128)}), f32[8,1024,128]{2,1,0:T(8,128)}, u32[]{:S(2)}, u32[]{:S(2)}) async-start(f32[8,1024,128]{2,1,0:T(8,128)} %get-tuple-element.67), calls=%async_computation.3 | async-start | bytes 8388608 | tf_op jit(solution)/shard_map/all_to_all | solution.py:638
  94.9 3.0 copy-start.36
  113.6 8.5 %collective-permute-start.5 = (f32[2,5,8,128]{3,2,1,0:T(8,128)}, f32[2,5,8,128]{3,2,1,0:T(8,128)S(1)}, u32[]{:S(2)}, u32[]{:S(2)}) collective-permute-start(f32[2,5,8,128]{3,2,1,0:T(8,128)} %get-tuple-element.64.refs_11_), channel_id=1, source_target_pairs={{0,1},{1,2},{2,3},{3,0},{4,5},{5,6},{6,7},{7,4},{8,9},{9,10},{10,1... | collective-permute-start | bytes 122888 | tf_op jit(solution)/shard_map/ppermute | solution.py:692
  117.7 5.8 %collective-permute-start.6 = (f32[2,5,8,128]{3,2,1,0:T(8,128)}, f32[2,5,8,128]{3,2,1,0:T(8,128)S(1)}, u32[]{:S(2)}, u32[]{:S(2)}) collective-permute-start(f32[2,5,8,128]{3,2,1,0:T(8,128)} %get-tuple-element.64.refs_11_), channel_id=1, source_target_pairs={{0,2},{1,3},{2,0},{3,1},{4,6},{5,7},{6,4},{7,5},{8,10},{9,11},{10,... | collective-permute-start | bytes 122888 | tf_op jit(solution)/shard_map/ppermute | solution.py:692
  119.9 4.2 collective-permute-start.7
  122.0 2.8 copy-start.19
  123.5 1.3 copy-start.20
  144.0 56.4 %all-to-all-start.2 = ((f32[8,1040,128]{2,1,0:T(8,128)}), f32[8,1040,128]{2,1,0:T(8,128)}, u32[]{:S(2)}, u32[]{:S(2)}) async-start(f32[8,1040,128]{2,1,0:T(8,128)} %get-tuple-element.65), calls=%async_computation.2 | async-start | bytes 8519680 | tf_op jit(solution)/shard_map/all_to_all | solution.py:638
  149.8 50.5 %collective-permute-start.14 = (f32[2,16,16,128]{3,2,1,0:T(8,128)S(1)}, f32[2,16,16,128]{3,2,1,0:T(8,128)S(1)}, u32[]{:S(2)}, u32[]{:S(2)}) collective-permute-start(f32[2,16,16,128]{3,2,1,0:T(8,128)S(1)} %get-tuple-element.117), channel_id=1, source_target_pairs={{0,1},{1,2},{2,3},{3,0},{4,5},{5,6},{6,7},{7,4},{8,9},{9,10},{10,1... | collective-permute-start | bytes 786440 | tf_op jit(solution)/shard_map/ppermute | solution.py:634
  154.0 46.3 %collective-permute-start.15 = (f32[2,16,16,128]{3,2,1,0:T(8,128)S(1)}, f32[2,16,16,128]{3,2,1,0:T(8,128)S(1)}, u32[]{:S(2)}, u32[]{:S(2)}) collective-permute-start(f32[2,16,16,128]{3,2,1,0:T(8,128)S(1)} %get-tuple-element.117), channel_id=1, source_target_pairs={{0,2},{1,3},{2,0},{3,1},{4,6},{5,7},{6,4},{7,5},{8,10},{9,11},{10,... | collective-permute-start | bytes 786440 | tf_op jit(solution)/shard_map/ppermute | solution.py:634
  156.2 44.2 %collective-permute-start.16 = (f32[2,16,16,128]{3,2,1,0:T(8,128)S(1)}, f32[2,16,16,128]{3,2,1,0:T(8,128)S(1)}, u32[]{:S(2)}, u32[]{:S(2)}) collective-permute-start(f32[2,16,16,128]{3,2,1,0:T(8,128)S(1)} %get-tuple-element.117), channel_id=1, source_target_pairs={{0,3},{1,0},{2,1},{3,2},{4,7},{5,4},{6,5},{7,6},{8,11},{9,8},{10,9... | collective-permute-start | bytes 786440 | tf_op jit(solution)/shard_map/ppermute | solution.py:634
  176.5 5.9 %collective-permute-start.11 = (f32[2,4,8,128]{3,2,1,0:T(8,128)}, f32[2,4,8,128]{3,2,1,0:T(8,128)S(1)}, u32[]{:S(2)}, u32[]{:S(2)}) collective-permute-start(f32[2,4,8,128]{3,2,1,0:T(8,128)} %get-tuple-element.70.refs_9_), channel_id=1, source_target_pairs={{0,1},{1,2},{2,3},{3,0},{4,5},{5,6},{6,7},{7,4},{8,9},{9,10},{10,1... | collective-permute-start | bytes 98312 | tf_op jit(solution)/shard_map/ppermute | solution.py:692
  178.4 5.0 collective-permute-start.12
  182.4 4.1 copy-start.27
  182.4 4.1 collective-permute-start.13
  183.4 3.2 copy-start.29
  200.3 4.9 copy-start.6
  201.2 30.7 %all-to-all-start.4 = ((f32[8,512,128]{2,1,0:T(8,128)}), f32[8,512,128]{2,1,0:T(8,128)S(1)}, u32[]{:S(2)}, u32[]{:S(2)}) async-start(f32[8,512,128]{2,1,0:T(8,128)} %get-tuple-element.73), calls=%async_computation.4 | async-start | bytes 4194304 | tf_op jit(solution)/shard_map/all_to_all | solution.py:638
  205.2 11.1 %collective-permute-start.17 = (f32[2,16,16,128]{3,2,1,0:T(8,128)S(1)}, f32[2,16,16,128]{3,2,1,0:T(8,128)S(1)}, u32[]{:S(2)}, u32[]{:S(2)}) collective-permute-start(f32[2,16,16,128]{3,2,1,0:T(8,128)S(1)} %copy-done.6), channel_id=1, source_target_pairs={{0,1},{1,2},{2,3},{3,0},{4,5},{5,6},{6,7},{7,4},{8,9},{9,10},{10,1... | collective-permute-start | bytes 786440 | tf_op jit(solution)/shard_map/ppermute | solution.py:634
  206.4 20.7 %collective-permute-start.18 = (f32[2,16,16,128]{3,2,1,0:T(8,128)S(1)}, f32[2,16,16,128]{3,2,1,0:T(8,128)S(1)}, u32[]{:S(2)}, u32[]{:S(2)}) collective-permute-start(f32[2,16,16,128]{3,2,1,0:T(8,128)S(1)} %copy-done.6), channel_id=1, source_target_pairs={{0,2},{1,3},{2,0},{3,1},{4,6},{5,7},{6,4},{7,5},{8,10},{9,11},{10,... | collective-permute-start | bytes 786440 | tf_op jit(solution)/shard_map/ppermute | solution.py:634
  208.6 18.5 %collective-permute-start.19 = (f32[2,16,16,128]{3,2,1,0:T(8,128)S(1)}, f32[2,16,16,128]{3,2,1,0:T(8,128)S(1)}, u32[]{:S(2)}, u32[]{:S(2)}) collective-permute-start(f32[2,16,16,128]{3,2,1,0:T(8,128)S(1)} %copy-done.6), channel_id=1, source_target_pairs={{0,3},{1,0},{2,1},{3,2},{4,7},{5,4},{6,5},{7,6},{8,11},{9,8},{10,9... | collective-permute-start | bytes 786440 | tf_op jit(solution)/shard_map/ppermute | solution.py:634
  216.3 39.8 %copy-start.13 = (f32[2,16,16,128]{3,2,1,0:T(8,128)}, f32[2,16,16,128]{3,2,1,0:T(8,128)S(1)}, u32[]{:S(2)}) copy-start(f32[2,16,16,128]{3,2,1,0:T(8,128)S(1)} %collective-permute-done.17) | copy-start | bytes 786436
  231.9 4.4 copy-start.3
  231.9 31.0 %all-to-all-start.6 = ((f32[8,512,128]{2,1,0:T(8,128)}), f32[8,512,128]{2,1,0:T(8,128)}, u32[]{:S(2)}, u32[]{:S(2)}) async-start(f32[8,512,128]{2,1,0:T(8,128)} %get-tuple-element.77), calls=%async_computation.6 | async-start | bytes 4194304 | tf_op jit(solution)/shard_map/all_to_all | solution.py:638
  262.9 30.5 %all-to-all-start.5 = ((f32[8,520,128]{2,1,0:T(8,128)}), f32[8,520,128]{2,1,0:T(8,128)S(1)}, u32[]{:S(2)}, u32[]{:S(2)}) async-start(f32[8,520,128]{2,1,0:T(8,128)} %get-tuple-element.74), calls=%async_computation.5 | async-start | bytes 4259840 | tf_op jit(solution)/shard_map/all_to_all | solution.py:638
  293.5 31.3 %copy-start.1 = (f32[8,520,128]{2,1,0:T(8,128)}, f32[8,520,128]{2,1,0:T(8,128)S(1)}, u32[]{:S(2)}) copy-start(f32[8,520,128]{2,1,0:T(8,128)S(1)} %all-to-all-done.5.refs_0_) | copy-start | bytes 6389764
  324.8 4.9 copy-start.10
  324.8 4.9 copy-start.12
  324.8 54.0 %all-to-all-start.9 = ((f32[8,1024,128]{2,1,0:T(8,128)}), f32[8,1024,128]{2,1,0:T(8,128)}, u32[]{:S(2)}, u32[]{:S(2)}) async-start(f32[8,1024,128]{2,1,0:T(8,128)} %get-tuple-element.87), calls=%async_computation.9 | async-start | bytes 8388608 | tf_op jit(solution)/shard_map/all_to_all | solution.py:638
  352.1 6.4 %collective-permute-start.20 = (f32[2,5,8,128]{3,2,1,0:T(8,128)}, f32[2,5,8,128]{3,2,1,0:T(8,128)S(1)}, u32[]{:S(2)}, u32[]{:S(2)}) collective-permute-start(f32[2,5,8,128]{3,2,1,0:T(8,128)} %get-tuple-element.84.refs_11_), channel_id=1, source_target_pairs={{0,1},{1,2},{2,3},{3,0},{4,5},{5,6},{6,7},{7,4},{8,9},{9,10},{10,1... | collective-permute-start | bytes 122888 | tf_op jit(solution)/shard_map/ppermute | solution.py:692
  354.0 5.8 %collective-permute-start.21 = (f32[2,5,8,128]{3,2,1,0:T(8,128)}, f32[2,5,8,128]{3,2,1,0:T(8,128)S(1)}, u32[]{:S(2)}, u32[]{:S(2)}) collective-permute-start(f32[2,5,8,128]{3,2,1,0:T(8,128)} %get-tuple-element.84.refs_11_), channel_id=1, source_target_pairs={{0,2},{1,3},{2,0},{3,1},{4,6},{5,7},{6,4},{7,5},{8,10},{9,11},{10,... | collective-permute-start | bytes 122888 | tf_op jit(solution)/shard_map/ppermute | solution.py:692
  355.3 4.8 collective-permute-start.22
  358.4 1.7 copy-start.21
  378.8 4.7 copy-start.14
  378.8 4.7 copy-start.16
  378.8 4.7 copy-start.18
  378.8 54.5 %all-to-all-start.8 = ((f32[8,1040,128]{2,1,0:T(8,128)}), f32[8,1040,128]{2,1,0:T(8,128)}, u32[]{:S(2)}, u32[]{:S(2)}) async-start(f32[8,1040,128]{2,1,0:T(8,128)} %get-tuple-element.85), calls=%async_computation.8 | async-start | bytes 8519680 | tf_op jit(solution)/shard_map/all_to_all | solution.py:638
  402.7 6.2 %collective-permute-start.23 = (f32[2,4,8,128]{3,2,1,0:T(8,128)}, f32[2,4,8,128]{3,2,1,0:T(8,128)S(1)}, u32[]{:S(2)}, u32[]{:S(2)}) collective-permute-start(f32[2,4,8,128]{3,2,1,0:T(8,128)} %get-tuple-element.90.refs_9_), channel_id=1, source_target_pairs={{0,1},{1,2},{2,3},{3,0},{4,5},{5,6},{6,7},{7,4},{8,9},{9,10},{10,1... | collective-permute-start | bytes 98312 | tf_op jit(solution)/shard_map/ppermute | solution.py:692
  404.6 5.4 %collective-permute-start.24 = (f32[2,4,8,128]{3,2,1,0:T(8,128)}, f32[2,4,8,128]{3,2,1,0:T(8,128)S(1)}, u32[]{:S(2)}, u32[]{:S(2)}) collective-permute-start(f32[2,4,8,128]{3,2,1,0:T(8,128)} %get-tuple-element.90.refs_9_), channel_id=1, source_target_pairs={{0,2},{1,3},{2,0},{3,1},{4,6},{5,7},{6,4},{7,5},{8,10},{9,11},{10,... | collective-permute-start | bytes 98312 | tf_op jit(solution)/shard_map/ppermute | solution.py:692
  405.9 4.2 collective-permute-start.25
  408.9 1.3 copy-start.25
  464.3 4.0 copy-start.4
  464.3 6.3 %copy-start.5 = (f32[2,6,64,8]{3,2,1,0:T(8,128)S(1)}, f32[2,6,64,8]{3,2,1,0:T(8,128)}, u32[]{:S(2)}) copy-start(f32[2,6,64,8]{3,2,1,0:T(8,128)} %get-tuple-element.96) | copy-start | bytes 73732
  464.3 30.6 %all-to-all-start.11 = ((f32[8,512,128]{2,1,0:T(8,128)}), f32[8,512,128]{2,1,0:T(8,128)S(1)}, u32[]{:S(2)}, u32[]{:S(2)}) async-start(f32[8,512,128]{2,1,0:T(8,128)} %get-tuple-element.94), calls=%async_computation.11 | async-start | bytes 4194304 | tf_op jit(solution)/shard_map/all_to_all | solution.py:638
  494.8 4.0 copy-start.2
  495.5 13.3 %all-to-all-start.12 = ((f32[8,1,384]{2,1,0:T(1,128)}), f32[8,1,384]{2,1,0:T(1,128)S(1)}, u32[]{:S(2)}, u32[]{:S(2)}) async-start(f32[8,1,384]{2,1,0:T(1,128)} %copy.51), calls=%async_computation.12 | async-start | bytes 24576 | tf_op jit(solution)/shard_map/all_to_all | solution.py:638
  (11 other events, 7.3 us)

commit v6 on v5

--- a/solution.py
+++ b/solution.py
@@ -59,7 +59,7 @@
 
 
 class Plan:
-    def __init__(self, shards, cells, width, rows):
+    def __init__(self, shards, cells, width, rows, batch=1):
         self.shards, self.cells, self.width, self.rows = shards, cells, width, rows
         self.half = width // 2
         self.chunk = min(CHUNK_ROWS, rows)
@@ -68,7 +68,7 @@
         self.main = 4 * self.chunk
         self.depth = shards * cells
         self.edge = cells * self.main
-        self.batch = 2 if cells % 2 == 0 else 1
+        self.batch = batch
         self.pad = (cells + 7) // 8 * 8
 
     def height(self, chunk):
@@ -611,6 +611,7 @@
     rows = forward.shape[3]
     steps = forward.shape[0]
     plan = Plan(shards, cells, width, rows)
+    wide = Plan(shards, cells, width, rows, 2 if cells % 2 == 0 else 1)
     depth = plan.depth
     consts = [jnp.asarray(part) for part in tables(width)]
     owner = place * rows == plan.half
@@ -701,8 +702,8 @@
         if step + 1 < steps:
             sent = into(lambda side, held: middle(plan, side, ends[side], coeff, consts, held))
         else:
-            upper = last(plan, 0, ends[0], coeff, consts, None)
-            phi = last(plan, 1, ends[1], coeff, consts, upper)
+            upper = last(wide, 0, ends[0], coeff, consts, None)
+            phi = last(wide, 1, ends[1], coeff, consts, upper)
 
     grads = []
     for way in range(2):

time: 520 us -> 511 us (0.983); the launches traced: 510 us -> 509 us
  transfers between devices with their start and end apart: 37 -> 37, of which waited for: 25 -> 25; matrix products, arithmetic and copies ran while one was open for 5% -> 5% of each run, Pallas kernels for 43% -> 44%
where the time goes in v6:
time: 511 us; the launch traced here: 509 us
  Pallas kernels  226 us (44%)
  waiting for transfers between devices  96.7 us (19%)
  starting transfers between devices  91.8 us (18%)
  blocking collectives  62.2 us (12%)
  local copies, waits for them, and re-layouts  16.8 us (3%)
  other arithmetic  14 us (3%)
    pallas_call x8, Pallas kernels, sweep(): pl.pallas_call(functools.partial(sweep_kernel, plan, at, upward, groups),...  111 us
    pallas_call x4, Pallas kernels, send(): pl.pallas_call(functools.partial(kernel, plan, len(aliases)), grid=(plan....  64.4 us
    all_to_all x2, blocking collectives, exchange(): return lax.all_to_all(array, 'gx', split_axis=0, concat_axis=0, tiled=True)  62.2 us
    all_to_all x11, starting transfers between devices, exchange(): return lax.all_to_all(array, 'gx', split_axis=0, concat_axis=0, tiled=True)  49.5 us
    all_to_all x11, waiting for transfers between devices, exchange(): return lax.all_to_all(array, 'gx', split_axis=0, concat_axis=0, tiled=True)  44.7 us
    ppermute x12, waiting for transfers between devices, spread_targets(): lax.ppermute(turned, 'ba', [(i, (i + shift) % groups) for i in range(grou...  29.3 us
    pallas_call x4, Pallas kernels, make_aims(): pl.pallas_call(functools.partial(aims_kernel, plan, at), grid_spec=spec,...  26.3 us
    ppermute x12, starting transfers between devices, spread_targets(): lax.ppermute(turned, 'ba', [(i, (i + shift) % groups) for i in range(grou...  20.9 us
  transfers between devices with their start and end apart: 37, of which 25 were waited for; matrix products, arithmetic and copies ran while one was open for 5% of the time, Pallas kernels for 44%

profile of v6, /device:TPU:0, one launch (start us, length us, event | category | flops | bytes accessed | tf_op | source)
XLA Modules:
  0.0 509.1 jit_solution(3042857094466691951)
XLA Ops:
  0.6 4.4 mirrored.1
  5.0 3.3 collective-permute-start.1
  9.8 12.0 %into_modes.2 = (f32[8,520,128]{2,1,0:T(8,128)}, f32[8,1024,128]{2,1,0:T(8,128)}) custom-call(f32[8,4,256,256]{3,2,1,0:T(8,128)} %phi.1, bf16[256,256]{1,0:T(8,128)(2,1)} %constant.161.clone.into_h.refs_3_, bf16[256,256]{1,0:T(8,128)(2,1)} %constant.162.clone.into_l.refs_4_, bf16[512,256]{1,0:T(8,128)(2,1)} %constant.163.clone.stacked_h.refs_5_, ...), custom_call_target="tpu_custom_call" | custom-call | bytes 44280000 | tf_op jit(solution)/shard_map/into_modes/pallas_call | solution.py:260
  21.8 4.9 all-to-all-start
  27.9 4.4 collective-permute-done.1
  32.7 2.4 collective-permute-start.2
  35.1 2.6 collective-permute-start.3
  39.1 12.1 %into_modes.3 = (f32[8,520,128]{2,1,0:T(8,128)}, f32[8,1024,128]{2,1,0:T(8,128)}) custom-call(f32[8,4,256,256]{3,2,1,0:T(8,128)} %phi.1, bf16[256,256]{1,0:T(8,128)(2,1)} %constant.161.clone.into_h.refs_3_, bf16[256,256]{1,0:T(8,128)(2,1)} %constant.162.clone.into_l.refs_4_, ...), custom_call_target="tpu_custom_call", output_to_operand_aliasing={{1}: (5, {})} | custom-call | bytes 44280000 | tf_op jit(solution)/shard_map/into_modes/pallas_call | solution.py:260
  51.2 4.2 collective-permute-done.3
  57.4 6.8 %all-to-all-start.1 = ((f32[8,520,128]{2,1,0:T(8,128)}), f32[8,520,128]{2,1,0:T(8,128)}, u32[]{:S(2)}, u32[]{:S(2)}) async-start(f32[8,520,128]{2,1,0:T(8,128)} %get-tuple-element.60), calls=%async_computation.1 | async-start | bytes 4259840 | tf_op jit(solution)/shard_map/all_to_all | solution.py:639
  65.3 3.0 collective-permute-start.8
  68.3 2.2 collective-permute-start.9
  71.3 2.2 pad_maximum_fusion.other
  74.1 7.0 %targets.4.refs_2_ = f32[64,2,5,8,128]{4,3,2,1,0:T(8,128)} custom-call(s32[1]{0:T(128)} %bitcast.group, f32[2,2,64,32,256]{4,3,2,1,0:T(8,128)} %own.7, f32[4,2,16,16,128]{4,3,2,1,0:T(8,128)} %pad_maximum_fusion.other, f32[8,128]{1,0:T(8,128)} %broadcast_in_dim.180.keep.refs_10_.refs_8_), custom_call_target="tpu_custom_call" | custom-call | bytes 14760000 | tf_op jit(solution)/shard_map/targets/pallas_call | solution.py:562
  81.1 7.1 %collective-permute-done.9 = f32[2,16,16,128]{3,2,1,0:T(8,128)S(1)} collective-permute-done((f32[2,16,16,128]{3,2,1,0:T(8,128)S(1)}, f32[2,16,16,128]{3,2,1,0:T(8,128)S(1)}, u32[]{:S(2)}, u32[]{:S(2)}) %collective-permute-start.9) | collective-permute-done | bytes 262176 | tf_op jit(solution)/shard_map/ppermute | solution.py:635
  88.1 3.3 all-to-all-done.1.refs_1_
  91.4 4.7 all-to-all-start.3
  100.5 14.3 %downward.4 = (f32[8,520,128]{2,1,0:T(8,128)}, f32[8,520,128]{2,1,0:T(8,128)}, f32[2,5,8,128]{3,2,1,0:T(8,128)}, f32[3,6,64,8]{3,2,1,0:T(8,128)}, f32[64,2,8,128]{3,2,1,0:T(8,128)}) custom-call(f32[8,520,128]{2,1,0:T(8,128)} %copy-done, f32[8,520,128]{2,1,0:T(8,128)} %all-to-all-done.1.refs_1_, f32[64,2,5,8,128]{4,3,2,1,0:T(8,128)} %targets.4.refs_2_, ...), custom_call_target="tpu_custom_call" | custom-call | bytes 47970000 | tf_op jit(solution)/shard_map/downward/pallas_call | solution.py:445
  114.8 2.9 collective-permute-start.5
  117.7 2.2 collective-permute-start.6
  120.1 1.9 collective-permute-done.5.refs_12_
  124.9 16.4 %upward.4 = (f32[8,1040,128]{2,1,0:T(8,128)}, f32[3,6,64,8]{3,2,1,0:T(8,128)}) custom-call(f32[8,520,128]{2,1,0:T(8,128)} %copy-done, f32[8,520,128]{2,1,0:T(8,128)} %all-to-all-done.1.refs_1_, f32[64,2,5,8,128]{4,3,2,1,0:T(8,128)} %targets.4.refs_2_, f32[2,6,9,8,128]{4,3,2,1,0:T(8,128)} %get-tuple-element.111.refs_3_, ...), custom_call_target="tpu_custom_call" | custom-call | bytes 47970000 | tf_op jit(solution)/shard_map/upward/pallas_call | solution.py:445
  141.2 4.1 all-to-all-done.3.refs_0_
  145.3 4.6 all-to-all-start.2
  150.9 2.9 collective-permute-start.14
  153.9 2.2 collective-permute-start.15
  158.3 6.2 %targets.5.refs_1_ = f32[64,2,4,8,128]{4,3,2,1,0:T(8,128)} custom-call(s32[1]{0:T(128)} %bitcast.group, f32[2,2,64,32,256]{4,3,2,1,0:T(8,128)} %own.7, f32[4,2,16,16,128]{4,3,2,1,0:T(8,128)} %pad_maximum_fusion.1.other, f32[8,128]{1,0:T(8,128)} %broadcast_in_dim.180.keep.refs_10_.refs_8_), custom_call_target="tpu_custom_call" | custom-call | bytes 14760000 | tf_op jit(solution)/shard_map/targets/pallas_call | solution.py:562
  164.5 11.8 %downward.5 = (f32[8,512,128]{2,1,0:T(8,128)}, f32[8,512,128]{2,1,0:T(8,128)}, f32[2,4,8,128]{3,2,1,0:T(8,128)}, f32[2,6,64,8]{3,2,1,0:T(8,128)}) custom-call(f32[8,1024,128]{2,1,0:T(8,128)} %all-to-all-done.3.refs_0_, f32[64,2,4,8,128]{4,3,2,1,0:T(8,128)} %targets.5.refs_1_, f32[2,6,8,8,128]{4,3,2,1,0:T(8,128)} %get-tuple-element.112.refs_2_, ...), custom_call_target="tpu_custom_call" | custom-call | bytes 47970000 | tf_op jit(solution)/shard_map/downward/pallas_call | solution.py:445
  176.3 1.8 collective-permute-start.11
  178.9 3.3 collective-permute-done.11.refs_10_
  183.2 3.2 collective-permute-done.13.refs_12_
  187.0 13.2 %upward.5 = (f32[8,512,128]{2,1,0:T(8,128)}, f32[8,512,128]{2,1,0:T(8,128)}, f32[2,6,64,8]{3,2,1,0:T(8,128)}) custom-call(f32[8,1024,128]{2,1,0:T(8,128)} %all-to-all-done.3.refs_0_, f32[64,2,4,8,128]{4,3,2,1,0:T(8,128)} %targets.5.refs_1_, f32[2,6,8,8,128]{4,3,2,1,0:T(8,128)} %get-tuple-element.113.refs_2_, ...), custom_call_target="tpu_custom_call" | custom-call | bytes 47970000 | tf_op jit(solution)/shard_map/upward/pallas_call | solution.py:445
  201.0 4.1 all-to-all-start.4
  206.3 2.2 collective-permute-start.18
  209.0 7.2 %collective-permute-done.17 = f32[2,16,16,128]{3,2,1,0:T(8,128)S(1)} collective-permute-done((f32[2,16,16,128]{3,2,1,0:T(8,128)S(1)}, f32[2,16,16,128]{3,2,1,0:T(8,128)S(1)}, u32[]{:S(2)}, u32[]{:S(2)}) %collective-permute-start.17) | collective-permute-done | bytes 262176 | tf_op jit(solution)/shard_map/ppermute | solution.py:635
  216.2 10.8 %collective-permute-done.18 = f32[2,16,16,128]{3,2,1,0:T(8,128)S(1)} collective-permute-done((f32[2,16,16,128]{3,2,1,0:T(8,128)S(1)}, f32[2,16,16,128]{3,2,1,0:T(8,128)S(1)}, u32[]{:S(2)}, u32[]{:S(2)}) %collective-permute-start.18) | collective-permute-done | bytes 262176 | tf_op jit(solution)/shard_map/ppermute | solution.py:635
  228.4 3.3 all-to-all-done.4.refs_1_
  231.7 4.4 all-to-all-start.6
  236.1 20.1 %between_steps.2 = (f32[8,520,128]{2,1,0:T(8,128)}, f32[8,1024,128]{2,1,0:T(8,128)}) custom-call(f32[8,1040,128]{2,1,0:T(8,128)} %all-to-all-done.2.refs_0_, f32[8,512,128]{2,1,0:T(8,128)} %copy-done.3, f32[8,256,256]{2,1,0:T(8,128)} %refs_2_.7, bf16[256,256]{1,0:T(8,128)(2,1)} %constant.161.clone.into_h.refs_3_, ...), custom_call_target="tpu_custom_call" | custom-call | bytes 92250000 | tf_op jit(solution)/shard_map/between_steps/pallas_call | solution.py:260
  256.2 6.5 %all-to-all-done.6.refs_1_ = f32[8,512,128]{2,1,0:T(8,128)} async-done(((f32[8,512,128]{2,1,0:T(8,128)}), f32[8,512,128]{2,1,0:T(8,128)}, u32[]{:S(2)}, u32[]{:S(2)}) %all-to-all-start.6) | async-done | bytes 2097184 | tf_op jit(solution)/shard_map/all_to_all | solution.py:639
  262.8 3.6 all-to-all-start.5
  266.4 20.2 %between_steps.3 = (f32[8,520,128]{2,1,0:T(8,128)}, f32[8,1024,128]{2,1,0:T(8,128)}) custom-call(f32[8,1040,128]{2,1,0:T(8,128)} %all-to-all-done.2.refs_0_, f32[8,512,128]{2,1,0:T(8,128)} %all-to-all-done.6.refs_1_, f32[8,256,256]{2,1,0:T(8,128)} %refs_2_.7, bf16[256,256]{1,0:T(8,128)(2,1)} %constant.161.clone.into_h.refs_3_, ...), custom_call_target="tpu_custom_call", output_to_operand_aliasing={{1}: (11, {})} | custom-call | bytes 92250000 | tf_op jit(solution)/shard_map/between_steps/pallas_call | solution.py:260
  286.6 6.7 %all-to-all-done.5.refs_0_ = f32[8,520,128]{2,1,0:T(8,128)S(1)} async-done(((f32[8,520,128]{2,1,0:T(8,128)}), f32[8,520,128]{2,1,0:T(8,128)S(1)}, u32[]{:S(2)}, u32[]{:S(2)}) %all-to-all-start.5) | async-done | bytes 2129952 | tf_op jit(solution)/shard_map/all_to_all | solution.py:639
  293.3 31.3 %all_to_all.69.refs_1_ = f32[8,520,128]{2,1,0:T(8,128)} all-to-all(f32[8,520,128]{2,1,0:T(8,128)} %get-tuple-element.80), channel_id=1, replica_groups=mesh['gx'=8,'ba'=4] {'gx'}, dimensions={0} | all-to-all | bytes 4259840 | tf_op jit(solution)/shard_map/all_to_all | solution.py:639
  324.6 4.7 all-to-all-start.9
  330.4 7.0 %targets.6.refs_2_ = f32[64,2,5,8,128]{4,3,2,1,0:T(8,128)} custom-call(s32[1]{0:T(128)} %bitcast.group, f32[2,2,64,32,256]{4,3,2,1,0:T(8,128)} %own.7, f32[4,2,16,16,128]{4,3,2,1,0:T(8,128)} %pad_maximum_fusion.2.other, f32[8,128]{1,0:T(8,128)} %broadcast_in_dim.180.keep.refs_10_.refs_8_), custom_call_target="tpu_custom_call" | custom-call | bytes 14760000 | tf_op jit(solution)/shard_map/targets/pallas_call | solution.py:562
  337.4 14.3 %downward.6 = (f32[8,520,128]{2,1,0:T(8,128)}, f32[8,520,128]{2,1,0:T(8,128)}, f32[2,5,8,128]{3,2,1,0:T(8,128)}, f32[3,6,64,8]{3,2,1,0:T(8,128)}, f32[64,2,8,128]{3,2,1,0:T(8,128)}) custom-call(f32[8,520,128]{2,1,0:T(8,128)} %copy-done.1, f32[8,520,128]{2,1,0:T(8,128)} %all_to_all.69.refs_1_, f32[64,2,5,8,128]{4,3,2,1,0:T(8,128)} %targets.6.refs_2_, ...), custom_call_target="tpu_custom_call" | custom-call | bytes 47970000 | tf_op jit(solution)/shard_map/downward/pallas_call | solution.py:445
  351.7 1.9 collective-permute-start.20
  356.0 2.1 collective-permute-done.20.refs_12_
  360.4 16.4 %upward.6 = (f32[8,1040,128]{2,1,0:T(8,128)}, f32[3,6,64,8]{3,2,1,0:T(8,128)}) custom-call(f32[8,520,128]{2,1,0:T(8,128)} %copy-done.1, f32[8,520,128]{2,1,0:T(8,128)} %all_to_all.69.refs_1_, f32[64,2,5,8,128]{4,3,2,1,0:T(8,128)} %targets.6.refs_2_, f32[2,6,9,8,128]{4,3,2,1,0:T(8,128)} %get-tuple-element.111.refs_3_, ...), custom_call_target="tpu_custom_call" | custom-call | bytes 47970000 | tf_op jit(solution)/shard_map/upward/pallas_call | solution.py:445
  376.7 1.7 all-to-all-done.9.refs_0_
  378.4 4.7 all-to-all-start.8
  384.2 6.2 %targets.7.refs_1_ = f32[64,2,4,8,128]{4,3,2,1,0:T(8,128)} custom-call(s32[1]{0:T(128)} %bitcast.group, f32[2,2,64,32,256]{4,3,2,1,0:T(8,128)} %own.7, f32[4,2,16,16,128]{4,3,2,1,0:T(8,128)} %pad_maximum_fusion.3.other, f32[8,128]{1,0:T(8,128)} %broadcast_in_dim.180.keep.refs_10_.refs_8_), custom_call_target="tpu_custom_call" | custom-call | bytes 14760000 | tf_op jit(solution)/shard_map/targets/pallas_call | solution.py:562
  390.4 11.9 %downward.7 = (f32[8,512,128]{2,1,0:T(8,128)}, f32[8,512,128]{2,1,0:T(8,128)}, f32[2,4,8,128]{3,2,1,0:T(8,128)}, f32[2,6,64,8]{3,2,1,0:T(8,128)}) custom-call(f32[8,1024,128]{2,1,0:T(8,128)} %all-to-all-done.9.refs_0_, f32[64,2,4,8,128]{4,3,2,1,0:T(8,128)} %targets.7.refs_1_, f32[2,6,8,8,128]{4,3,2,1,0:T(8,128)} %get-tuple-element.112.refs_2_, ...), custom_call_target="tpu_custom_call" | custom-call | bytes 47970000 | tf_op jit(solution)/shard_map/downward/pallas_call | solution.py:445
  402.3 1.9 collective-permute-start.23
  406.6 1.9 collective-permute-done.23.refs_10_
  410.4 13.1 %upward.7 = (f32[8,512,128]{2,1,0:T(8,128)}, f32[8,512,128]{2,1,0:T(8,128)}, f32[2,6,64,8]{3,2,1,0:T(8,128)}) custom-call(f32[8,1024,128]{2,1,0:T(8,128)} %all-to-all-done.9.refs_0_, f32[64,2,4,8,128]{4,3,2,1,0:T(8,128)} %targets.7.refs_1_, f32[2,6,8,8,128]{4,3,2,1,0:T(8,128)} %get-tuple-element.113.refs_2_, ...), custom_call_target="tpu_custom_call" | custom-call | bytes 47970000 | tf_op jit(solution)/shard_map/upward/pallas_call | solution.py:445
  423.5 9.4 %all-to-all-done.8.refs_0_ = f32[8,1040,128]{2,1,0:T(8,128)} async-done(((f32[8,1040,128]{2,1,0:T(8,128)}), f32[8,1040,128]{2,1,0:T(8,128)}, u32[]{:S(2)}, u32[]{:S(2)}) %all-to-all-start.8) | async-done | bytes 4259872 | tf_op jit(solution)/shard_map/all_to_all | solution.py:639
  432.9 30.9 %all_to_all.70.refs_1_ = f32[8,512,128]{2,1,0:T(8,128)} all-to-all(f32[8,512,128]{2,1,0:T(8,128)} %get-tuple-element.93), channel_id=1, replica_groups=mesh['gx'=8,'ba'=4] {'gx'}, dimensions={0} | all-to-all | bytes 4194304 | tf_op jit(solution)/shard_map/all_to_all | solution.py:639
  463.9 3.7 all-to-all-start.11
  474.6 10.0 %out_of_modes.2.refs_7_ = f32[8,4,256,256]{3,2,1,0:T(8,128)} custom-call(f32[8,1040,128]{2,1,0:T(8,128)} %all-to-all-done.8.refs_0_, f32[8,512,128]{2,1,0:T(8,128)} %all_to_all.70.refs_1_, f32[8,256,256]{2,1,0:T(8,128)} %refs_2_.7, bf16[256,512]{1,0:T(8,128)(2,1)} %constant.165.clone.refs_7_.refs_3_, bf16[256,512]{1,0:T(8,128)(2,1)} %constant.166.clone.refs_8_.refs_4_, ...), custom_call_target="tpu_custom_call" | custom-call | bytes 59040000 | tf_op jit(solution)/shard_map/out_of_modes/pallas_call | solution.py:293
  484.6 9.6 %all-to-all-done.11.refs_1_ = f32[8,512,128]{2,1,0:T(8,128)S(1)} async-done(((f32[8,512,128]{2,1,0:T(8,128)}), f32[8,512,128]{2,1,0:T(8,128)S(1)}, u32[]{:S(2)}, u32[]{:S(2)}) %all-to-all-start.11) | async-done | bytes 2097184 | tf_op jit(solution)/shard_map/all_to_all | solution.py:639
  494.9 3.3 all-to-all-start.12
  498.2 10.0 %out_of_modes.3 = f32[8,4,256,256]{3,2,1,0:T(8,128)} custom-call(f32[8,1040,128]{2,1,0:T(8,128)} %all-to-all-done.8.refs_0_, f32[8,512,128]{2,1,0:T(8,128)} %copy-done.2, f32[8,256,256]{2,1,0:T(8,128)} %refs_2_.7, bf16[256,512]{1,0:T(8,128)(2,1)} %constant.165.clone.refs_7_.refs_3_, ...), custom_call_target="tpu_custom_call", output_to_operand_aliasing={{}: (7, {})} | custom-call | bytes 59040000 | tf_op jit(solution)/shard_map/out_of_modes/pallas_call | solution.py:293
  (219 shorter events, 45.3 us)
Async XLA Ops:
  5.0 27.2 %collective-permute-start.1 = (f32[2,2,16,32,128]{4,3,2,1,0:T(8,128)}, f32[2,2,16,32,128]{4,3,2,1,0:T(8,128)S(1)}, u32[]{:S(2)}, u32[]{:S(2)}) collective-permute-start(f32[2,2,16,32,128]{4,3,2,1,0:T(8,128)} %get-tuple-element.53), channel_id=1, source_target_pairs={{0,28},{4,24},{8,20},{12,16},{16,12},{20,8},{24,4},{28,0},{1,29},{... | collective-permute-start | bytes 3145736 | tf_op jit(solution)/shard_map/ppermute | solution.py:628
  8.4 19.5 %collective-permute-start = (f32[2,2,16,128]{3,2,1,0:T(8,128)}, f32[2,2,16,128]{3,2,1,0:T(8,128)S(1)}, u32[]{:S(2)}, u32[]{:S(2)}) collective-permute-start(f32[2,2,16,128]{3,2,1,0:T(8,128)} %get-tuple-element.54), channel_id=1, source_target_pairs={{0,0},{4,28},{8,24},{12,20},{16,16},{20,12},{24,8},{28,4},{1,1},{5... | collective-permute-start | bytes 98312 | tf_op jit(solution)/shard_map/ppermute | solution.py:629
  21.8 4.9 copy-start.31
  21.8 5.9 %copy-start.32 = (f32[4]{0:T(128)S(1)}, f32[4]{0:T(128)}, u32[]{:S(2)}) copy-start(f32[4]{0:T(128)} %param.26) | copy-start | bytes 52
  21.8 34.3 %all-to-all-start = ((f32[8,520,128]{2,1,0:T(8,128)}), f32[8,520,128]{2,1,0:T(8,128)S(1)}, u32[]{:S(2)}, u32[]{:S(2)}) async-start(f32[8,520,128]{2,1,0:T(8,128)} %get-tuple-element.56), calls=%async_computation | async-start | bytes 4259840 | tf_op jit(solution)/shard_map/all_to_all | solution.py:639
  32.7 18.5 %collective-permute-start.2 = (f32[2,16,16,128]{3,2,1,0:T(8,128)S(1)}, f32[2,16,16,128]{3,2,1,0:T(8,128)S(1)}, u32[]{:S(2)}, u32[]{:S(2)}) collective-permute-start(f32[2,16,16,128]{3,2,1,0:T(8,128)S(1)} %get-tuple-element.121), channel_id=1, source_target_pairs={{0,1},{1,2},{2,3},{3,0},{4,5},{5,6},{6,7},{7,4},{8,9},{9,10},{10,1... | collective-permute-start | bytes 786440 | tf_op jit(solution)/shard_map/ppermute | solution.py:635
  35.1 20.3 %collective-permute-start.3 = (f32[2,16,16,128]{3,2,1,0:T(8,128)S(1)}, f32[2,16,16,128]{3,2,1,0:T(8,128)S(1)}, u32[]{:S(2)}, u32[]{:S(2)}) collective-permute-start(f32[2,16,16,128]{3,2,1,0:T(8,128)S(1)} %get-tuple-element.121), channel_id=1, source_target_pairs={{0,2},{1,3},{2,0},{3,1},{4,6},{5,7},{6,4},{7,5},{8,10},{9,11},{10,... | collective-permute-start | bytes 786440 | tf_op jit(solution)/shard_map/ppermute | solution.py:635
  37.7 18.4 %collective-permute-start.4 = (f32[2,16,16,128]{3,2,1,0:T(8,128)S(1)}, f32[2,16,16,128]{3,2,1,0:T(8,128)}, u32[]{:S(2)}, u32[]{:S(2)}) collective-permute-start(f32[2,16,16,128]{3,2,1,0:T(8,128)S(1)} %get-tuple-element.121), channel_id=1, source_target_pairs={{0,3},{1,0},{2,1},{3,2},{4,7},{5,4},{6,5},{7,6},{8,11},{9,8},{10,9... | collective-permute-start | bytes 786440 | tf_op jit(solution)/shard_map/ppermute | solution.py:635
  51.2 4.3 copy-start.7
  56.1 1.3 copy-start
  57.4 33.9 %all-to-all-start.1 = ((f32[8,520,128]{2,1,0:T(8,128)}), f32[8,520,128]{2,1,0:T(8,128)}, u32[]{:S(2)}, u32[]{:S(2)}) async-start(f32[8,520,128]{2,1,0:T(8,128)} %get-tuple-element.60), calls=%async_computation.1 | async-start | bytes 4259840 | tf_op jit(solution)/shard_map/all_to_all | solution.py:639
  65.3 15.7 %collective-permute-start.8 = (f32[2,16,16,128]{3,2,1,0:T(8,128)S(1)}, f32[2,16,16,128]{3,2,1,0:T(8,128)S(1)}, u32[]{:S(2)}, u32[]{:S(2)}) collective-permute-start(f32[2,16,16,128]{3,2,1,0:T(8,128)S(1)} %get-tuple-element.120), channel_id=1, source_target_pairs={{0,1},{1,2},{2,3},{3,0},{4,5},{5,6},{6,7},{7,4},{8,9},{9,10},{10,1... | collective-permute-start | bytes 786440 | tf_op jit(solution)/shard_map/ppermute | solution.py:635
  68.3 19.8 %collective-permute-start.9 = (f32[2,16,16,128]{3,2,1,0:T(8,128)S(1)}, f32[2,16,16,128]{3,2,1,0:T(8,128)S(1)}, u32[]{:S(2)}, u32[]{:S(2)}) collective-permute-start(f32[2,16,16,128]{3,2,1,0:T(8,128)S(1)} %get-tuple-element.120), channel_id=1, source_target_pairs={{0,2},{1,3},{2,0},{3,1},{4,6},{5,7},{6,4},{7,5},{8,10},{9,11},{10,... | collective-permute-start | bytes 786440 | tf_op jit(solution)/shard_map/ppermute | solution.py:635
  70.5 17.6 %collective-permute-start.10 = (f32[2,16,16,128]{3,2,1,0:T(8,128)S(1)}, f32[2,16,16,128]{3,2,1,0:T(8,128)S(1)}, u32[]{:S(2)}, u32[]{:S(2)}) collective-permute-start(f32[2,16,16,128]{3,2,1,0:T(8,128)S(1)} %get-tuple-element.120), channel_id=1, source_target_pairs={{0,3},{1,0},{2,1},{3,2},{4,7},{5,4},{6,5},{7,6},{8,11},{9,8},{10,9... | collective-permute-start | bytes 786440 | tf_op jit(solution)/shard_map/ppermute | solution.py:635
  91.4 5.1 %copy-start.37 = (f32[4]{0:T(128)S(1)}, f32[4]{0:T(128)}, u32[]{:S(2)}) copy-start(f32[4]{0:T(128)} %param.28) | copy-start | bytes 52
  91.4 6.4 %copy-start.33 = (f32[12]{0:T(128)S(1)}, f32[12]{0:T(128)}, u32[]{:S(2)}) copy-start(f32[12]{0:T(128)} %constant.177) | copy-start | bytes 148
  91.4 6.4 %copy-start.34 = (f32[12]{0:T(128)S(1)}, f32[12]{0:T(128)}, u32[]{:S(2)}) copy-start(f32[12]{0:T(128)} %constant.176) | copy-start | bytes 148
  91.4 6.4 %copy-start.35 = (f32[12]{0:T(128)S(1)}, f32[12]{0:T(128)}, u32[]{:S(2)}) copy-start(f32[12]{0:T(128)} %constant.175) | copy-start | bytes 148
  91.4 53.9 %all-to-all-start.3 = ((f32[8,1024,128]{2,1,0:T(8,128)}), f32[8,1024,128]{2,1,0:T(8,128)}, u32[]{:S(2)}, u32[]{:S(2)}) async-start(f32[8,1024,128]{2,1,0:T(8,128)} %get-tuple-element.67), calls=%async_computation.3 | async-start | bytes 8388608 | tf_op jit(solution)/shard_map/all_to_all | solution.py:639
  96.2 3.0 copy-start.36
  114.8 7.2 %collective-permute-start.5 = (f32[2,5,8,128]{3,2,1,0:T(8,128)}, f32[2,5,8,128]{3,2,1,0:T(8,128)S(1)}, u32[]{:S(2)}, u32[]{:S(2)}) collective-permute-start(f32[2,5,8,128]{3,2,1,0:T(8,128)} %get-tuple-element.64.refs_11_), channel_id=1, source_target_pairs={{0,1},{1,2},{2,3},{3,0},{4,5},{5,6},{6,7},{7,4},{8,9},{9,10},{10,1... | collective-permute-start | bytes 122888 | tf_op jit(solution)/shard_map/ppermute | solution.py:693
  117.7 5.8 %collective-permute-start.6 = (f32[2,5,8,128]{3,2,1,0:T(8,128)}, f32[2,5,8,128]{3,2,1,0:T(8,128)S(1)}, u32[]{:S(2)}, u32[]{:S(2)}) collective-permute-start(f32[2,5,8,128]{3,2,1,0:T(8,128)} %get-tuple-element.64.refs_11_), channel_id=1, source_target_pairs={{0,2},{1,3},{2,0},{3,1},{4,6},{5,7},{6,4},{7,5},{8,10},{9,11},{10,... | collective-permute-start | bytes 122888 | tf_op jit(solution)/shard_map/ppermute | solution.py:693
  119.9 4.2 collective-permute-start.7
  122.0 2.8 copy-start.19
  123.5 1.3 copy-start.20
  145.3 55.0 %all-to-all-start.2 = ((f32[8,1040,128]{2,1,0:T(8,128)}), f32[8,1040,128]{2,1,0:T(8,128)}, u32[]{:S(2)}, u32[]{:S(2)}) async-start(f32[8,1040,128]{2,1,0:T(8,128)} %get-tuple-element.65), calls=%async_computation.2 | async-start | bytes 8519680 | tf_op jit(solution)/shard_map/all_to_all | solution.py:639
  150.9 49.2 %collective-permute-start.14 = (f32[2,16,16,128]{3,2,1,0:T(8,128)S(1)}, f32[2,16,16,128]{3,2,1,0:T(8,128)S(1)}, u32[]{:S(2)}, u32[]{:S(2)}) collective-permute-start(f32[2,16,16,128]{3,2,1,0:T(8,128)S(1)} %get-tuple-element.117), channel_id=1, source_target_pairs={{0,1},{1,2},{2,3},{3,0},{4,5},{5,6},{6,7},{7,4},{8,9},{9,10},{10,1... | collective-permute-start | bytes 786440 | tf_op jit(solution)/shard_map/ppermute | solution.py:635
  153.9 46.3 %collective-permute-start.15 = (f32[2,16,16,128]{3,2,1,0:T(8,128)S(1)}, f32[2,16,16,128]{3,2,1,0:T(8,128)S(1)}, u32[]{:S(2)}, u32[]{:S(2)}) collective-permute-start(f32[2,16,16,128]{3,2,1,0:T(8,128)S(1)} %get-tuple-element.117), channel_id=1, source_target_pairs={{0,2},{1,3},{2,0},{3,1},{4,6},{5,7},{6,4},{7,5},{8,10},{9,11},{10,... | collective-permute-start | bytes 786440 | tf_op jit(solution)/shard_map/ppermute | solution.py:635
  156.0 44.2 %collective-permute-start.16 = (f32[2,16,16,128]{3,2,1,0:T(8,128)S(1)}, f32[2,16,16,128]{3,2,1,0:T(8,128)S(1)}, u32[]{:S(2)}, u32[]{:S(2)}) collective-permute-start(f32[2,16,16,128]{3,2,1,0:T(8,128)S(1)} %get-tuple-element.117), channel_id=1, source_target_pairs={{0,3},{1,0},{2,1},{3,2},{4,7},{5,4},{6,5},{7,6},{8,11},{9,8},{10,9... | collective-permute-start | bytes 786440 | tf_op jit(solution)/shard_map/ppermute | solution.py:635
  176.3 5.9 %collective-permute-start.11 = (f32[2,4,8,128]{3,2,1,0:T(8,128)}, f32[2,4,8,128]{3,2,1,0:T(8,128)S(1)}, u32[]{:S(2)}, u32[]{:S(2)}) collective-permute-start(f32[2,4,8,128]{3,2,1,0:T(8,128)} %get-tuple-element.70.refs_9_), channel_id=1, source_target_pairs={{0,1},{1,2},{2,3},{3,0},{4,5},{5,6},{6,7},{7,4},{8,9},{9,10},{10,1... | collective-permute-start | bytes 98312 | tf_op jit(solution)/shard_map/ppermute | solution.py:693
  178.2 5.0 collective-permute-start.12
  182.3 4.1 copy-start.27
  182.3 4.1 collective-permute-start.13
  183.2 3.2 copy-start.29
  200.2 4.9 copy-start.6
  201.0 30.7 %all-to-all-start.4 = ((f32[8,512,128]{2,1,0:T(8,128)}), f32[8,512,128]{2,1,0:T(8,128)S(1)}, u32[]{:S(2)}, u32[]{:S(2)}) async-start(f32[8,512,128]{2,1,0:T(8,128)} %get-tuple-element.73), calls=%async_computation.4 | async-start | bytes 4194304 | tf_op jit(solution)/shard_map/all_to_all | solution.py:639
  205.1 11.1 %collective-permute-start.17 = (f32[2,16,16,128]{3,2,1,0:T(8,128)S(1)}, f32[2,16,16,128]{3,2,1,0:T(8,128)S(1)}, u32[]{:S(2)}, u32[]{:S(2)}) collective-permute-start(f32[2,16,16,128]{3,2,1,0:T(8,128)S(1)} %copy-done.6), channel_id=1, source_target_pairs={{0,1},{1,2},{2,3},{3,0},{4,5},{5,6},{6,7},{7,4},{8,9},{9,10},{10,1... | collective-permute-start | bytes 786440 | tf_op jit(solution)/shard_map/ppermute | solution.py:635
  206.3 20.7 %collective-permute-start.18 = (f32[2,16,16,128]{3,2,1,0:T(8,128)S(1)}, f32[2,16,16,128]{3,2,1,0:T(8,128)S(1)}, u32[]{:S(2)}, u32[]{:S(2)}) collective-permute-start(f32[2,16,16,128]{3,2,1,0:T(8,128)S(1)} %copy-done.6), channel_id=1, source_target_pairs={{0,2},{1,3},{2,0},{3,1},{4,6},{5,7},{6,4},{7,5},{8,10},{9,11},{10,... | collective-permute-start | bytes 786440 | tf_op jit(solution)/shard_map/ppermute | solution.py:635
  208.4 18.5 %collective-permute-start.19 = (f32[2,16,16,128]{3,2,1,0:T(8,128)S(1)}, f32[2,16,16,128]{3,2,1,0:T(8,128)S(1)}, u32[]{:S(2)}, u32[]{:S(2)}) collective-permute-start(f32[2,16,16,128]{3,2,1,0:T(8,128)S(1)} %copy-done.6), channel_id=1, source_target_pairs={{0,3},{1,0},{2,1},{3,2},{4,7},{5,4},{6,5},{7,6},{8,11},{9,8},{10,9... | collective-permute-start | bytes 786440 | tf_op jit(solution)/shard_map/ppermute | solution.py:635
  216.2 40.1 %copy-start.13 = (f32[2,16,16,128]{3,2,1,0:T(8,128)}, f32[2,16,16,128]{3,2,1,0:T(8,128)S(1)}, u32[]{:S(2)}) copy-start(f32[2,16,16,128]{3,2,1,0:T(8,128)S(1)} %collective-permute-done.17) | copy-start | bytes 786436
  231.7 4.4 copy-start.3
  231.7 31.0 %all-to-all-start.6 = ((f32[8,512,128]{2,1,0:T(8,128)}), f32[8,512,128]{2,1,0:T(8,128)}, u32[]{:S(2)}, u32[]{:S(2)}) async-start(f32[8,512,128]{2,1,0:T(8,128)} %get-tuple-element.77), calls=%async_computation.6 | async-start | bytes 4194304 | tf_op jit(solution)/shard_map/all_to_all | solution.py:639
  262.8 30.5 %all-to-all-start.5 = ((f32[8,520,128]{2,1,0:T(8,128)}), f32[8,520,128]{2,1,0:T(8,128)S(1)}, u32[]{:S(2)}, u32[]{:S(2)}) async-start(f32[8,520,128]{2,1,0:T(8,128)} %get-tuple-element.74), calls=%async_computation.5 | async-start | bytes 4259840 | tf_op jit(solution)/shard_map/all_to_all | solution.py:639
  293.3 31.3 %copy-start.1 = (f32[8,520,128]{2,1,0:T(8,128)}, f32[8,520,128]{2,1,0:T(8,128)S(1)}, u32[]{:S(2)}) copy-start(f32[8,520,128]{2,1,0:T(8,128)S(1)} %all-to-all-done.5.refs_0_) | copy-start | bytes 6389764
  324.6 4.7 copy-start.10
  324.6 4.7 copy-start.12
  324.6 53.8 %all-to-all-start.9 = ((f32[8,1024,128]{2,1,0:T(8,128)}), f32[8,1024,128]{2,1,0:T(8,128)}, u32[]{:S(2)}, u32[]{:S(2)}) async-start(f32[8,1024,128]{2,1,0:T(8,128)} %get-tuple-element.87), calls=%async_computation.9 | async-start | bytes 8388608 | tf_op jit(solution)/shard_map/all_to_all | solution.py:639
  351.7 6.4 %collective-permute-start.20 = (f32[2,5,8,128]{3,2,1,0:T(8,128)}, f32[2,5,8,128]{3,2,1,0:T(8,128)S(1)}, u32[]{:S(2)}, u32[]{:S(2)}) collective-permute-start(f32[2,5,8,128]{3,2,1,0:T(8,128)} %get-tuple-element.84.refs_11_), channel_id=1, source_target_pairs={{0,1},{1,2},{2,3},{3,0},{4,5},{5,6},{6,7},{7,4},{8,9},{9,10},{10,1... | collective-permute-start | bytes 122888 | tf_op jit(solution)/shard_map/ppermute | solution.py:693
  353.6 5.8 %collective-permute-start.21 = (f32[2,5,8,128]{3,2,1,0:T(8,128)}, f32[2,5,8,128]{3,2,1,0:T(8,128)S(1)}, u32[]{:S(2)}, u32[]{:S(2)}) collective-permute-start(f32[2,5,8,128]{3,2,1,0:T(8,128)} %get-tuple-element.84.refs_11_), channel_id=1, source_target_pairs={{0,2},{1,3},{2,0},{3,1},{4,6},{5,7},{6,4},{7,5},{8,10},{9,11},{10,... | collective-permute-start | bytes 122888 | tf_op jit(solution)/shard_map/ppermute | solution.py:693
  355.0 4.8 collective-permute-start.22
  358.1 1.7 copy-start.21
  378.4 4.7 copy-start.14
  378.4 4.7 copy-start.16
  378.4 4.7 copy-start.18
  378.4 54.5 %all-to-all-start.8 = ((f32[8,1040,128]{2,1,0:T(8,128)}), f32[8,1040,128]{2,1,0:T(8,128)}, u32[]{:S(2)}, u32[]{:S(2)}) async-start(f32[8,1040,128]{2,1,0:T(8,128)} %get-tuple-element.85), calls=%async_computation.8 | async-start | bytes 8519680 | tf_op jit(solution)/shard_map/all_to_all | solution.py:639
  402.3 6.2 %collective-permute-start.23 = (f32[2,4,8,128]{3,2,1,0:T(8,128)}, f32[2,4,8,128]{3,2,1,0:T(8,128)S(1)}, u32[]{:S(2)}, u32[]{:S(2)}) collective-permute-start(f32[2,4,8,128]{3,2,1,0:T(8,128)} %get-tuple-element.90.refs_9_), channel_id=1, source_target_pairs={{0,1},{1,2},{2,3},{3,0},{4,5},{5,6},{6,7},{7,4},{8,9},{9,10},{10,1... | collective-permute-start | bytes 98312 | tf_op jit(solution)/shard_map/ppermute | solution.py:693
  404.2 5.4 %collective-permute-start.24 = (f32[2,4,8,128]{3,2,1,0:T(8,128)}, f32[2,4,8,128]{3,2,1,0:T(8,128)S(1)}, u32[]{:S(2)}, u32[]{:S(2)}) collective-permute-start(f32[2,4,8,128]{3,2,1,0:T(8,128)} %get-tuple-element.90.refs_9_), channel_id=1, source_target_pairs={{0,2},{1,3},{2,0},{3,1},{4,6},{5,7},{6,4},{7,5},{8,10},{9,11},{10,... | collective-permute-start | bytes 98312 | tf_op jit(solution)/shard_map/ppermute | solution.py:693
  405.5 4.3 collective-permute-start.25
  408.5 1.3 copy-start.25
  463.9 3.7 copy-start.4
  463.9 6.0 %copy-start.5 = (f32[2,6,64,8]{3,2,1,0:T(8,128)S(1)}, f32[2,6,64,8]{3,2,1,0:T(8,128)}, u32[]{:S(2)}) copy-start(f32[2,6,64,8]{3,2,1,0:T(8,128)} %get-tuple-element.96) | copy-start | bytes 73732
  463.9 30.3 %all-to-all-start.11 = ((f32[8,512,128]{2,1,0:T(8,128)}), f32[8,512,128]{2,1,0:T(8,128)S(1)}, u32[]{:S(2)}, u32[]{:S(2)}) async-start(f32[8,512,128]{2,1,0:T(8,128)} %get-tuple-element.94), calls=%async_computation.11 | async-start | bytes 4194304 | tf_op jit(solution)/shard_map/all_to_all | solution.py:639
  494.2 4.0 copy-start.2
  494.9 13.3 %all-to-all-start.12 = ((f32[8,1,384]{2,1,0:T(1,128)}), f32[8,1,384]{2,1,0:T(1,128)S(1)}, u32[]{:S(2)}, u32[]{:S(2)}) async-start(f32[8,1,384]{2,1,0:T(1,128)} %copy.51), calls=%async_computation.12 | async-start | bytes 24576 | tf_op jit(solution)/shard_map/all_to_all | solution.py:639
  (11 other events, 7.3 us)
